TPU v7x, 32 devices: a whole 2x2x4 slice. The times are simulated.
32 devices in a mesh: segment: 8 (over z, core), space: 2 (over x), ens: 2 (over y).
Axes of the slice: x: 2, y: 2, z: 4, core: 2. Of those that a mesh axis runs over, the one named last changes fastest.
Arguments:
- state_in: bfloat16 [2, 8, 1, 12, 180, 768], P('ens', 'segment', None, 'space'), may hold values from -6 to 6
- member_ids: int32 [2, 8, 1], P('ens'), may hold values from 0 to 99
- member_table: bfloat16 [100, 768], replicated, may hold values from -3 to 3
- pos_embed: bfloat16 [12, 180, 768], P('space'), may hold values from -3 to 3
- readout_tile_matrix: bfloat16 [768, 1280], replicated, may hold values from -0.21875 to 0.21875
- tile_lifting_matrix: bfloat16 [1280, 768], replicated, may hold values from -0.15625 to 0.15625
- norm_gain: float32 [8, 2, 768], P('segment'), may hold values from 0.5 to 1.5
- norm_shift: float32 [8, 2, 768], P('segment'), may hold values from -1.25 to 1.25
- spectral: float32 [8, 2, 2, 8, 96, 96], P('segment'), may hold values from -0.4375 to 0.4375
- up_weight: bfloat16 [8, 768, 3072], P('segment', ('space', 'ens')), may hold values from -0.21875 to 0.21875
- down_weight: bfloat16 [8, 3072, 768], P('segment', ('space', 'ens')), may hold values from -0.109375 to 0.109375
Outputs:
- state_out: bfloat16 [2, 8, 1, 12, 180, 768], P('ens', 'segment', None, 'space')
All inputs are finite; a program needn't handle non-finite values.
Results may differ from a plain program's by a relative error of at most 0.0035.
Values may be sent and summed in bfloat16 or wider, within the bound.
No kernel may reach another device: no remote copies, remote signals or barrier semaphores. Data moves between devices by JAX's collectives and lax.ppermute only.
A program may use at most 128 MiB of HBM per device.

v0:
```python
import math

import jax
import jax.numpy as jnp
from jax import lax
from jax.sharding import PartitionSpec as P

KW = 88


EPSILON = 1e-05
SHRINK_LEVEL = 0.01
HIGHEST_PRECISION = lax.Precision.HIGHEST


def shifted(value, axis, steps):
    count = lax.axis_size(axis)
    pairs = [(source, (source + steps) % count) for source in range(count)]
    return lax.ppermute(value, axis, pairs)


def layer_norm(values):
    average = jnp.mean(values, axis=-1, keepdims=True)
    centred = values - average
    spread = jnp.mean(centred * centred, axis=-1, keepdims=True)
    return centred * lax.rsqrt(spread + EPSILON)


def longitude_tables(longitudes, kept, latitudes):
    number = jnp.arange(kept, dtype=jnp.int32)[:, None]
    points = jnp.arange(longitudes, dtype=jnp.int32)[None, :]
    angles = (number * points % longitudes).astype(jnp.float32) * (2.0 * math.pi / longitudes)
    factor = 1.0 / math.sqrt(latitudes * longitudes)
    doubled = jnp.where(number == 0, 1.0, 2.0).astype(jnp.float32) * factor
    forward = jnp.stack([jnp.cos(angles) * factor, -jnp.sin(angles) * factor])
    backward = jnp.stack([jnp.cos(angles) * doubled, -jnp.sin(angles) * doubled])
    return (forward, backward)


def latitude_tables(latitudes):
    number = jnp.arange(latitudes, dtype=jnp.int32)[:, None]
    points = jnp.arange(latitudes, dtype=jnp.int32)[None, :]
    angles = (number * points % latitudes).astype(jnp.float32) * (2.0 * math.pi / latitudes)
    cosine_table = jnp.cos(angles)
    sine_table = jnp.sin(angles)
    forward = jnp.concatenate(
        [
            jnp.concatenate([cosine_table, sine_table], 1),
            jnp.concatenate([-sine_table, cosine_table], 1),
        ],
        0,
    )
    backward = jnp.concatenate(
        [
            jnp.concatenate([cosine_table, -sine_table], 1),
            jnp.concatenate([sine_table, cosine_table], 1),
        ],
        0,
    )
    return (forward, backward)


def mix_blocks(spectra, filters):
    extent = spectra.shape
    halves = spectra.reshape(extent[0], 2, extent[2], extent[3], filters.shape[2], filters.shape[3])
    nonimaginary_component = halves[:, 0]
    imag_part = halves[:, 1]

    def product(operand, matrix):
        return jnp.einsum("mhknb,nbc->mhknc", operand, matrix, precision=HIGHEST_PRECISION)

    first_real = jax.nn.relu(
        product(nonimaginary_component, filters[0, 0]) - product(imag_part, filters[0, 1])
    )
    first_imag = jax.nn.relu(
        product(nonimaginary_component, filters[0, 1]) + product(imag_part, filters[0, 0])
    )
    second_real = product(first_real, filters[1, 0]) - product(first_imag, filters[1, 1])
    second_imag = product(first_real, filters[1, 1]) + product(first_imag, filters[1, 0])
    blended = jnp.stack([second_real, second_imag], axis=1)
    blended = blended - jnp.clip(blended, -SHRINK_LEVEL, SHRINK_LEVEL)
    return blended.reshape(extent)


def spectral_filter(normed_one, filters, tables):
    forward, backward, lat_forward, lat_backward = tables
    spectra = jnp.einsum("rkw,mhwd->mrhkd", forward, normed_one, precision=HIGHEST_PRECISION)
    collected_fields = lax.all_to_all(spectra, "space", split_axis=3, concat_axis=2, tiled=True)
    extent = collected_fields.shape
    stacked = collected_fields.reshape(extent[0], 2 * extent[2], extent[3], extent[4])
    turned = jnp.einsum("ab,mbkd->makd", lat_forward, stacked, precision=HIGHEST_PRECISION)
    blended_modes = mix_blocks(turned.reshape(extent), filters).reshape(stacked.shape)
    inverse = jnp.einsum(
        "ab,mbkd->makd", lat_backward, blended_modes, precision=HIGHEST_PRECISION
    ).reshape(extent)
    returned = lax.all_to_all(inverse, "space", split_axis=2, concat_axis=3, tiled=True)
    return jnp.einsum("rkw,mrhkd->mhwd", backward, returned, precision=HIGHEST_PRECISION)


def on_device(
    state_in,
    member_ids,
    member_table,
    pos_embed,
    readout_tile_matrix,
    tile_lifting_matrix,
    norm_gain,
    norm_shift,
    spectral,
    up_weight,
    down_weight,
):
    position = lax.axis_index("segment")
    segment_count = lax.axis_size("segment")
    current = state_in[0, 0]
    channels = current.shape[3]
    latitudes = current.shape[1] * lax.axis_size("space")
    forward, backward = longitude_tables(current.shape[2], KW, latitudes)
    lat_forward, lat_backward = latitude_tables(latitudes)
    tables = (forward, backward, lat_forward, lat_backward)
    gains = norm_gain[0]
    shifts = norm_shift[0]
    filters = spectral[0]
    slot_index = -0 % segment_count
    chosen = member_ids[0, slot_index]
    onehot = (
        chosen[:, None] == jnp.arange(member_table.shape[0], dtype=jnp.int32)[None, :]
    ).astype(jnp.bfloat16)
    sample_trajectory_lines = jnp.dot(onehot, member_table, preferred_element_type=jnp.float32)

    def enter_grid(values):
        standardized_field = layer_norm(values.astype(jnp.float32)).astype(jnp.bfloat16)
        prediction_increment = jnp.einsum(
            "fbrd,do->fbro",
            standardized_field,
            readout_tile_matrix,
            preferred_element_type=jnp.float32,
        ).astype(jnp.bfloat16)
        admitted_lines = jnp.einsum(
            "nzwt,tl->nzwl",
            prediction_increment,
            tile_lifting_matrix,
            preferred_element_type=jnp.float32,
        )
        return (
            admitted_lines
            + pos_embed.astype(jnp.float32)[None]
            + sample_trajectory_lines[:, None, None, :]
        )

    def cast_values(values):
        return values.astype(jnp.float32)

    carried = lax.cond(position == 0, enter_grid, cast_values, current)
    normed_one = layer_norm(carried) * gains[0] + shifts[0]
    blended = carried + normed_one + spectral_filter(normed_one, filters, tables)
    normed_two = (layer_norm(blended) * gains[1] + shifts[1]).astype(jnp.bfloat16)
    flat_rows = normed_two.reshape(-1, channels)
    columns = flat_rows
    lifted = jnp.dot(
        columns,
        lax.all_gather(up_weight, ("space", "ens"), axis=1, tiled=True)[0],
        preferred_element_type=jnp.float32,
    )
    hidden = jax.nn.gelu(lifted, approximate=False).astype(jnp.bfloat16)
    columns = hidden
    update = jnp.dot(
        columns,
        lax.all_gather(down_weight, ("space", "ens"), axis=1, tiled=True)[0],
        preferred_element_type=jnp.float32,
    ).reshape(blended.shape)
    current = shifted((blended + update).astype(jnp.bfloat16), "segment", 1)
    return current[None, None]


def solution(mesh):
    placed = (
        P("ens", "segment", None, "space", None, None),
        P("ens", None, None),
        P(),
        P("space", None, None),
        P(),
        P(),
        P("segment", None, None),
        P("segment", None, None),
        P("segment", None, None, None, None, None),
        P("segment", ("space", "ens"), None),
        P("segment", ("space", "ens"), None),
    )
    return jax.shard_map(
        on_device,
        mesh=mesh,
        in_specs=placed,
        out_specs=P("ens", "segment", None, "space", None, None),
        check_vma=False,
    )
```

profile of v0, /device:TPU:1, one launch (start us, length us, event | category | flops | bytes accessed | tf_op | source)
XLA Modules:
  0.0 305.4 jit_solution(16498307155999679571)
XLA Ops:
  6.5 0.0 copy-start
  6.5 0.0 all-gather.3.cloned.1.call-start
  6.5 0.7 all-gather.3.cloned.1.call-update
  7.3 1.0 fusion.81
  8.3 0.0 copy-done
  8.3 0.8 fusion.103
  9.1 2.6 conditional.1
  9.1 2.4 fusion.115
  11.7 0.0 copy-start.7
  11.7 0.0 copy-start.8
  11.7 0.0 copy-start.6
  11.8 0.5 multiply_reduce_fusion.1
  12.3 0.1 copy-done.7
  12.4 0.0 copy-done.8
  12.5 0.2 copy-done.6
  12.6 4.0 %fusion.55 = f32[1,2,6,88,768]{4,3,1,2,0:T(8,128)S(1)} fusion(f32[1,6,180,768]{3,2,1,0:T(8,128)S(1)} %get-tuple-element.26, f32[768]{0:T(1024)S(1)} %get-tuple-element.38, f32[768]{0:T(1024)S(1)} %get-tuple-element.51, f32[6,180]{1,0:T(8,128)S(1)} %add_rsqrt_fusion.2, f32[6,180]{1,0:T(8,128)S(1)} %multiply_bitcast_fusion, f32[1,88,180]{2,1,0:T(8,128)S(1)} %copy-done.6, ...), kind=kOutput, calls=%fused_computation.75 | convolution fusion | flops 1755126784 | bytes 6703296 | tf_op jit(solution)/shard_map/rkw,mhwd->mrhkd/dot_general | solution.py:87
  16.6 3.5 %copy.29 = f32[1,2,6,88,768]{4,1,2,0,3:T(2,128)} copy(f32[1,2,6,88,768]{4,3,1,2,0:T(8,128)S(1)} %fusion.55) | data formatting | bytes 6488064 | tf_op jit(solution)/shard_map/rkw,mhwd->mrhkd/transpose | solution.py:87
  20.1 5.5 %all-to-all-start = ((f32[1,2,6,88,768]{4,1,2,0,3:T(2,128)}), f32[1,2,6,88,768]{4,1,2,0,3:T(2,128)}, u32[]{:S(2)}, u32[]{:S(2)}) async-start(f32[1,2,6,88,768]{4,1,2,0,3:T(2,128)} %copy.29), calls=%async_computation | async-start | bytes 6488064 | tf_op jit(solution)/shard_map/all_to_all | solution.py:88
  25.5 0.1 fusion.102
  25.6 0.1 fusion.99
  25.7 56.3 %all-to-all-done = f32[1,2,6,88,768]{4,1,2,0,3:T(2,128)} async-done(((f32[1,2,6,88,768]{4,1,2,0,3:T(2,128)}), f32[1,2,6,88,768]{4,1,2,0,3:T(2,128)}, u32[]{:S(2)}, u32[]{:S(2)}) %all-to-all-start) | async-done | bytes 3244064 | tf_op jit(solution)/shard_map/all_to_all | solution.py:88
  81.9 3.0 copy.30
  85.0 0.4 copy.31
  85.4 6.3 %fusion.58 = f32[1,24,44,768]{3,1,2,0:T(8,128)} fusion(f32[24,44,768]{2,1,0:T(8,128)S(1)} %bitcast.194, f32[12,12]{1,0:T(8,128)S(1)} %get-tuple-element.54, f32[12,12]{1,0:T(8,128)S(1)} %fusion.102, f32[12,12]{1,0:T(8,128)S(1)} %get-tuple-element.53), kind=kOutput, calls=%fused_computation.76 | convolution fusion | flops 233572032 | bytes 6489792 | tf_op jit(solution)/shard_map/ab,mbkd->makd/dot_general | solution.py:91
  91.8 5.9 %reshape_reshape.4 = f32[1,2,12,44,8,96]{5,4,2,1,3,0:T(8,128)} reshape(f32[1,24,44,768]{3,1,2,0:T(8,128)} %fusion.58) | data formatting | bytes 6488064 | tf_op jit(solution)/shard_map/reshape;reshape | solution.py:65
  97.6 0.0 copy-start.4
  97.7 2.7 fusion.116
  100.3 0.0 copy-done.4
  100.4 3.5 %fusion.46 = f32[8,12,44,96]{3,2,1,0:T(8,128)S(1)} fusion(f32[1,1,12,44,8,96]{5,4,2,1,3,0:T(8,128)S(1)} %get-tuple-element.44, f32[2,2,8,96,96]{4,3,2,1,0:T(8,128)S(1)} %bitcast.199), kind=kOutput, calls=%fused_computation.70 | convolution fusion | flops 467140608 | bytes 4177920 | tf_op jit(solution)/shard_map/mhknb,nbc->mhknc/dot_general | solution.py:70
  103.9 3.4 %fusion.47 = f32[8,12,44,96]{3,2,1,0:T(8,128)S(1)} fusion(f32[1,1,12,44,8,96]{5,4,2,1,3,0:T(8,128)S(1)} %get-tuple-element.44, f32[2,2,8,96,96]{4,3,2,1,0:T(8,128)S(1)} %bitcast.200), kind=kOutput, calls=%fused_computation.71 | convolution fusion | flops 467140608 | bytes 4177920 | tf_op jit(solution)/shard_map/mhknb,nbc->mhknc/dot_general | solution.py:70
  107.3 3.7 %add_maximum_fusion = f32[8,12,44,96]{3,2,1,0:T(8,128)S(1)} fusion(f32[8,12,44,96]{3,2,1,0:T(8,128)S(1)} %fusion.46, f32[1,1,12,44,8,96]{5,4,2,1,3,0:T(8,128)S(1)} %get-tuple-element.43, f32[2,2,8,96,96]{4,3,2,1,0:T(8,128)S(1)} %bitcast.201), kind=kOutput, calls=%fused_computation.68 | convolution fusion | flops 467951616 | bytes 6537216 | tf_op jit(solution)/shard_map/mhknb,nbc->mhknc/dot_general | solution.py:70
  111.0 2.4 fusion.40
  113.3 3.6 %subtract_maximum_fusion = f32[8,12,44,96]{3,2,1,0:T(8,128)S(1)} fusion(f32[8,12,44,96]{3,2,1,0:T(8,128)S(1)} %fusion.47, f32[1,1,12,44,8,96]{5,4,2,1,3,0:T(8,128)S(1)} %get-tuple-element.43, f32[2,2,8,96,96]{4,3,2,1,0:T(8,128)S(1)} %bitcast.203), kind=kOutput, calls=%fused_computation.69 | convolution fusion | flops 467951616 | bytes 6537216 | tf_op jit(solution)/shard_map/mhknb,nbc->mhknc/dot_general | solution.py:70
  117.0 2.2 subtract_bitcast_fusion
  119.2 2.2 fusion.38
  121.4 2.3 add_bitcast_fusion
  123.7 0.7 pad_maximum_fusion
  124.4 4.6 %copy.35 = f32[1,2,12,44,8,96]{5,4,2,1,3,0:T(8,128)} copy(f32[1,2,12,44,8,96]{5,3,2,4,1,0:T(8,128)S(1)} %pad_maximum_fusion) | data formatting | bytes 6488064 | tf_op jit(solution)/shard_map/stack | solution.py:80
  129.0 5.1 %stack.25 = f32[24,44,768]{2,0,1:T(8,128)} reshape(f32[1,2,12,44,8,96]{5,4,2,1,3,0:T(8,128)} %copy.35) | data formatting | bytes 6488064 | tf_op jit(solution)/shard_map/stack | solution.py:80
  134.1 5.1 %fusion.54 = f32[1,24,44,768]{3,1,2,0:T(8,128)S(1)} fusion(f32[24,44,768]{2,0,1:T(8,128)} %stack.25, f32[12,12]{1,0:T(8,128)S(1)} %get-tuple-element.54, f32[12,12]{1,0:T(8,128)S(1)} %get-tuple-element.53, f32[12,12]{1,0:T(8,128)S(1)} %fusion.102), kind=kOutput, calls=%fused_computation.74 | convolution fusion | flops 235194048 | bytes 6489792 | tf_op jit(solution)/shard_map/ab,mbkd->makd/dot_general | solution.py:93
  139.2 3.3 %copy.36 = f32[1,24,44,768]{3,0,2,1:T(1,128)S(1)} copy(f32[1,24,44,768]{3,1,2,0:T(8,128)S(1)} %fusion.54) | data formatting | bytes 6488064 | tf_op jit(solution)/shard_map/ab,mbkd->makd/transpose | solution.py:93
  142.6 4.0 %copy.37 = f32[1,2,12,44,768]{4,0,3,1,2:T(1,128)} copy(f32[1,2,12,44,768]{4,0,3,2,1:T(1,128)S(1)} %bitcast.197) | data formatting | bytes 6488064 | tf_op jit(solution)/shard_map/reshape | solution.py:95
  146.6 5.2 %all-to-all-start.1 = ((f32[1,2,12,44,768]{4,0,3,1,2:T(1,128)}), f32[1,2,12,44,768]{4,0,3,1,2:T(1,128)}, u32[]{:S(2)}, u32[]{:S(2)}) async-start(f32[1,2,12,44,768]{4,0,3,1,2:T(1,128)} %copy.37), calls=%async_computation.1 | async-start | bytes 6488064 | tf_op jit(solution)/shard_map/all_to_all | solution.py:96
  151.8 0.4 all-gather.5.cloned.1.call-start
  152.3 0.3 all-gather.5.cloned.1.call-update
  152.6 1.0 fusion.80
  153.6 23.4 %all-to-all-done.1 = f32[1,2,12,44,768]{4,0,3,1,2:T(1,128)} async-done(((f32[1,2,12,44,768]{4,0,3,1,2:T(1,128)}), f32[1,2,12,44,768]{4,0,3,1,2:T(1,128)}, u32[]{:S(2)}, u32[]{:S(2)}) %all-to-all-start.1) | async-done | bytes 3244064 | tf_op jit(solution)/shard_map/all_to_all | solution.py:96
  177.1 3.6 %copy.38 = f32[1,2,12,44,768]{4,1,3,2,0:T(2,128)S(1)} copy(f32[1,2,12,44,768]{4,0,3,1,2:T(1,128)} %all-to-all-done.1) | data formatting | bytes 6488064 | tf_op jit(solution)/shard_map/all_to_all | solution.py:96
  180.7 0.0 copy-start.5
  180.7 1.1 copy.39
  181.8 0.0 copy-done.5
  181.8 4.5 %fusion.117 = (f32[6,180]{1,0:T(8,128)S(1)}, f32[1,6,180,768]{3,2,1,0:T(8,128)S(1)}) fusion(f32[1,88,180]{2,1,0:T(8,128)S(1)} %copy-done.5, f32[1,88,180]{2,1,0:T(8,128)S(1)} %get-tuple-element.45, f32[2,6,88,768]{3,0,2,1:T(2,128)S(1)} %bitcast.195, f32[1,6,180,768]{3,2,1,0:T(8,128)S(1)} %get-tuple-element.26, f32[768]{0:T(1024)S(1)} %get-tuple-element.38, ...), kind=kOutput, calls=%fused_computation.151 | convolution fusion | flops 1757613952 | bytes 10025376 | tf_op jit(solution)/shard_map/rkw,mrhkd->mhwd/dot_general | solution.py:97
  186.3 0.5 multiply_reduce_fusion
  186.9 1.1 copy-done.2
  188.0 0.6 add_convert_fusion
  188.6 0.6 reshape.335
  189.2 0.0 all-gather.3.cloned.1.call-done
  189.2 36.5 %fusion.19 = bf16[1080,3072]{1,0:T(8,128)(2,1)} fusion(bf16[1080,768]{1,0:T(8,128)(2,1)S(1)} %reshape.335, bf16[1,768,3072]{2,1,0:T(8,128)(2,1)} %all-gather.3.cloned.1.call-done), kind=kOutput, calls=%fused_computation.21 | convolution fusion | flops 5311733760 | bytes 13012992 | tf_op jit(solution)/shard_map/dot_general | solution.py:160
  225.7 7.5 %reshape.336 = bf16[6,180,3072]{2,1,0:T(8,128)(2,1)} reshape(bf16[1080,3072]{1,0:T(8,128)(2,1)} %fusion.19) | data formatting | bytes 13271040 | tf_op jit(solution)/shard_map/reshape.189
  233.2 2.1 all-gather.5.cloned.1.call-done
  235.3 9.0 %fusion.32 = bf16[1,6,180,768]{3,2,1,0:T(8,128)(2,1)S(1)} fusion(f32[1,6,180,768]{3,2,1,0:T(8,128)S(1)} %copy-done.3, bf16[6,180,3072]{2,1,0:T(8,128)(2,1)} %reshape.336, bf16[1,3072,768]{2,1,0:T(8,128)(2,1)} %all-gather.5.cloned.1.call-done), kind=kOutput, calls=%fused_computation.46 | convolution fusion | flops 5097738240 | bytes 16330752 | tf_op jit(solution)/shard_map/dot_general | solution.py:167
  244.4 34.1 %collective-permute-start = (bf16[1,6,180,768]{3,2,1,0:T(8,128)(2,1)S(1)}, bf16[1,6,180,768]{3,2,1,0:T(8,128)(2,1)S(1)}, u32[]{:S(2)}, u32[]{:S(2)}) collective-permute-start(bf16[1,6,180,768]{3,2,1,0:T(8,128)(2,1)S(1)} %fusion.32), channel_id=1, source_target_pairs={{0,4},{4,8},{8,12},{12,16},{16,20},{20,24},{24,28},{28,0},{1,5},{5... | collective-permute-start | bytes 4976648 | tf_op jit(solution)/shard_map/ppermute | solution.py:19
  278.5 18.7 %collective-permute-done = bf16[1,6,180,768]{3,2,1,0:T(8,128)(2,1)S(1)} collective-permute-done((bf16[1,6,180,768]{3,2,1,0:T(8,128)(2,1)S(1)}, bf16[1,6,180,768]{3,2,1,0:T(8,128)(2,1)S(1)}, u32[]{:S(2)}, u32[]{:S(2)}) %collective-permute-start) | collective-permute-done | bytes 1658912 | tf_op jit(solution)/shard_map/ppermute | solution.py:19
  297.2 1.2 copy.74
  (11 shorter events, 0.1 us)
Async XLA Ops:
  6.5 1.8 copy-start
  6.5 182.7 %all-gather.3.cloned.1.call-start = ((), (), s32[]{:S(2)}) async-start(), calls=%async_computation.2 | async-start | bytes 5898240 | tf_op jit(solution)/shard_map/all_gather | solution.py:162
  11.7 0.7 copy-start.7
  11.7 0.7 copy-start.8
  11.7 0.9 copy-start.6
  20.1 61.9 %all-to-all-start = ((f32[1,2,6,88,768]{4,1,2,0,3:T(2,128)}), f32[1,2,6,88,768]{4,1,2,0,3:T(2,128)}, u32[]{:S(2)}, u32[]{:S(2)}) async-start(f32[1,2,6,88,768]{4,1,2,0,3:T(2,128)} %copy.29), calls=%async_computation | async-start | bytes 6488064 | tf_op jit(solution)/shard_map/all_to_all | solution.py:88
  97.6 2.7 copy-start.4
  146.6 30.5 %all-to-all-start.1 = ((f32[1,2,12,44,768]{4,0,3,1,2:T(1,128)}), f32[1,2,12,44,768]{4,0,3,1,2:T(1,128)}, u32[]{:S(2)}, u32[]{:S(2)}) async-start(f32[1,2,12,44,768]{4,0,3,1,2:T(1,128)} %copy.37), calls=%async_computation.1 | async-start | bytes 6488064 | tf_op jit(solution)/shard_map/all_to_all | solution.py:96
  151.8 83.5 %all-gather.5.cloned.1.call-start = ((), (), s32[]{:S(2)}) async-start(), calls=%async_computation.3 | async-start | bytes 5898240 | tf_op jit(solution)/shard_map/all_gather | solution.py:169
  180.7 1.1 copy-start.5
  186.3 1.7 copy-start.2
  225.7 9.6 %copy-start.3 = (f32[1,6,180,768]{3,2,1,0:T(8,128)S(1)}, f32[1,6,180,768]{3,2,1,0:T(8,128)}, u32[]{:S(2)}) copy-start(f32[1,6,180,768]{3,2,1,0:T(8,128)} %copy-done.2) | copy-start | bytes 9953284
  235.3 63.0 %copy-start.1 = (bf16[100,768]{1,0:T(8,128)(2,1)S(1)}, bf16[100,768]{1,0:T(8,128)(2,1)}, u32[]{:S(2)}) copy-start(bf16[100,768]{1,0:T(8,128)(2,1)} %param.15) | copy-start | bytes 460804
  244.4 52.8 %collective-permute-start = (bf16[1,6,180,768]{3,2,1,0:T(8,128)(2,1)S(1)}, bf16[1,6,180,768]{3,2,1,0:T(8,128)(2,1)S(1)}, u32[]{:S(2)}, u32[]{:S(2)}) collective-permute-start(bf16[1,6,180,768]{3,2,1,0:T(8,128)(2,1)S(1)} %fusion.32), channel_id=1, source_target_pairs={{0,4},{4,8},{8,12},{12,16},{16,20},{20,24},{24,28},{28,0},{1,5},{5... | collective-permute-start | bytes 4976648 | tf_op jit(solution)/shard_map/ppermute | solution.py:19
Sparse Core Ops, SparseCore 0:
  9.2 85.4 all-gather.2
  154.5 80.7 all-gather.4
where the time goes:
time: 312 us; the launch traced here: 305 us
  waiting for transfers between devices  102 us (33%)
  matrix products  89.5 us (29%)
  local copies, waits for them, and re-layouts  48 us (15%)
  starting transfers between devices  45.2 us (14%)
  between operations  13.9 us (4%)
  other arithmetic  6.97 us (2%)
    all_to_all x1, waiting for transfers between devices, spectral_filter(): lax.all_to_all(spectra, 'space', split_axis=3, concat_axis=2, tiled=True)  56.3 us
    dot_general x1, matrix products, on_device(): jnp.dot(columns, lax.all_gather(up_weight, ('space', 'ens'), axis=1, tile...  36.5 us
    ppermute x1, starting transfers between devices, shifted(): return lax.ppermute(value, axis, pairs)  34.1 us
    all_to_all x1, waiting for transfers between devices, spectral_filter(): lax.all_to_all(inverse, 'space', split_axis=2, concat_axis=3, tiled=True)  23.4 us
    dot_general x8, matrix products, product(): jnp.einsum('mhknb,nbc->mhknc', operand, matrix, precision=HIGHEST_PRECISION)  23.3 us
    ppermute x1, waiting for transfers between devices, shifted(): return lax.ppermute(value, axis, pairs)  18.7 us
    another operation x2, local copies, waits for them, and re-layouts, mix_blocks(): blended = jnp.stack([second_real, second_imag], axis=1)  9.72 us
    dot_general x1, matrix products, on_device(): jnp.dot(columns, lax.all_gather(down_weight, ('space', 'ens'), axis=1, ti...  9.04 us
  transfers between devices with their start and end apart: 5, of which 4 were waited for; matrix products, arithmetic and copies ran while one was open for 43% of the time, Pallas kernels for 0%

commit v1 on v0

--- a/solution.py
+++ b/solution.py
@@ -1,8 +1,13 @@
+import functools
 import math
 
 import jax
 import jax.numpy as jnp
+import ml_dtypes
+import numpy as np
 from jax import lax
+from jax.experimental import pallas as pl
+from jax.experimental.pallas import tpu as pltpu
 from jax.sharding import PartitionSpec as P
 
 KW = 88
@@ -173,6 +178,621 @@
     return current[None, None]
 
 
+ROW_STEP = 192
+GROUP_LANES = 128
+MESH_AXES = ("segment", "space", "ens")
+
+
+def split_table(table):
+    high = table.astype(ml_dtypes.bfloat16)
+    low = (table - high.astype(np.float64)).astype(ml_dtypes.bfloat16)
+    return np.stack([high, low])
+
+
+def split_longitude_tables(longitudes, kept, latitudes):
+    number = np.arange(kept)[:, None]
+    points = np.arange(longitudes)[None, :]
+    angles = (number * points % longitudes) * (2.0 * math.pi / longitudes)
+    factor = 1.0 / math.sqrt(latitudes * longitudes)
+    doubled = np.where(number == 0, 1.0, 2.0) * factor
+    forward = np.concatenate([np.cos(angles) * factor, -np.sin(angles) * factor], 0)
+    backward = np.concatenate([np.cos(angles) * doubled, -np.sin(angles) * doubled], 0).T
+    return split_table(forward), split_table(backward)
+
+
+def three_point(x, sign):
+    (ar, ai), (br, bi), (cr, ci) = x
+    tr, ti = br + cr, bi + ci
+    mr, mi = ar - 0.5 * tr, ai - 0.5 * ti
+    scale = math.sin(math.pi / 3.0) * sign
+    dr, di = (br - cr) * scale, (bi - ci) * scale
+    return [(ar + tr, ai + ti), (mr - di, mi + dr), (mr + di, mi - dr)]
+
+
+def four_point(x, sign):
+    (ar, ai), (br, bi), (cr, ci), (dr, di) = x
+    sr, si, tr, ti = ar + cr, ai + ci, ar - cr, ai - ci
+    ur, ui, vr, vi = br + dr, bi + di, br - dr, bi - di
+    plus, minus = (tr - vi, ti + vr), (tr + vi, ti - vr)
+    if sign < 0:
+        plus, minus = minus, plus
+    return [(sr + ur, si + ui), plus, (sr - ur, si - ui), minus]
+
+
+def twelve_point(x, sign):
+    columns = [three_point([x[(4 * a + 3 * b) % 12] for a in range(3)], sign) for b in range(4)]
+    out = [None] * 12
+    for a in range(3):
+        line = four_point([columns[b][a] for b in range(4)], sign)
+        for b in range(4):
+            out[(4 * a + 9 * b) % 12] = line[b]
+    return out
+
+
+def lane_index(shape):
+    return lax.broadcasted_iota(jnp.int32, shape, len(shape) - 1)
+
+
+def spread_groups(values):
+    a, b, c = (values[:, 128 * i : 128 * i + 128] for i in range(3))
+    lanes = lane_index(a.shape)
+    second = jnp.where(lanes < 32, pltpu.roll(a, 32, 1), pltpu.roll(b, 32, 1))
+    third = jnp.where(lanes < 64, pltpu.roll(b, 64, 1), pltpu.roll(c, 64, 1))
+    return jnp.concatenate([a, second, third, pltpu.roll(c, 96, 1)], 1)
+
+
+def gather_groups(values):
+    a, b, c, d = (values[:, 128 * i : 128 * i + 128] for i in range(4))
+    lanes = lane_index(a.shape)
+    first = jnp.where(lanes < 96, a, pltpu.roll(b, 96, 1))
+    second = jnp.where(lanes < 64, pltpu.roll(b, 96, 1), pltpu.roll(c, 64, 1))
+    third = jnp.where(lanes < 32, pltpu.roll(c, 64, 1), pltpu.roll(d, 32, 1))
+    return jnp.concatenate([first, second, third], 1)
+
+
+def gelu(x):
+    return 0.5 * x * (1.0 + lax.erf(x * math.sqrt(0.5)))
+
+
+def enter_kernel(
+    scalars_ref,
+    state_ref,
+    readout_hbm,
+    lifting_hbm,
+    pos_hbm,
+    table_hbm,
+    out_ref,
+    readout_ref,
+    lifting_ref,
+    pos_ref,
+    table_ref,
+    rows_ref,
+    sems,
+):
+    first_segment, member = scalars_ref[0] == 0, scalars_ref[1]
+    rows, width = state_ref.shape[:2]
+
+    @pl.when(first_segment)
+    def _():
+        pairs = (
+            (readout_hbm, readout_ref),
+            (lifting_hbm, lifting_ref),
+            (pos_hbm, pos_ref),
+            (table_hbm, table_ref),
+        )
+        loads = [
+            pltpu.make_async_copy(source, target, sems.at[number])
+            for number, (source, target) in enumerate(pairs)
+        ]
+        for load in loads:
+            load.start()
+        rows_ref[...] = jnp.zeros_like(rows_ref)
+        for row in range(rows):
+            normed = layer_norm(state_ref[row].astype(jnp.float32)).astype(jnp.bfloat16)
+            rows_ref[pl.ds(ROW_STEP * row, width)] = normed
+        loads[0].wait()
+        loads[3].wait()
+        members = table_ref.shape[0]
+        chosen = lax.broadcasted_iota(jnp.int32, (8, members), 1) == member
+        line = jnp.dot(
+            jnp.where(chosen, 1.0, 0.0).astype(jnp.bfloat16),
+            table_ref[...],
+            preferred_element_type=jnp.float32,
+        )[0:1]
+        for first in range(0, rows, 2):
+            block = rows_ref[pl.ds(ROW_STEP * first, 2 * ROW_STEP)]
+            forecast = jnp.dot(block, readout_ref[...], preferred_element_type=jnp.float32)
+            if first == 0:
+                loads[1].wait()
+                loads[2].wait()
+            lifted = jnp.dot(
+                forecast.astype(jnp.bfloat16), lifting_ref[...], preferred_element_type=jnp.float32
+            )
+            for row in range(2):
+                part = lifted[ROW_STEP * row : ROW_STEP * row + width]
+                carried = part + pos_ref[first + row].astype(jnp.float32) + line
+                out_ref[first + row] = carried.astype(jnp.bfloat16)
+
+    @pl.when(jnp.logical_not(first_segment))
+    def _():
+        out_ref[...] = state_ref[...]
+
+
+def filter_kernel(
+    scalars_ref,
+    own_ref,
+    other_ref,
+    norms_ref,
+    forward_ref,
+    backward_ref,
+    first_ref,
+    second_ref,
+    out_ref,
+    grid_ref,
+    modes_ref,
+):
+    half = scalars_ref[0]
+    lower = half == 0
+    rows = own_ref.shape[0]
+    channels = own_ref.shape[2] // 2
+    kept = grid_ref.shape[1] // 2
+    groups = modes_ref.shape[0]
+    bases = (half * rows, (1 - half) * rows)
+
+    def dot(a, b):
+        return jnp.dot(a, b, preferred_element_type=jnp.float32)
+
+    def chosen(values):
+        return jnp.where(lower, values[:, :channels], values[:, channels:])
+
+    gain, shift = chosen(norms_ref[0:1]), chosen(norms_ref[2:3])
+    for row in range(rows):
+        for source, base in zip((own_ref, other_ref), bases):
+            values = source[row].astype(jnp.float32)
+            average = jnp.mean(values, axis=-1, keepdims=True)
+            centred = values - average
+            spread = jnp.mean(centred * centred, axis=-1, keepdims=True)
+            normed = chosen(centred) * lax.rsqrt(spread + EPSILON) * gain + shift
+            points = spread_groups(normed).astype(jnp.bfloat16)
+            grid_ref[base + row] = dot(forward_ref[0], points) + dot(forward_ref[1], points)
+
+    def turn(step, carry):
+        low = pl.multiple_of(step * 8, 8)
+        for group in range(groups):
+            lanes = pl.ds(GROUP_LANES * group, GROUP_LANES)
+            values = [
+                (grid_ref[h, pl.ds(low, 8), lanes], grid_ref[h, pl.ds(kept + low, 8), lanes])
+                for h in range(12)
+            ]
+            for k, (real, imag) in enumerate(twelve_point(values, -1)):
+                at = pl.ds(k * kept + low, 8)
+                modes_ref[group, at, pl.ds(0, GROUP_LANES)] = real
+                modes_ref[group, at, pl.ds(GROUP_LANES, GROUP_LANES)] = imag
+        return carry
+
+    lax.fori_loop(0, kept // 8, turn, 0)
+    for group in range(groups):
+        u = jax.nn.relu(dot(modes_ref[group].astype(jnp.bfloat16), first_ref[group]))
+        v = dot(u.astype(jnp.bfloat16), second_ref[group])
+        modes_ref[group] = v - jnp.clip(v, -SHRINK_LEVEL, SHRINK_LEVEL)
+
+    def turn_back(step, carry):
+        low = pl.multiple_of(step * 8, 8)
+        for group in range(groups):
+            lanes = pl.ds(GROUP_LANES * group, GROUP_LANES)
+            values = []
+            for k in range(12):
+                at = pl.ds(k * kept + low, 8)
+                values.append(
+                    (
+                        modes_ref[group, at, pl.ds(0, GROUP_LANES)],
+                        modes_ref[group, at, pl.ds(GROUP_LANES, GROUP_LANES)],
+                    )
+                )
+            for h, (real, imag) in enumerate(twelve_point(values, 1)):
+                grid_ref[h, pl.ds(low, 8), lanes] = real
+                grid_ref[h, pl.ds(kept + low, 8), lanes] = imag
+        return carry
+
+    lax.fori_loop(0, kept // 8, turn_back, 0)
+    for part, base in enumerate(bases):
+        for row in range(rows):
+            spectra = grid_ref[base + row].astype(jnp.bfloat16)
+            filtered = dot(backward_ref[0], spectra) + dot(backward_ref[1], spectra)
+            out_ref[part * rows + row] = gather_groups(filtered).astype(out_ref.dtype)
+
+
+def start_loads(near, near_refs, far_refs, targets, sems):
+    def copies(refs):
+        return [
+            pltpu.make_async_copy(ref, target, sems.at[number])
+            for number, (ref, target) in enumerate(zip(refs, targets))
+        ]
+
+    @pl.when(near)
+    def _():
+        for copy in copies(near_refs):
+            copy.start()
+
+    @pl.when(jnp.logical_not(near))
+    def _():
+        for copy in copies(far_refs):
+            copy.start()
+
+    return copies(near_refs)
+
+
+def hidden_kernel(
+    scalars_ref,
+    own_ref,
+    other_ref,
+    mine_ref,
+    theirs_ref,
+    norms_ref,
+    held_ref,
+    first_ref,
+    second_ref,
+    third_ref,
+    relayed_ref,
+    blended_ref,
+    hidden_ref,
+    rows_ref,
+    up_ref,
+    sems,
+):
+    half, space, member = scalars_ref[0], scalars_ref[1], scalars_ref[2]
+    rows, width, channels = own_ref.shape
+    depth = held_ref.shape[0]
+    here, away = 2 * space, 2 * (1 - space)
+    order = [here + member, here + 1 - member, away + member, away + 1 - member]
+    loads = start_loads(
+        half == space,
+        [held_ref, first_ref, second_ref, relayed_ref],
+        [second_ref, third_ref, first_ref, relayed_ref],
+        [up_ref.at[pl.ds(pl.multiple_of(shard * depth, depth), depth)] for shard in order],
+        sems,
+    )
+    rows_ref[...] = jnp.zeros_like(rows_ref)
+
+    def enter_rows(part, row):
+        source = (own_ref, other_ref)[part]
+        carried = source[row].astype(jnp.float32)
+        normed = layer_norm(carried) * norms_ref[0:1] + norms_ref[2:3]
+        mine = mine_ref[part * rows + row].astype(jnp.float32)
+        theirs = theirs_ref[(1 - part) * rows + row].astype(jnp.float32)
+        low = jnp.where(half == 0, mine, theirs)
+        high = jnp.where(half == 0, theirs, mine)
+        blended = carried + normed + jnp.concatenate([low, high], 1)
+        if part == 0:
+            blended_ref[row] = blended
+        again = layer_norm(blended) * norms_ref[1:2] + norms_ref[3:4]
+        place = row // 2 * 4 + part * 2 + row % 2
+        rows_ref[pl.ds(ROW_STEP * place, width)] = again.astype(jnp.bfloat16)
+
+    step = up_ref.shape[1] // 2
+    for block in range(rows // 2):
+        for part in range(2):
+            for row in range(2):
+                enter_rows(part, 2 * block + row)
+        if block == 0:
+            for copy in loads:
+                copy.wait()
+        at = pl.ds(4 * ROW_STEP * block, 4 * ROW_STEP)
+        values = rows_ref[at]
+        for column in range(0, up_ref.shape[1], step):
+            lifted = jnp.dot(
+                values, up_ref[:, pl.ds(column, step)], preferred_element_type=jnp.float32
+            )
+            hidden_ref[at, pl.ds(column, step)] = gelu(lifted).astype(jnp.bfloat16)
+
+
+def update_kernel(
+    number,
+    scalars_ref,
+    blended_ref,
+    hidden_ref,
+    held_ref,
+    near_ref,
+    far_ref,
+    relayed_ref,
+    own_ref,
+    other_ref,
+    down_ref,
+    sems,
+):
+    half, space, member = scalars_ref[0], scalars_ref[1], scalars_ref[2]
+    count, width, channels = own_ref.shape
+    depth = held_ref.shape[0]
+    loads = start_loads(
+        half == space,
+        [held_ref, near_ref],
+        [far_ref, relayed_ref],
+        [
+            down_ref.at[pl.ds(pl.multiple_of(shard * depth, depth), depth)]
+            for shard in (member, 1 - member)
+        ],
+        sems,
+    )
+    for copy in loads:
+        copy.wait()
+    block = hidden_ref[pl.ds(4 * ROW_STEP * number, 4 * ROW_STEP)]
+    update = jnp.dot(block, down_ref[...], preferred_element_type=jnp.float32)
+    for row in range(count):
+        part = update[ROW_STEP * row : ROW_STEP * row + width]
+        own_ref[row] = blended_ref[count * number + row] + part
+        part = update[ROW_STEP * (count + row) : ROW_STEP * (count + row) + width]
+        other_ref[row] = part.astype(other_ref.dtype)
+
+
+def collect_kernel(relayed_ref, *refs):
+    sources, out_ref, sems = refs[:-2], refs[-2], refs[-1]
+    parts = (len(sources) + 1) // 2
+    count = sources[0].shape[0]
+
+    def copies(step):
+        return [
+            pltpu.make_async_copy(
+                sources[min(2 * part + step, len(sources) - 1)],
+                out_ref.at[pl.ds(count * part, count)],
+                sems.at[part],
+            )
+            for part in range(parts)
+        ]
+
+    for step in range(2):
+
+        @pl.when(relayed_ref[0] == step)
+        def _():
+            for copy in copies(step):
+                copy.start()
+
+    for copy in copies(0):
+        copy.wait()
+
+
+VMEM = pltpu.VMEM
+SCALARS = pl.BlockSpec(memory_space=pltpu.SMEM)
+WHOLE = pl.BlockSpec(memory_space=pltpu.VMEM)
+LEFT = pl.BlockSpec(memory_space=pltpu.HBM)
+
+
+def cost(microseconds):
+    return pl.CostEstimate(
+        flops=int(microseconds * 1.1e9), bytes_accessed=0, transcendentals=0
+    )
+
+
+def params(megabytes):
+    return pltpu.CompilerParams(vmem_limit_bytes=megabytes * 2**20)
+
+
+def mixing_matrix(parts):
+    room = GROUP_LANES - parts.shape[-1]
+    real, imag = jnp.pad(parts, ((0, 0), (0, 0), (0, room), (0, room)))
+    top = jnp.concatenate([real, imag], 2)
+    low = jnp.concatenate([-imag, real], 2)
+    return jnp.concatenate([top, low], 1).astype(jnp.bfloat16)
+
+
+def fast_on_device(
+    sizes,
+    state_in,
+    member_ids,
+    member_table,
+    pos_embed,
+    readout_tile_matrix,
+    tile_lifting_matrix,
+    norm_gain,
+    norm_shift,
+    spectral,
+    up_weight,
+    down_weight,
+):
+    segments, spaces, members = sizes
+    position = lax.axis_index("segment")
+    core = position % 2
+    space = lax.axis_index("space")
+    member = lax.axis_index("ens")
+    near = core == space
+
+    def table(target):
+        pairs = []
+        for g in range(segments):
+            for s in range(spaces):
+                for e in range(members):
+                    to = target(g, s, e)
+                    if to is not None:
+                        flat = (to[0] * spaces + to[1]) * members + to[2]
+                        pairs.append(((g * spaces + s) * members + e, flat))
+        return pairs
+
+    def send(value, pairs):
+        return lax.ppermute(value, MESH_AXES, pairs)
+
+    def keeps(g, s):
+        return g % 2 == s
+
+    def moved_place(g, s, e):
+        return (g // 2 * 2 + s, g % 2, e)
+
+    relocate = table(moved_place)
+    far_relocate = table(lambda g, s, e: None if keeps(g, s) else moved_place(g, s, e))
+    first_way = table(lambda g, s, e: (g, s, 1 - e) if keeps(g, s) else moved_place(g, s, e))
+    second_way = table(lambda g, s, e: (g ^ 1, s, e) if keeps(g, s) else (g, 1 - s, e))
+    third_way = table(lambda g, s, e: (g ^ 1, s, 1 - e) if keeps(g, s) else None)
+    across = table(lambda g, s, e: (g, s, 1 - e))
+    near_across = table(lambda g, s, e: (g, s, 1 - e) if keeps(g, s) else None)
+    far_across = table(lambda g, s, e: (g, s, 1 - e) if not keeps(g, s) else None)
+    swap_cores = table(lambda g, s, e: (g ^ 1, s, e))
+    near_to_other = table(lambda g, s, e: (g ^ 1, s, e) if keeps(g, s) else None)
+    onward = table(lambda g, s, e: ((g // 2 * 2 + s + 1) % segments, g % 2, e))
+    onward_by_space = table(
+        lambda g, s, e: (g, 0, e)
+        if s == 1 and g % 2 == 0
+        else ((g // 2 * 2 + s + 1) % segments, g % 2, e)
+    )
+    onward_rest = table(
+        lambda g, s, e: ((g + 2) % segments, 0, e) if s == 0 and g % 2 == 0 else None
+    )
+
+    state = state_in[0, 0, 0]
+    rows, width, channels = state.shape
+    latitudes = rows * spaces
+    bf16, f32, i32 = jnp.bfloat16, jnp.float32, jnp.int32
+    up, down = up_weight[0], down_weight[0]
+    hidden_half = up.shape[1] // 2
+    scalars = jnp.stack([core, space, member]).astype(i32)
+
+    up_held = lax.dynamic_slice_in_dim(up, space * hidden_half, hidden_half, 1)
+    up_given = lax.dynamic_slice_in_dim(up, (1 - space) * hidden_half, hidden_half, 1)
+    up_first = send(up_held, first_way)
+    entered = pl.pallas_call(
+        enter_kernel,
+        out_shape=jax.ShapeDtypeStruct(state.shape, bf16),
+        in_specs=[SCALARS, WHOLE] + [LEFT] * 4,
+        out_specs=WHOLE,
+        scratch_shapes=[
+            VMEM(readout_tile_matrix.shape, bf16),
+            VMEM(tile_lifting_matrix.shape, bf16),
+            VMEM(pos_embed.shape, bf16),
+            VMEM(member_table.shape, bf16),
+            VMEM((rows * ROW_STEP, channels), bf16),
+            pltpu.SemaphoreType.DMA((4,)),
+        ],
+        cost_estimate=cost(9),
+        compiler_params=params(60),
+    )(
+        jnp.stack([position, member_ids[0, 0, 0]]).astype(i32),
+        state,
+        readout_tile_matrix,
+        tile_lifting_matrix,
+        pos_embed,
+        member_table,
+    )
+    entered, up_first = lax.optimization_barrier((entered, up_first))
+    moved = send(entered, relocate)
+    down_near = send(down, near_across)
+    up_third = send(up_given, third_way)
+
+    half_groups = spectral.shape[3] // 2
+    side = spectral.shape[-1]
+    norms = jnp.concatenate([norm_gain[0], norm_shift[0]], 0)
+    norm_lines = norms.reshape(-1, side)
+    wanted = lax.dynamic_slice_in_dim(spectral[0], core * half_groups, half_groups, 2)
+    offered = lax.dynamic_slice_in_dim(spectral[0], (1 - core) * half_groups, half_groups, 2)
+    offered = jnp.concatenate([offered.reshape(-1, side), norm_lines], 0)
+    taken = send(offered, near_to_other)
+    norms = jnp.where(near, norms, taken[-norm_lines.shape[0] :].reshape(norms.shape))
+    filters = jnp.where(near, wanted, taken[: -norm_lines.shape[0]].reshape(wanted.shape))
+    first_matrix = mixing_matrix(filters[0])
+    second_matrix = mixing_matrix(filters[1])
+
+    moved, up_given_later, down_near, up_third = lax.optimization_barrier(
+        (moved, up_given, down_near, up_third)
+    )
+    up_second = send(up_given_later, second_way)
+    moved_other = send(moved, swap_cores)
+    moved_other, up_second, norms, first_matrix, second_matrix = lax.optimization_barrier(
+        (moved_other, up_second, norms, first_matrix, second_matrix)
+    )
+    up_relayed = send(jnp.where(near, up_second, up_first), across)
+    _, down_later = lax.optimization_barrier((up_second, down))
+    down_far = send(down_later, far_relocate)
+
+    forward, backward = split_longitude_tables(width, KW, latitudes)
+    lanes = half_groups * GROUP_LANES
+    filtered = pl.pallas_call(
+        filter_kernel,
+        out_shape=jax.ShapeDtypeStruct((2 * rows, width, channels // 2), bf16),
+        in_specs=[SCALARS] + [WHOLE] * 7,
+        out_specs=WHOLE,
+        scratch_shapes=[
+            VMEM((latitudes, 2 * KW, lanes), f32),
+            VMEM((half_groups, latitudes * KW, 2 * GROUP_LANES), f32),
+        ],
+        cost_estimate=cost(11),
+        compiler_params=params(40),
+    )(
+        scalars,
+        moved,
+        moved_other,
+        norms,
+        jnp.asarray(forward),
+        jnp.asarray(backward),
+        first_matrix,
+        second_matrix,
+    )
+    filtered, down_far, up_relayed = lax.optimization_barrier((filtered, down_far, up_relayed))
+    down_relayed = send(down_far, far_across)
+    filtered_other = send(filtered, swap_cores)
+
+    parts = rows // 2
+    blended, hidden = pl.pallas_call(
+        hidden_kernel,
+        out_shape=[
+            VMEM(state.shape, f32),
+            VMEM((2 * rows * ROW_STEP, hidden_half), bf16),
+        ],
+        in_specs=[SCALARS] + [WHOLE] * 5 + [LEFT] * 5,
+        out_specs=[WHOLE] * 2,
+        scratch_shapes=[
+            VMEM((2 * rows * ROW_STEP, channels), bf16),
+            VMEM((channels, hidden_half), bf16),
+            pltpu.SemaphoreType.DMA((4,)),
+        ],
+        cost_estimate=cost(11),
+        compiler_params=params(40),
+    )(
+        scalars,
+        moved,
+        moved_other,
+        filtered,
+        filtered_other,
+        norms,
+        up_held,
+        up_first,
+        up_second,
+        up_third,
+        up_relayed,
+    )
+    landed, ready = [], []
+    for number in range(parts):
+        if number > 1:
+            scalars, _ = lax.optimization_barrier((scalars, ready[number - 2]))
+        own, other = pl.pallas_call(
+            functools.partial(update_kernel, number),
+            out_shape=[
+                jax.ShapeDtypeStruct((2, width, channels), f32),
+                jax.ShapeDtypeStruct((2, width, channels), bf16),
+            ],
+            in_specs=[SCALARS] + [WHOLE] * 2 + [LEFT] * 4,
+            out_specs=[WHOLE] * 2,
+            scratch_shapes=[
+                VMEM((2 * hidden_half // 2, channels), bf16),
+                pltpu.SemaphoreType.DMA((2,)),
+            ],
+            cost_estimate=cost(4),
+            compiler_params=params(24),
+        )(scalars, blended, hidden, down, down_near, down_far, down_relayed)
+        ready.append((own + send(other, swap_cores).astype(f32)).astype(bf16))
+        if number + 1 < parts:
+            first_hop = send(ready[-1], onward_by_space)
+            landed.append((first_hop, send(first_hop, onward_rest)))
+        else:
+            landed.append((send(ready[-1], onward),))
+    relayed = (core + space == 0).astype(i32)[None]
+    arrived = [value for chunk in landed for value in chunk]
+    out = pl.pallas_call(
+        collect_kernel,
+        out_shape=jax.ShapeDtypeStruct(state.shape, bf16),
+        in_specs=[SCALARS] + [LEFT] * len(arrived),
+        out_specs=LEFT,
+        scratch_shapes=[pltpu.SemaphoreType.DMA((parts,))],
+        compiler_params=params(16),
+    )(relayed, *arrived)
+    return out[None, None, None]
+
+
 def solution(mesh):
     placed = (
         P("ens", "segment", None, "space", None, None),
@@ -187,8 +807,14 @@
         P("segment", ("space", "ens"), None),
         P("segment", ("space", "ens"), None),
     )
+    sizes = tuple(mesh.shape[axis] for axis in MESH_AXES)
+    whole_micro_batch_on_a_chip = sizes[0] % 2 == 0 and sizes[1:] == (2, 2)
+    if whole_micro_batch_on_a_chip:
+        program = functools.partial(fast_on_device, sizes)
+    else:
+        program = on_device
     return jax.shard_map(
-        on_device,
+        program,
         mesh=mesh,
         in_specs=placed,
         out_specs=P("ens", "segment", None, "space", None, None),

time: 312 us -> 143 us (0.46)
  the two profiles are of different devices: /device:TPU:1 before, /device:TPU:0 now
where the time goes in v1:
time: 143 us; the launch traced here: 142 us
  waiting for transfers between devices  48.9 us (34%)
  Pallas kernels  48.2 us (34%)
  starting transfers between devices  21.1 us (15%)
  local copies, waits for them, and re-layouts  19 us (13%)
  other arithmetic  4.48 us (3%)
    ppermute x19, waiting for transfers between devices, send(): return lax.ppermute(value, MESH_AXES, pairs)  48.9 us
    ppermute x19, starting transfers between devices, send(): return lax.ppermute(value, MESH_AXES, pairs)  21.1 us
    pallas_call x1, Pallas kernels, fast_on_device(): pl.pallas_call(hidden_kernel, out_shape=[VMEM(state.shape, f32), VMEM((2...  13.5 us
    pallas_call x3, Pallas kernels, fast_on_device(): pl.pallas_call(functools.partial(update_kernel, number), out_shape=[jax.S...  12.2 us
    pallas_call x1, Pallas kernels, fast_on_device(): pl.pallas_call(filter_kernel, out_shape=jax.ShapeDtypeStruct((2 * rows, w...  10.9 us
    pallas_call x1, Pallas kernels, fast_on_device(): pl.pallas_call(enter_kernel, out_shape=jax.ShapeDtypeStruct(state.shape,...  10.3 us
    slice x2, local copies, waits for them, and re-layouts, fast_on_device(): taken[:-norm_lines.shape[0]].reshape(wanted.shape)  4.14 us
  transfers between devices with their start and end apart: 19, of which 10 were waited for; matrix products, arithmetic and copies ran while one was open for 12% of the time, Pallas kernels for 30%

profile of v1, /device:TPU:0, one launch (start us, length us, event | category | flops | bytes accessed | tf_op | source)
XLA Modules:
  0.0 142.2 jit_solution(1119501828918304351)
XLA Ops:
  0.0 2.2 %dynamic-slice_bitcast_fusion = (bf16[192,1536]{1,0:T(8,128)(2,1)}, bf16[192,1536]{1,0:T(8,128)(2,1)S(1)}) fusion(bf16[1,192,3072]{2,1,0:T(8,128)(2,1)} %param.22, s32[]{:T(128)S(6)} %select_n.45, s32[]{:T(128)S(6)} %select_n.44), kind=kLoop, calls=%fused_computation.5 | loop fusion | bytes 2359304 | tf_op jit(solution)/shard_map/dynamic_slice | solution.py:647
  2.2 3.0 %collective-permute-start = (bf16[192,1536]{1,0:T(8,128)(2,1)S(1)}, bf16[192,1536]{1,0:T(8,128)(2,1)S(1)}, u32[]{:S(2)}, u32[]{:S(2)}) collective-permute-start(bf16[192,1536]{1,0:T(8,128)(2,1)S(1)} %get-tuple-element.54.held_ref), channel_id=1, source_target_pairs={{0,1},{1,0},{2,4},{3,5},{4,2},{5,3},{6,7},{7,6},{8,9},{9,8},{10,12... | collective-permute-start | bytes 1769480 | tf_op jit(solution)/shard_map/ppermute | solution.py:610
  5.1 0.6 pad_add_fusion.1.scalars_ref
  5.8 10.3 %shard_map.127 = bf16[6,180,768]{2,1,0:T(8,128)(2,1)} custom-call(s32[2]{0:T(128)} %pad_add_fusion.1.scalars_ref, bf16[6,180,768]{2,1,0:T(8,128)(2,1)} %bitcast.47, bf16[768,1280]{1,0:T(8,128)(2,1)} %readout_hbm.1, bf16[1280,768]{1,0:T(8,128)(2,1)} %lifting_hbm.1, bf16[6,180,768]{2,1,0:T(8,128)(2,1)} %pos_hbm.1, bf16[100,768]{1,0:T(8,128)(2,1)} %table_hbm.1), custom_call_target="tpu_custom_call" | custom-call | flops 9900000256 | tf_op jit(solution)/shard_map/pallas_call | solution.py:649
  16.1 2.1 %collective-permute-start.1 = (bf16[6,180,768]{2,1,0:T(8,128)(2,1)}, bf16[6,180,768]{2,1,0:T(8,128)(2,1)S(1)}, u32[]{:S(2)}, u32[]{:S(2)}) collective-permute-start(bf16[6,180,768]{2,1,0:T(8,128)(2,1)} %shard_map.127), channel_id=1, source_target_pairs={{0,0},{1,1},{2,4},{3,5},{4,2},{5,3},{6,6},{7,7},{8,8},{9,9},{10,12... | collective-permute-start | bytes 4976648 | tf_op jit(solution)/shard_map/ppermute | solution.py:610
  18.2 1.9 %collective-permute-start.2 = (bf16[768,768]{1,0:T(8,128)(2,1)}, bf16[768,768]{1,0:T(8,128)(2,1)}, u32[]{:S(2)}, u32[]{:S(2)}) collective-permute-start(bf16[768,768]{1,0:T(8,128)(2,1)} %bitcast.36), channel_id=1, source_target_pairs={{0,1},{1,0},{6,7},{7,6},{8,9},{9,8},{14,15},{15,14},{16,17},{17,16... | collective-permute-start | bytes 3538952 | tf_op jit(solution)/shard_map/ppermute | solution.py:610
  20.2 2.7 %collective-permute-start.3 = (bf16[192,1536]{1,0:T(8,128)(2,1)}, bf16[192,1536]{1,0:T(8,128)(2,1)S(1)}, u32[]{:S(2)}, u32[]{:S(2)}) collective-permute-start(bf16[192,1536]{1,0:T(8,128)(2,1)} %get-tuple-element.31), channel_id=1, source_target_pairs={{0,5},{1,4},{6,3},{7,2},{8,13},{9,12},{14,11},{15,10},{16,21},{17,... | collective-permute-start | bytes 1769480 | tf_op jit(solution)/shard_map/ppermute | solution.py:610
  23.0 0.1 reshape.18
  23.0 0.1 copy.15
  23.1 2.1 %constant_dynamic-slice_fusion = f32[1,2,2,4,96,96]{5,4,3,2,1,0:T(8,128)} fusion(f32[1,2,2,8,96,96]{5,4,3,2,1,0:T(8,128)} %param.21, s32[]{:T(128)S(6)} %select_n.47), kind=kLoop, calls=%fused_computation.30 | loop fusion | bytes 1179652 | tf_op jit(solution)/shard_map/dynamic_slice | solution.py:682
  25.2 2.2 %copy.32 = f32[1536,96]{0,1:T(8,128)} copy(f32[1536,96]{1,0:T(8,128)} %bitcast.41) | data formatting | bytes 1179648 | tf_op jit(solution)/shard_map/reshape | solution.py:683
  27.4 2.0 %pad_maximum_fusion = f32[1568,96]{0,1:T(8,128)} fusion(f32[32,96]{0,1:T(8,128)S(1)} %copy.15, f32[1536,96]{0,1:T(8,128)} %copy.32), kind=kLoop, calls=%fused_computation.4 | loop fusion | flops 150528 | bytes 1204224 | tf_op jit(solution)/shard_map/concatenate | solution.py:683
  29.4 2.1 %collective-permute-start.6 = (f32[1568,96]{0,1:T(8,128)}, f32[1568,96]{0,1:T(8,128)}, u32[]{:S(2)}, u32[]{:S(2)}) collective-permute-start(f32[1568,96]{0,1:T(8,128)} %pad_maximum_fusion), channel_id=1, source_target_pairs={{0,4},{1,5},{6,2},{7,3},{8,12},{9,13},{14,10},{15,11},{16,20},{17,... | collective-permute-start | bytes 1806344 | tf_op jit(solution)/shard_map/ppermute | solution.py:610
  31.5 9.0 %collective-permute-done.3.third_ref = bf16[192,1536]{1,0:T(8,128)(2,1)S(1)} collective-permute-done((bf16[192,1536]{1,0:T(8,128)(2,1)}, bf16[192,1536]{1,0:T(8,128)(2,1)S(1)}, u32[]{:S(2)}, u32[]{:S(2)}) %collective-permute-start.3) | collective-permute-done | bytes 589856 | tf_op jit(solution)/shard_map/ppermute | solution.py:610
  40.5 2.3 %collective-permute-start.4 = (bf16[6,180,768]{2,1,0:T(8,128)(2,1)S(1)}, bf16[6,180,768]{2,1,0:T(8,128)(2,1)}, u32[]{:S(2)}, u32[]{:S(2)}) collective-permute-start(bf16[6,180,768]{2,1,0:T(8,128)(2,1)S(1)} %collective-permute-done.1.own_ref), channel_id=1, source_target_pairs={{0,4},{1,5},{2,6},{3,7},{4,0},{5,1},{6,2},{7,3},{8,12},{9,13},{10,... | collective-permute-start | bytes 4976648 | tf_op jit(solution)/shard_map/ppermute | solution.py:610
  42.8 0.1 pad_add_fusion.scalars_ref
  42.8 0.8 slice.20
  43.6 0.1 copy.16
  43.7 0.1 reshape.19
  43.8 1.9 %slice.21 = f32[1536,96]{0,1:T(8,128)} slice(f32[1568,96]{0,1:T(8,128)} %collective-permute-done.6), slice={[0:1536], [0:96]} | slice | bytes 1179648 | tf_op jit(solution)/shard_map/slice | solution.py:686
  45.7 2.2 %copy.17 = f32[1536,96]{1,0:T(8,128)} copy(f32[1536,96]{0,1:T(8,128)} %slice.21) | data formatting | bytes 1179648 | tf_op jit(solution)/shard_map/slice | solution.py:686
  47.9 1.2 bitcast_select_fusion
  49.2 0.1 fusion.4
  49.3 0.9 copy-done.5
  50.2 0.3 collective-permute-start.5
  50.8 9.3 %collective-permute-done.5.second_ref = bf16[192,1536]{1,0:T(8,128)(2,1)S(1)} collective-permute-done((bf16[192,1536]{1,0:T(8,128)(2,1)S(1)}, bf16[192,1536]{1,0:T(8,128)(2,1)S(1)}, u32[]{:S(2)}, u32[]{:S(2)}) %collective-permute-start.5) | collective-permute-done | bytes 589856 | tf_op jit(solution)/shard_map/ppermute | solution.py:610
  60.1 0.9 collective-permute-start.7
  61.0 0.1 broadcast_select_fusion
  61.1 0.1 collective-permute-start.8
  61.3 10.9 %shard_map.128.mine_ref = bf16[12,180,384]{2,1,0:T(8,128)(2,1)S(1)} custom-call(s32[3]{0:T(128)S(1)} %pad_add_fusion.scalars_ref, bf16[6,180,768]{2,1,0:T(8,128)(2,1)S(1)} %collective-permute-done.1.own_ref, bf16[6,180,768]{2,1,0:T(8,128)(2,1)} %collective-permute-done.4.other_ref, f32[4,768]{1,0:T(4,128)S(1)} %broadcast_select_fusion.1.norms_ref, ...), custom_call_target="tpu_custom_call" | custom-call | flops 12099999744 | tf_op jit(solution)/shard_map/pallas_call | solution.py:704
  72.2 5.1 %collective-permute-done.8.relayed_ref = bf16[192,1536]{1,0:T(8,128)(2,1)S(1)} collective-permute-done((bf16[192,1536]{1,0:T(8,128)(2,1)S(1)}, bf16[192,1536]{1,0:T(8,128)(2,1)S(1)}, u32[]{:S(2)}, u32[]{:S(2)}) %collective-permute-start.8) | collective-permute-done | bytes 589856 | tf_op jit(solution)/shard_map/ppermute | solution.py:610
  77.2 0.7 collective-permute-start.10
  78.0 2.8 %collective-permute-done.9.theirs_ref = bf16[12,180,384]{2,1,0:T(8,128)(2,1)S(1)} collective-permute-done((bf16[12,180,384]{2,1,0:T(8,128)(2,1)S(1)}, bf16[12,180,384]{2,1,0:T(8,128)(2,1)S(1)}, u32[]{:S(2)}, u32[]{:S(2)}) %collective-permute-start.9) | collective-permute-done | bytes 1658912 | tf_op jit(solution)/shard_map/ppermute | solution.py:610
  80.8 1.2 copy-done.8
  82.0 13.5 %shard_map.129 = (f32[6,180,768]{2,1,0:T(8,128)S(1)}, bf16[2304,1536]{1,0:T(8,128)(2,1)S(1)}) custom-call(s32[3]{0:T(128)S(1)} %pad_add_fusion.scalars_ref, bf16[6,180,768]{2,1,0:T(8,128)(2,1)} %copy-done, bf16[6,180,768]{2,1,0:T(8,128)(2,1)} %collective-permute-done.4.other_ref, bf16[12,180,384]{2,1,0:T(8,128)(2,1)} %copy-done.1, ...), custom_call_target="tpu_custom_call" | custom-call | flops 12099999744 | tf_op jit(solution)/shard_map/pallas_call | solution.py:730
  95.6 4.1 %shard_map.130 = (f32[2,180,768]{2,1,0:T(8,128)S(1)}, bf16[2,180,768]{2,1,0:T(8,128)(2,1)S(1)}) custom-call(s32[3]{0:T(128)S(1)} %pad_add_fusion.scalars_ref, f32[6,180,768]{2,1,0:T(8,128)S(1)} %get-tuple-element.42.blended_ref, bf16[2304,1536]{1,0:T(8,128)(2,1)S(1)} %get-tuple-element.43.hidden_ref, bf16[768,768]{1,0:T(8,128)(2,1)S(1)} %bitcast.38, ...), custom_call_target="tpu_custom_call" | custom-call | flops 4400000000 | tf_op jit(solution)/shard_map/pallas_call | solution.py:762
  99.7 0.4 copy.18
  100.1 0.1 collective-permute-start.11
  100.2 4.1 %shard_map.131 = (f32[2,180,768]{2,1,0:T(8,128)S(1)}, bf16[2,180,768]{2,1,0:T(8,128)(2,1)S(1)}) custom-call(s32[3]{0:T(128)S(1)} %pad_add_fusion.scalars_ref, f32[6,180,768]{2,1,0:T(8,128)S(1)} %get-tuple-element.42.blended_ref, bf16[2304,1536]{1,0:T(8,128)(2,1)S(1)} %get-tuple-element.43.hidden_ref, bf16[768,768]{1,0:T(8,128)(2,1)S(1)} %bitcast.39, ...), custom_call_target="tpu_custom_call" | custom-call | flops 4400000000 | tf_op jit(solution)/shard_map/pallas_call | solution.py:762
  104.3 0.4 copy.21
  104.7 0.1 collective-permute-start.14
  104.8 0.1 add_convert_fusion.2
  104.9 0.4 copy.20
  105.3 0.5 collective-permute-start.12
  105.9 0.8 collective-permute-done.14
  106.7 0.1 add_convert_fusion.1
  106.8 0.4 copy.23
  107.3 0.2 collective-permute-start.15
  107.5 4.1 %shard_map.132 = (f32[2,180,768]{2,1,0:T(8,128)S(1)}, bf16[2,180,768]{2,1,0:T(8,128)(2,1)S(1)}) custom-call(s32[3]{0:T(128)S(1)} %pad_add_fusion.scalars_ref, f32[6,180,768]{2,1,0:T(8,128)S(1)} %get-tuple-element.42.blended_ref, bf16[2304,1536]{1,0:T(8,128)(2,1)S(1)} %get-tuple-element.43.hidden_ref, bf16[768,768]{1,0:T(8,128)(2,1)S(1)} %bitcast.40, ...), custom_call_target="tpu_custom_call" | custom-call | flops 4400000000 | tf_op jit(solution)/shard_map/pallas_call | solution.py:762
  111.6 0.4 copy.24
  112.0 0.1 collective-permute-start.17
  112.1 2.8 %collective-permute-done.12 = bf16[2,180,768]{2,0,1:T(2,128)(2,1)S(1)} collective-permute-done((bf16[2,180,768]{2,0,1:T(2,128)(2,1)S(1)}, bf16[2,180,768]{2,0,1:T(2,128)(2,1)S(1)}, u32[]{:S(2)}, u32[]{:S(2)}) %collective-permute-start.12) | collective-permute-done | bytes 552992 | tf_op jit(solution)/shard_map/ppermute | solution.py:610
  114.9 1.9 %collective-permute-start.13 = (bf16[2,180,768]{2,0,1:T(2,128)(2,1)S(1)}, bf16[2,180,768]{2,0,1:T(2,128)(2,1)S(1)}, u32[]{:S(2)}, u32[]{:S(2)}) collective-permute-start(bf16[2,180,768]{2,0,1:T(2,128)(2,1)S(1)} %collective-permute-done.12), channel_id=1, source_target_pairs={{0,8},{1,9},{8,16},{9,17},{16,24},{17,25},{24,0},{25,1}} | collective-permute-start | bytes 1658888 | tf_op jit(solution)/shard_map/ppermute | solution.py:610
  116.8 4.1 %collective-permute-done.15 = bf16[2,180,768]{2,0,1:T(2,128)(2,1)} collective-permute-done((bf16[2,180,768]{2,0,1:T(2,128)(2,1)S(1)}, bf16[2,180,768]{2,0,1:T(2,128)(2,1)}, u32[]{:S(2)}, u32[]{:S(2)}) %collective-permute-start.15) | collective-permute-done | bytes 552992 | tf_op jit(solution)/shard_map/ppermute | solution.py:610
  120.9 1.9 %collective-permute-start.16 = (bf16[2,180,768]{2,0,1:T(2,128)(2,1)}, bf16[2,180,768]{2,0,1:T(2,128)(2,1)S(1)}, u32[]{:S(2)}, u32[]{:S(2)}) collective-permute-start(bf16[2,180,768]{2,0,1:T(2,128)(2,1)} %collective-permute-done.15), channel_id=1, source_target_pairs={{0,8},{1,9},{8,16},{9,17},{16,24},{17,25},{24,0},{25,1}} | collective-permute-start | bytes 1658888 | tf_op jit(solution)/shard_map/ppermute | solution.py:610
  122.9 0.1 add_convert_fusion
  123.0 0.4 copy.26
  123.4 0.1 collective-permute-start.18
  123.6 1.1 copy.29.refs_2_
  124.7 3.4 %collective-permute-done.13 = bf16[2,180,768]{2,0,1:T(2,128)(2,1)S(1)} collective-permute-done((bf16[2,180,768]{2,0,1:T(2,128)(2,1)S(1)}, bf16[2,180,768]{2,0,1:T(2,128)(2,1)S(1)}, u32[]{:S(2)}, u32[]{:S(2)}) %collective-permute-start.13) | collective-permute-done | bytes 552992 | tf_op jit(solution)/shard_map/ppermute | solution.py:610
  128.1 6.2 %collective-permute-done.16 = bf16[2,180,768]{2,0,1:T(2,128)(2,1)S(1)} collective-permute-done((bf16[2,180,768]{2,0,1:T(2,128)(2,1)}, bf16[2,180,768]{2,0,1:T(2,128)(2,1)S(1)}, u32[]{:S(2)}, u32[]{:S(2)}) %collective-permute-start.16) | collective-permute-done | bytes 552992 | tf_op jit(solution)/shard_map/ppermute | solution.py:610
  134.4 5.3 %collective-permute-done.18 = bf16[2,180,768]{2,0,1:T(2,128)(2,1)} collective-permute-done((bf16[2,180,768]{2,0,1:T(2,128)(2,1)S(1)}, bf16[2,180,768]{2,0,1:T(2,128)(2,1)}, u32[]{:S(2)}, u32[]{:S(2)}) %collective-permute-start.18) | collective-permute-done | bytes 552992 | tf_op jit(solution)/shard_map/ppermute | solution.py:610
  139.7 1.1 copy.31.refs_4_
  140.8 1.2 shard_map.133
  (37 shorter events, 0.5 us)
Async XLA Ops:
  0.0 5.1 %copy-start.9 = (s32[1,8,1]{1,2,0:T(1,128)S(1)}, s32[1,8,1]{1,2,0:T(1,128)}, u32[]{:S(2)}) copy-start(s32[1,8,1]{1,2,0:T(1,128)} %param.14) | copy-start | bytes 100
  2.2 14.0 %collective-permute-start = (bf16[192,1536]{1,0:T(8,128)(2,1)S(1)}, bf16[192,1536]{1,0:T(8,128)(2,1)S(1)}, u32[]{:S(2)}, u32[]{:S(2)}) collective-permute-start(bf16[192,1536]{1,0:T(8,128)(2,1)S(1)} %get-tuple-element.54.held_ref), channel_id=1, source_target_pairs={{0,1},{1,0},{2,4},{3,5},{4,2},{5,3},{6,7},{7,6},{8,9},{9,8},{10,12... | collective-permute-start | bytes 1769480 | tf_op jit(solution)/shard_map/ppermute | solution.py:610
  5.8 17.2 %copy-start.6 = (f32[1,2,768]{2,1,0:T(2,128)S(1)}, f32[1,2,768]{2,1,0:T(2,128)}, u32[]{:S(2)}) copy-start(f32[1,2,768]{2,1,0:T(2,128)} %param.20) | copy-start | bytes 18436
  5.8 17.2 %copy-start.7 = (f32[1,2,768]{2,1,0:T(2,128)S(1)}, f32[1,2,768]{2,1,0:T(2,128)}, u32[]{:S(2)}) copy-start(f32[1,2,768]{2,1,0:T(2,128)} %param.19) | copy-start | bytes 18436
  16.1 24.4 %collective-permute-start.1 = (bf16[6,180,768]{2,1,0:T(8,128)(2,1)}, bf16[6,180,768]{2,1,0:T(8,128)(2,1)S(1)}, u32[]{:S(2)}, u32[]{:S(2)}) collective-permute-start(bf16[6,180,768]{2,1,0:T(8,128)(2,1)} %shard_map.127), channel_id=1, source_target_pairs={{0,0},{1,1},{2,4},{3,5},{4,2},{5,3},{6,6},{7,7},{8,8},{9,9},{10,12... | collective-permute-start | bytes 4976648 | tf_op jit(solution)/shard_map/ppermute | solution.py:610
  18.2 22.3 %collective-permute-start.2 = (bf16[768,768]{1,0:T(8,128)(2,1)}, bf16[768,768]{1,0:T(8,128)(2,1)}, u32[]{:S(2)}, u32[]{:S(2)}) collective-permute-start(bf16[768,768]{1,0:T(8,128)(2,1)} %bitcast.36), channel_id=1, source_target_pairs={{0,1},{1,0},{6,7},{7,6},{8,9},{9,8},{14,15},{15,14},{16,17},{17,16... | collective-permute-start | bytes 3538952 | tf_op jit(solution)/shard_map/ppermute | solution.py:610
  20.2 20.3 %collective-permute-start.3 = (bf16[192,1536]{1,0:T(8,128)(2,1)}, bf16[192,1536]{1,0:T(8,128)(2,1)S(1)}, u32[]{:S(2)}, u32[]{:S(2)}) collective-permute-start(bf16[192,1536]{1,0:T(8,128)(2,1)} %get-tuple-element.31), channel_id=1, source_target_pairs={{0,5},{1,4},{6,3},{7,2},{8,13},{9,12},{14,11},{15,10},{16,21},{17,... | collective-permute-start | bytes 1769480 | tf_op jit(solution)/shard_map/ppermute | solution.py:610
  29.4 13.4 %collective-permute-start.6 = (f32[1568,96]{0,1:T(8,128)}, f32[1568,96]{0,1:T(8,128)}, u32[]{:S(2)}, u32[]{:S(2)}) collective-permute-start(f32[1568,96]{0,1:T(8,128)} %pad_maximum_fusion), channel_id=1, source_target_pairs={{0,4},{1,5},{6,2},{7,3},{8,12},{9,13},{14,10},{15,11},{16,20},{17,... | collective-permute-start | bytes 1806344 | tf_op jit(solution)/shard_map/ppermute | solution.py:610
  40.5 20.7 %copy-start = (bf16[6,180,768]{2,1,0:T(8,128)(2,1)}, bf16[6,180,768]{2,1,0:T(8,128)(2,1)S(1)}, u32[]{:S(2)}) copy-start(bf16[6,180,768]{2,1,0:T(8,128)(2,1)S(1)} %collective-permute-done.1.own_ref) | copy-start | bytes 4976644
  40.5 19.6 %collective-permute-start.4 = (bf16[6,180,768]{2,1,0:T(8,128)(2,1)S(1)}, bf16[6,180,768]{2,1,0:T(8,128)(2,1)}, u32[]{:S(2)}, u32[]{:S(2)}) collective-permute-start(bf16[6,180,768]{2,1,0:T(8,128)(2,1)S(1)} %collective-permute-done.1.own_ref), channel_id=1, source_target_pairs={{0,4},{1,5},{2,6},{3,7},{4,0},{5,1},{6,2},{7,3},{8,12},{9,13},{10,... | collective-permute-start | bytes 4976648 | tf_op jit(solution)/shard_map/ppermute | solution.py:610
  49.2 1.1 copy-start.5
  50.2 9.9 %collective-permute-start.5 = (bf16[192,1536]{1,0:T(8,128)(2,1)S(1)}, bf16[192,1536]{1,0:T(8,128)(2,1)S(1)}, u32[]{:S(2)}, u32[]{:S(2)}) collective-permute-start(bf16[192,1536]{1,0:T(8,128)(2,1)S(1)} %copy-done.5), channel_id=1, source_target_pairs={{0,4},{1,5},{2,0},{3,1},{4,6},{5,7},{6,2},{7,3},{8,12},{9,13},{10,... | collective-permute-start | bytes 1769480 | tf_op jit(solution)/shard_map/ppermute | solution.py:610
  50.6 9.5 %copy-start.2 = (bf16[1,768,768]{2,1,0:T(8,128)(2,1)S(1)}, bf16[1,768,768]{2,1,0:T(8,128)(2,1)}, u32[]{:S(2)}) copy-start(bf16[1,768,768]{2,1,0:T(8,128)(2,1)} %param.23) | copy-start | bytes 3538948
  50.7 10.6 %copy-start.3 = (bf16[2,180,176]{2,1,0:T(8,128)(2,1)S(1)}, bf16[2,180,176]{2,1,0:T(8,128)(2,1)}, u32[]{:S(2)}) copy-start(bf16[2,180,176]{2,1,0:T(8,128)(2,1)} %constant.46.clone.backward_ref) | copy-start | bytes 380164
  50.7 10.6 %copy-start.4 = (bf16[2,176,180]{2,1,0:T(8,128)(2,1)S(1)}, bf16[2,176,180]{2,1,0:T(8,128)(2,1)}, u32[]{:S(2)}) copy-start(bf16[2,176,180]{2,1,0:T(8,128)(2,1)} %constant.45.clone.forward_ref) | copy-start | bytes 380164
  60.1 17.1 %collective-permute-start.7 = (bf16[768,768]{1,0:T(8,128)(2,1)S(1)}, bf16[768,768]{1,0:T(8,128)(2,1)S(1)}, u32[]{:S(2)}, u32[]{:S(2)}) collective-permute-start(bf16[768,768]{1,0:T(8,128)(2,1)S(1)} %bitcast.37), channel_id=1, source_target_pairs={{2,4},{3,5},{4,2},{5,3},{10,12},{11,13},{12,10},{13,11},{18,20},{1... | collective-permute-start | bytes 3538952 | tf_op jit(solution)/shard_map/ppermute | solution.py:610
  61.1 16.1 %collective-permute-start.8 = (bf16[192,1536]{1,0:T(8,128)(2,1)S(1)}, bf16[192,1536]{1,0:T(8,128)(2,1)S(1)}, u32[]{:S(2)}, u32[]{:S(2)}) collective-permute-start(bf16[192,1536]{1,0:T(8,128)(2,1)S(1)} %broadcast_select_fusion), channel_id=1, source_target_pairs={{0,1},{1,0},{2,3},{3,2},{4,5},{5,4},{6,7},{7,6},{8,9},{9,8},{10,11... | collective-permute-start | bytes 1769480 | tf_op jit(solution)/shard_map/ppermute | solution.py:610
  72.2 8.7 %copy-start.1 = (bf16[12,180,384]{2,1,0:T(8,128)(2,1)}, bf16[12,180,384]{2,1,0:T(8,128)(2,1)S(1)}, u32[]{:S(2)}) copy-start(bf16[12,180,384]{2,1,0:T(8,128)(2,1)S(1)} %shard_map.128.mine_ref) | copy-start | bytes 4976644
  77.2 3.6 %collective-permute-start.9 = (bf16[12,180,384]{2,1,0:T(8,128)(2,1)S(1)}, bf16[12,180,384]{2,1,0:T(8,128)(2,1)S(1)}, u32[]{:S(2)}, u32[]{:S(2)}) collective-permute-start(bf16[12,180,384]{2,1,0:T(8,128)(2,1)S(1)} %shard_map.128.mine_ref), channel_id=1, source_target_pairs={{0,4},{1,5},{2,6},{3,7},{4,0},{5,1},{6,2},{7,3},{8,12},{9,13},{10,... | collective-permute-start | bytes 4976648 | tf_op jit(solution)/shard_map/ppermute | solution.py:610
  77.2 18.3 %collective-permute-start.10 = (bf16[768,768]{1,0:T(8,128)(2,1)S(1)}, bf16[768,768]{1,0:T(8,128)(2,1)S(1)}, u32[]{:S(2)}, u32[]{:S(2)}) collective-permute-start(bf16[768,768]{1,0:T(8,128)(2,1)S(1)} %collective-permute-done.7.far_ref), channel_id=1, source_target_pairs={{2,3},{3,2},{4,5},{5,4},{10,11},{11,10},{12,13},{13,12},{18,19},{1... | collective-permute-start | bytes 3538952 | tf_op jit(solution)/shard_map/ppermute | solution.py:610
  80.8 1.2 copy-start.8
  100.1 4.7 %collective-permute-start.11 = (bf16[2,180,768]{2,0,1:T(2,128)(2,1)S(1)}, bf16[2,180,768]{2,0,1:T(2,128)(2,1)S(1)}, u32[]{:S(2)}, u32[]{:S(2)}) collective-permute-start(bf16[2,180,768]{2,0,1:T(2,128)(2,1)S(1)} %copy.18), channel_id=1, source_target_pairs={{0,4},{1,5},{2,6},{3,7},{4,0},{5,1},{6,2},{7,3},{8,12},{9,13},{10,... | collective-permute-start | bytes 1658888 | tf_op jit(solution)/shard_map/ppermute | solution.py:610
  104.7 2.0 %collective-permute-start.14 = (bf16[2,180,768]{2,0,1:T(2,128)(2,1)S(1)}, bf16[2,180,768]{2,0,1:T(2,128)(2,1)S(1)}, u32[]{:S(2)}, u32[]{:S(2)}) collective-permute-start(bf16[2,180,768]{2,0,1:T(2,128)(2,1)S(1)} %copy.21), channel_id=1, source_target_pairs={{0,4},{1,5},{2,6},{3,7},{4,0},{5,1},{6,2},{7,3},{8,12},{9,13},{10,... | collective-permute-start | bytes 1658888 | tf_op jit(solution)/shard_map/ppermute | solution.py:610
  105.3 9.6 %collective-permute-start.12 = (bf16[2,180,768]{2,0,1:T(2,128)(2,1)S(1)}, bf16[2,180,768]{2,0,1:T(2,128)(2,1)S(1)}, u32[]{:S(2)}, u32[]{:S(2)}) collective-permute-start(bf16[2,180,768]{2,0,1:T(2,128)(2,1)S(1)} %copy.20), channel_id=1, source_target_pairs={{0,4},{1,5},{2,0},{3,1},{4,6},{5,7},{6,10},{7,11},{8,12},{9,13},{1... | collective-permute-start | bytes 1658888 | tf_op jit(solution)/shard_map/ppermute | solution.py:610
  107.3 13.7 %collective-permute-start.15 = (bf16[2,180,768]{2,0,1:T(2,128)(2,1)S(1)}, bf16[2,180,768]{2,0,1:T(2,128)(2,1)}, u32[]{:S(2)}, u32[]{:S(2)}) collective-permute-start(bf16[2,180,768]{2,0,1:T(2,128)(2,1)S(1)} %copy.23), channel_id=1, source_target_pairs={{0,4},{1,5},{2,0},{3,1},{4,6},{5,7},{6,10},{7,11},{8,12},{9,13},{1... | collective-permute-start | bytes 1658888 | tf_op jit(solution)/shard_map/ppermute | solution.py:610
  112.0 10.9 %collective-permute-start.17 = (bf16[2,180,768]{2,0,1:T(2,128)(2,1)S(1)}, bf16[2,180,768]{2,0,1:T(2,128)(2,1)S(1)}, u32[]{:S(2)}, u32[]{:S(2)}) collective-permute-start(bf16[2,180,768]{2,0,1:T(2,128)(2,1)S(1)} %copy.24), channel_id=1, source_target_pairs={{0,4},{1,5},{2,6},{3,7},{4,0},{5,1},{6,2},{7,3},{8,12},{9,13},{10,... | collective-permute-start | bytes 1658888 | tf_op jit(solution)/shard_map/ppermute | solution.py:610
  114.9 13.2 %collective-permute-start.13 = (bf16[2,180,768]{2,0,1:T(2,128)(2,1)S(1)}, bf16[2,180,768]{2,0,1:T(2,128)(2,1)S(1)}, u32[]{:S(2)}, u32[]{:S(2)}) collective-permute-start(bf16[2,180,768]{2,0,1:T(2,128)(2,1)S(1)} %collective-permute-done.12), channel_id=1, source_target_pairs={{0,8},{1,9},{8,16},{9,17},{16,24},{17,25},{24,0},{25,1}} | collective-permute-start | bytes 1658888 | tf_op jit(solution)/shard_map/ppermute | solution.py:610
  120.9 13.4 %collective-permute-start.16 = (bf16[2,180,768]{2,0,1:T(2,128)(2,1)}, bf16[2,180,768]{2,0,1:T(2,128)(2,1)S(1)}, u32[]{:S(2)}, u32[]{:S(2)}) collective-permute-start(bf16[2,180,768]{2,0,1:T(2,128)(2,1)} %collective-permute-done.15), channel_id=1, source_target_pairs={{0,8},{1,9},{8,16},{9,17},{16,24},{17,25},{24,0},{25,1}} | collective-permute-start | bytes 1658888 | tf_op jit(solution)/shard_map/ppermute | solution.py:610
  123.4 16.3 %collective-permute-start.18 = (bf16[2,180,768]{2,0,1:T(2,128)(2,1)S(1)}, bf16[2,180,768]{2,0,1:T(2,128)(2,1)}, u32[]{:S(2)}, u32[]{:S(2)}) collective-permute-start(bf16[2,180,768]{2,0,1:T(2,128)(2,1)S(1)} %copy.26), channel_id=1, source_target_pairs={{0,4},{1,5},{2,8},{3,9},{4,6},{5,7},{6,10},{7,11},{8,12},{9,13},{1... | collective-permute-start | bytes 1658888 | tf_op jit(solution)/shard_map/ppermute | solution.py:610

commit v2 on v1

--- a/solution.py
+++ b/solution.py
@@ -320,16 +320,25 @@
 
 def filter_kernel(
     scalars_ref,
-    own_ref,
-    other_ref,
+    entered_ref,
+    moved_ref,
+    near_state_ref,
+    far_state_ref,
     norms_ref,
+    taken_norms_ref,
     forward_ref,
     backward_ref,
-    first_ref,
-    second_ref,
+    filters_hbm,
+    taken_filters_hbm,
     out_ref,
     grid_ref,
     modes_ref,
+    filters_ref,
+    mixing_ref,
+    own_ref,
+    other_ref,
+    sem,
+    state_sems,
 ):
     half = scalars_ref[0]
     lower = half == 0
@@ -337,6 +346,21 @@
     channels = own_ref.shape[2] // 2
     kept = grid_ref.shape[1] // 2
     groups = modes_ref.shape[0]
+    side = filters_ref.shape[-1]
+    near = half == scalars_ref[1]
+    state_loads = start_loads(
+        near,
+        [entered_ref, far_state_ref],
+        [moved_ref, near_state_ref],
+        [own_ref, other_ref],
+        state_sems,
+    )
+    wanted = pl.ds(half * groups, groups)
+    own_load = pltpu.make_async_copy(filters_hbm.at[:, :, wanted], filters_ref, sem)
+    taken_load = pltpu.make_async_copy(taken_filters_hbm.at[:, :, wanted], filters_ref, sem)
+    pl.when(near)(own_load.start)
+    pl.when(jnp.logical_not(near))(taken_load.start)
+    norms = jnp.where(near, norms_ref[...], taken_norms_ref[...])
     bases = (half * rows, (1 - half) * rows)
 
     def dot(a, b):
@@ -345,9 +369,11 @@
     def chosen(values):
         return jnp.where(lower, values[:, :channels], values[:, channels:])
 
-    gain, shift = chosen(norms_ref[0:1]), chosen(norms_ref[2:3])
+    gain, shift = chosen(norms[0:1]), chosen(norms[2:3])
     for row in range(rows):
-        for source, base in zip((own_ref, other_ref), bases):
+        for source, base, load in zip((own_ref, other_ref), bases, state_loads):
+            if row == 0:
+                load.wait()
             values = source[row].astype(jnp.float32)
             average = jnp.mean(values, axis=-1, keepdims=True)
             centred = values - average
@@ -355,6 +381,18 @@
             normed = chosen(centred) * lax.rsqrt(spread + EPSILON) * gain + shift
             points = spread_groups(normed).astype(jnp.bfloat16)
             grid_ref[base + row] = dot(forward_ref[0], points) + dot(forward_ref[1], points)
+
+    mixing_ref[...] = jnp.zeros_like(mixing_ref)
+    own_load.wait()
+    first, second = pl.ds(0, side), pl.ds(GROUP_LANES, side)
+    for layer in range(2):
+        for group in range(groups):
+            real = filters_ref[layer, 0, group].astype(jnp.bfloat16)
+            imag = filters_ref[layer, 1, group].astype(jnp.bfloat16)
+            mixing_ref[layer, group, first, first] = real
+            mixing_ref[layer, group, first, second] = imag
+            mixing_ref[layer, group, second, first] = -imag
+            mixing_ref[layer, group, second, second] = real
 
     def turn(step, carry):
         low = pl.multiple_of(step * 8, 8)
@@ -372,8 +410,8 @@
 
     lax.fori_loop(0, kept // 8, turn, 0)
     for group in range(groups):
-        u = jax.nn.relu(dot(modes_ref[group].astype(jnp.bfloat16), first_ref[group]))
-        v = dot(u.astype(jnp.bfloat16), second_ref[group])
+        u = jax.nn.relu(dot(modes_ref[group].astype(jnp.bfloat16), mixing_ref[0, group]))
+        v = dot(u.astype(jnp.bfloat16), mixing_ref[1, group])
         modes_ref[group] = v - jnp.clip(v, -SHRINK_LEVEL, SHRINK_LEVEL)
 
     def turn_back(step, carry):
@@ -423,12 +461,16 @@
 
 
 def hidden_kernel(
+    count,
     scalars_ref,
-    own_ref,
-    other_ref,
+    entered_ref,
+    moved_ref,
+    near_state_ref,
+    far_state_ref,
     mine_ref,
     theirs_ref,
     norms_ref,
+    taken_norms_ref,
     held_ref,
     first_ref,
     second_ref,
@@ -438,10 +480,20 @@
     hidden_ref,
     rows_ref,
     up_ref,
+    own_ref,
+    other_ref,
     sems,
+    state_sems,
 ):
     half, space, member = scalars_ref[0], scalars_ref[1], scalars_ref[2]
     rows, width, channels = own_ref.shape
+    state_loads = start_loads(
+        half == space,
+        [entered_ref, far_state_ref],
+        [moved_ref, near_state_ref],
+        [own_ref, other_ref],
+        state_sems,
+    )
     depth = held_ref.shape[0]
     here, away = 2 * space, 2 * (1 - space)
     order = [here + member, here + 1 - member, away + member, away + 1 - member]
@@ -453,11 +505,12 @@
         sems,
     )
     rows_ref[...] = jnp.zeros_like(rows_ref)
+    norms = jnp.where(half == space, norms_ref[...], taken_norms_ref[...])
 
     def enter_rows(part, row):
         source = (own_ref, other_ref)[part]
         carried = source[row].astype(jnp.float32)
-        normed = layer_norm(carried) * norms_ref[0:1] + norms_ref[2:3]
+        normed = layer_norm(carried) * norms[0:1] + norms[2:3]
         mine = mine_ref[part * rows + row].astype(jnp.float32)
         theirs = theirs_ref[(1 - part) * rows + row].astype(jnp.float32)
         low = jnp.where(half == 0, mine, theirs)
@@ -465,19 +518,21 @@
         blended = carried + normed + jnp.concatenate([low, high], 1)
         if part == 0:
             blended_ref[row] = blended
-        again = layer_norm(blended) * norms_ref[1:2] + norms_ref[3:4]
-        place = row // 2 * 4 + part * 2 + row % 2
+        again = layer_norm(blended) * norms[1:2] + norms[3:4]
+        place = row // count * 2 * count + part * count + row % count
         rows_ref[pl.ds(ROW_STEP * place, width)] = again.astype(jnp.bfloat16)
 
+    for load in state_loads:
+        load.wait()
     step = up_ref.shape[1] // 2
-    for block in range(rows // 2):
+    for block in range(rows // count):
         for part in range(2):
-            for row in range(2):
-                enter_rows(part, 2 * block + row)
+            for row in range(count):
+                enter_rows(part, count * block + row)
         if block == 0:
             for copy in loads:
                 copy.wait()
-        at = pl.ds(4 * ROW_STEP * block, 4 * ROW_STEP)
+        at = pl.ds(2 * count * ROW_STEP * block, 2 * count * ROW_STEP)
         values = rows_ref[at]
         for column in range(0, up_ref.shape[1], step):
             lifted = jnp.dot(
@@ -513,10 +568,15 @@
         ],
         sems,
     )
-    for copy in loads:
+    rows_here = pl.ds(2 * count * ROW_STEP * number, 2 * count * ROW_STEP)
+    update = None
+    for copy, shard in zip(loads, (member, 1 - member)):
         copy.wait()
-    block = hidden_ref[pl.ds(4 * ROW_STEP * number, 4 * ROW_STEP)]
-    update = jnp.dot(block, down_ref[...], preferred_element_type=jnp.float32)
+        at = pl.ds(pl.multiple_of(shard * depth, depth), depth)
+        more = jnp.dot(
+            hidden_ref[rows_here, at], down_ref[at], preferred_element_type=jnp.float32
+        )
+        update = more if update is None else update + more
     for row in range(count):
         part = update[ROW_STEP * row : ROW_STEP * row + width]
         own_ref[row] = blended_ref[count * number + row] + part
@@ -524,15 +584,21 @@
         other_ref[row] = part.astype(other_ref.dtype)
 
 
+def place_kernel(start, chunk_ref, out_ref, sem):
+    copy = pltpu.make_async_copy(chunk_ref, out_ref.at[pl.ds(start, chunk_ref.shape[0])], sem)
+    copy.start()
+    copy.wait()
+
+
 def collect_kernel(relayed_ref, *refs):
-    sources, out_ref, sems = refs[:-2], refs[-2], refs[-1]
-    parts = (len(sources) + 1) // 2
+    sources, out_ref, sems = refs[:-3], refs[-2], refs[-1]
+    parts = len(sources) // 2
     count = sources[0].shape[0]
 
     def copies(step):
         return [
             pltpu.make_async_copy(
-                sources[min(2 * part + step, len(sources) - 1)],
+                sources[2 * part + step],
                 out_ref.at[pl.ds(count * part, count)],
                 sems.at[part],
             )
@@ -558,20 +624,12 @@
 
 def cost(microseconds):
     return pl.CostEstimate(
-        flops=int(microseconds * 1.1e9), bytes_accessed=0, transcendentals=0
+        flops=int(microseconds * 2e8), bytes_accessed=0, transcendentals=0
     )
 
 
 def params(megabytes):
     return pltpu.CompilerParams(vmem_limit_bytes=megabytes * 2**20)
-
-
-def mixing_matrix(parts):
-    room = GROUP_LANES - parts.shape[-1]
-    real, imag = jnp.pad(parts, ((0, 0), (0, 0), (0, room), (0, room)))
-    top = jnp.concatenate([real, imag], 2)
-    low = jnp.concatenate([-imag, real], 2)
-    return jnp.concatenate([top, low], 1).astype(jnp.bfloat16)
 
 
 def fast_on_device(
@@ -615,14 +673,14 @@
     def moved_place(g, s, e):
         return (g // 2 * 2 + s, g % 2, e)
 
-    relocate = table(moved_place)
     far_relocate = table(lambda g, s, e: None if keeps(g, s) else moved_place(g, s, e))
     first_way = table(lambda g, s, e: (g, s, 1 - e) if keeps(g, s) else moved_place(g, s, e))
     second_way = table(lambda g, s, e: (g ^ 1, s, e) if keeps(g, s) else (g, 1 - s, e))
+    near_across = table(lambda g, s, e: (g, s, 1 - e) if keeps(g, s) else None)
+    across = table(lambda g, s, e: (g, s, 1 - e))
     third_way = table(lambda g, s, e: (g ^ 1, s, 1 - e) if keeps(g, s) else None)
-    across = table(lambda g, s, e: (g, s, 1 - e))
-    near_across = table(lambda g, s, e: (g, s, 1 - e) if keeps(g, s) else None)
     far_across = table(lambda g, s, e: (g, s, 1 - e) if not keeps(g, s) else None)
+    far_to_other = table(lambda g, s, e: (g ^ 1, s, e) if not keeps(g, s) else None)
     swap_cores = table(lambda g, s, e: (g ^ 1, s, e))
     near_to_other = table(lambda g, s, e: (g ^ 1, s, e) if keeps(g, s) else None)
     onward = table(lambda g, s, e: ((g // 2 * 2 + s + 1) % segments, g % 2, e))
@@ -644,11 +702,13 @@
     scalars = jnp.stack([core, space, member]).astype(i32)
 
     up_held = lax.dynamic_slice_in_dim(up, space * hidden_half, hidden_half, 1)
-    up_given = lax.dynamic_slice_in_dim(up, (1 - space) * hidden_half, hidden_half, 1)
+    up_held, up_again = lax.optimization_barrier((up_held, up))
+    up_given = lax.dynamic_slice_in_dim(up_again, (1 - space) * hidden_half, hidden_half, 1)
     up_first = send(up_held, first_way)
+    up_second = send(up_given, second_way)
     entered = pl.pallas_call(
         enter_kernel,
-        out_shape=jax.ShapeDtypeStruct(state.shape, bf16),
+        out_shape=VMEM(state.shape, bf16),
         in_specs=[SCALARS, WHOLE] + [LEFT] * 4,
         out_specs=WHOLE,
         scratch_shapes=[
@@ -660,7 +720,7 @@
             pltpu.SemaphoreType.DMA((4,)),
         ],
         cost_estimate=cost(9),
-        compiler_params=params(60),
+        compiler_params=params(58),
     )(
         jnp.stack([position, member_ids[0, 0, 0]]).astype(i32),
         state,
@@ -669,86 +729,87 @@
         pos_embed,
         member_table,
     )
-    entered, up_first = lax.optimization_barrier((entered, up_first))
-    moved = send(entered, relocate)
-    down_near = send(down, near_across)
     up_third = send(up_given, third_way)
-
+    entered, up_first, up_second, up_third = lax.optimization_barrier(
+        (entered, up_first, up_second, up_third)
+    )
+    moved = send(entered, far_relocate)
+    near_state = send(entered, near_to_other)
+    up_relayed = send(jnp.where(near, up_second, up_first), across)
+    norms = jnp.concatenate([norm_gain[0], norm_shift[0]], 0)
+    taken_norms = send(norms, near_to_other)
+    filters = spectral[0]
+    taken_filters = send(filters, near_to_other)
+    moved, near_state, up_relayed, taken_norms, taken_filters, down_later = (
+        lax.optimization_barrier(
+            (moved, near_state, up_relayed, taken_norms, taken_filters, down)
+        )
+    )
+    far_state = send(moved, far_to_other)
+    down_far = send(down_later, far_relocate)
+    down_near = send(down_later, near_across)
+    states = (entered, moved, near_state, far_state)
+
+    forward, backward = split_longitude_tables(width, KW, latitudes)
     half_groups = spectral.shape[3] // 2
-    side = spectral.shape[-1]
-    norms = jnp.concatenate([norm_gain[0], norm_shift[0]], 0)
-    norm_lines = norms.reshape(-1, side)
-    wanted = lax.dynamic_slice_in_dim(spectral[0], core * half_groups, half_groups, 2)
-    offered = lax.dynamic_slice_in_dim(spectral[0], (1 - core) * half_groups, half_groups, 2)
-    offered = jnp.concatenate([offered.reshape(-1, side), norm_lines], 0)
-    taken = send(offered, near_to_other)
-    norms = jnp.where(near, norms, taken[-norm_lines.shape[0] :].reshape(norms.shape))
-    filters = jnp.where(near, wanted, taken[: -norm_lines.shape[0]].reshape(wanted.shape))
-    first_matrix = mixing_matrix(filters[0])
-    second_matrix = mixing_matrix(filters[1])
-
-    moved, up_given_later, down_near, up_third = lax.optimization_barrier(
-        (moved, up_given, down_near, up_third)
-    )
-    up_second = send(up_given_later, second_way)
-    moved_other = send(moved, swap_cores)
-    moved_other, up_second, norms, first_matrix, second_matrix = lax.optimization_barrier(
-        (moved_other, up_second, norms, first_matrix, second_matrix)
-    )
-    up_relayed = send(jnp.where(near, up_second, up_first), across)
-    _, down_later = lax.optimization_barrier((up_second, down))
-    down_far = send(down_later, far_relocate)
-
-    forward, backward = split_longitude_tables(width, KW, latitudes)
     lanes = half_groups * GROUP_LANES
     filtered = pl.pallas_call(
         filter_kernel,
         out_shape=jax.ShapeDtypeStruct((2 * rows, width, channels // 2), bf16),
-        in_specs=[SCALARS] + [WHOLE] * 7,
+        in_specs=[SCALARS] + [LEFT] * 4 + [WHOLE] * 4 + [LEFT] * 2,
         out_specs=WHOLE,
         scratch_shapes=[
             VMEM((latitudes, 2 * KW, lanes), f32),
             VMEM((half_groups, latitudes * KW, 2 * GROUP_LANES), f32),
+            VMEM((2, 2, half_groups) + filters.shape[3:], f32),
+            VMEM((2, half_groups, 2 * GROUP_LANES, 2 * GROUP_LANES), bf16),
+            VMEM(state.shape, bf16),
+            VMEM(state.shape, bf16),
+            pltpu.SemaphoreType.DMA,
+            pltpu.SemaphoreType.DMA((2,)),
         ],
         cost_estimate=cost(11),
-        compiler_params=params(40),
+        compiler_params=params(24),
     )(
         scalars,
-        moved,
-        moved_other,
+        *states,
         norms,
+        taken_norms,
         jnp.asarray(forward),
         jnp.asarray(backward),
-        first_matrix,
-        second_matrix,
-    )
-    filtered, down_far, up_relayed = lax.optimization_barrier((filtered, down_far, up_relayed))
+        filters,
+        taken_filters,
+    )
+    filtered, down_far, down_near = lax.optimization_barrier((filtered, down_far, down_near))
     down_relayed = send(down_far, far_across)
     filtered_other = send(filtered, swap_cores)
 
-    parts = rows // 2
+    parts = 2
     blended, hidden = pl.pallas_call(
-        hidden_kernel,
+        functools.partial(hidden_kernel, rows // parts),
         out_shape=[
             VMEM(state.shape, f32),
             VMEM((2 * rows * ROW_STEP, hidden_half), bf16),
         ],
-        in_specs=[SCALARS] + [WHOLE] * 5 + [LEFT] * 5,
+        in_specs=[SCALARS] + [LEFT] * 4 + [WHOLE] * 4 + [LEFT] * 5,
         out_specs=[WHOLE] * 2,
         scratch_shapes=[
             VMEM((2 * rows * ROW_STEP, channels), bf16),
             VMEM((channels, hidden_half), bf16),
+            VMEM(state.shape, bf16),
+            VMEM(state.shape, bf16),
             pltpu.SemaphoreType.DMA((4,)),
+            pltpu.SemaphoreType.DMA((2,)),
         ],
         cost_estimate=cost(11),
-        compiler_params=params(40),
+        compiler_params=params(30),
     )(
         scalars,
-        moved,
-        moved_other,
+        *states,
         filtered,
         filtered_other,
         norms,
+        taken_norms,
         up_held,
         up_first,
         up_second,
@@ -757,13 +818,11 @@
     )
     landed, ready = [], []
     for number in range(parts):
-        if number > 1:
-            scalars, _ = lax.optimization_barrier((scalars, ready[number - 2]))
         own, other = pl.pallas_call(
             functools.partial(update_kernel, number),
             out_shape=[
-                jax.ShapeDtypeStruct((2, width, channels), f32),
-                jax.ShapeDtypeStruct((2, width, channels), bf16),
+                jax.ShapeDtypeStruct((rows // parts, width, channels), f32),
+                jax.ShapeDtypeStruct((rows // parts, width, channels), bf16),
             ],
             in_specs=[SCALARS] + [WHOLE] * 2 + [LEFT] * 4,
             out_specs=[WHOLE] * 2,
@@ -771,25 +830,39 @@
                 VMEM((2 * hidden_half // 2, channels), bf16),
                 pltpu.SemaphoreType.DMA((2,)),
             ],
-            cost_estimate=cost(4),
+            cost_estimate=cost(50),
             compiler_params=params(24),
         )(scalars, blended, hidden, down, down_near, down_far, down_relayed)
         ready.append((own + send(other, swap_cores).astype(f32)).astype(bf16))
         if number + 1 < parts:
-            first_hop = send(ready[-1], onward_by_space)
-            landed.append((first_hop, send(first_hop, onward_rest)))
+            landed.append([send(ready[-1], onward_by_space)])
         else:
-            landed.append((send(ready[-1], onward),))
+            landed.append([send(ready[-1], onward)])
+    for number in range(parts - 1):
+        first_hop = landed[number][0]
+        if number > 0:
+            first_hop, _ = lax.optimization_barrier((first_hop, ready[-1]))
+        landed[number].append(send(first_hop, onward_rest))
     relayed = (core + space == 0).astype(i32)[None]
-    arrived = [value for chunk in landed for value in chunk]
+    out = pl.pallas_call(
+        functools.partial(place_kernel, rows // parts * (parts - 1)),
+        out_shape=jax.ShapeDtypeStruct(state.shape, bf16),
+        in_specs=[WHOLE],
+        out_specs=LEFT,
+        scratch_shapes=[pltpu.SemaphoreType.DMA],
+        cost_estimate=cost(100),
+        compiler_params=params(16),
+    )(landed[-1][0])
+    arrived = [value for chunk in landed[:-1] for value in chunk]
     out = pl.pallas_call(
         collect_kernel,
         out_shape=jax.ShapeDtypeStruct(state.shape, bf16),
-        in_specs=[SCALARS] + [LEFT] * len(arrived),
+        in_specs=[SCALARS] + [WHOLE] * len(arrived) + [LEFT],
         out_specs=LEFT,
-        scratch_shapes=[pltpu.SemaphoreType.DMA((parts,))],
+        input_output_aliases={1 + len(arrived): 0},
+        scratch_shapes=[pltpu.SemaphoreType.DMA((parts - 1,))],
         compiler_params=params(16),
-    )(relayed, *arrived)
+    )(relayed, *arrived, out)
     return out[None, None, None]
 
 

time: 143 us -> 129 us (0.902)
  local copies, waits for them, and re-layouts: 19 us -> 4.9 us
  starting transfers between devices: 21.1 us -> 33.6 us
  waiting for transfers between devices: 48.9 us -> 40.1 us
  Pallas kernels: 48.2 us -> 45.5 us
    ppermute x19 -> x18, starting transfers between devices: 21.1 us -> 33.6 us  [send(): return lax.ppermute(value, MESH_AXES, pairs)]
    ppermute x19 -> x18, waiting for transfers between devices: 48.9 us -> 40.1 us  [send(): return lax.ppermute(value, MESH_AXES, pairs)]
    slice x4 -> x0, local copies, waits for them, and re-layouts: 5.01 us -> none  [the longest x2 4.14 us: fast_on_device(): taken[:-norm_lines.shape[0]].reshape(wanted.shape)]
    dynamic_slice x2, local copies, waits for them, and re-layouts: 4.25 us -> 0.89 us  [the longest x1 0.85 us: fast_on_device(): lax.dynamic_slice_in_dim(up_again, (1 - space) * hidden_half, hidden_half...]
    reshape x4 -> x0, local copies, waits for them, and re-layouts: 2.47 us -> none  [the longest x1 2.21 us: fast_on_device(): offered = jnp.concatenate([offered.reshape(-1, side), norm_lines], 0)]
    ppermute x5 -> x0, local copies, waits for them, and re-layouts: 2.39 us -> none  [send(): return lax.ppermute(value, MESH_AXES, pairs)]
    concatenate x3 -> x0, other arithmetic: 2.06 us -> none  [the longest x1 1.95 us: fast_on_device(): offered = jnp.concatenate([offered.reshape(-1, side), norm_lines], 0)]
    convert_element_type x3 -> x2, other arithmetic: 0.35 us -> 2.28 us  [fast_on_device(): ready.append((own + send(other, swap_cores).astype(f32)).astype(bf16))]
  transfers between devices with their start and end apart: 19 -> 18, of which waited for: 10 -> 8; matrix products, arithmetic and copies ran while one was open for 12% -> 4% of each run, Pallas kernels for 30% -> 31%
where the time goes in v2:
time: 129 us
  Pallas kernels  45.5 us (35%)
  waiting for transfers between devices  40.1 us (31%)
  starting transfers between devices  33.6 us (26%)
  local copies, waits for them, and re-layouts  4.9 us (4%)
  other arithmetic  4.19 us (3%)
    ppermute x18, waiting for transfers between devices, send(): return lax.ppermute(value, MESH_AXES, pairs)  40.1 us
    ppermute x18, starting transfers between devices, send(): return lax.ppermute(value, MESH_AXES, pairs)  33.6 us
    pallas_call x1, Pallas kernels, fast_on_device(): pl.pallas_call(functools.partial(hidden_kernel, rows // parts), out_shape...  12.8 us
    pallas_call x1, Pallas kernels, fast_on_device(): pl.pallas_call(filter_kernel, out_shape=jax.ShapeDtypeStruct((2 * rows, w...  11.4 us
    pallas_call x2, Pallas kernels, fast_on_device(): pl.pallas_call(functools.partial(update_kernel, number), out_shape=[jax.S...  10.3 us
    pallas_call x1, Pallas kernels, fast_on_device(): pl.pallas_call(enter_kernel, out_shape=VMEM(state.shape, bf16), in_specs=...  9.18 us
    unnamed x16, local copies, waits for them, and re-layouts  4.01 us
  transfers between devices with their start and end apart: 18, of which 8 were waited for; matrix products, arithmetic and copies ran while one was open for 4% of the time, Pallas kernels for 31%

profile of v2, /device:TPU:0, one launch (start us, length us, event | category | flops | bytes accessed | tf_op | source)
XLA Modules:
  0.0 128.8 jit_solution(6891795256727422271)
XLA Ops:
  0.0 0.0 copy-start
  0.0 0.0 copy-start.7
  0.0 1.3 copy-done
  1.3 3.0 %collective-permute-start = (bf16[192,1536]{1,0:T(8,128)(2,1)S(1)}, bf16[192,1536]{1,0:T(8,128)(2,1)}, u32[]{:S(2)}, u32[]{:S(2)}) collective-permute-start(bf16[192,1536]{1,0:T(8,128)(2,1)S(1)} %dynamic-slice_bitcast_fusion.held_ref), channel_id=1, source_target_pairs={{0,1},{1,0},{2,4},{3,5},{4,2},{5,3},{6,7},{7,6},{8,9},{9,8},{10,12... | collective-permute-start | bytes 1769480 | tf_op jit(solution)/shard_map/ppermute | solution.py:668
  4.3 0.9 constant_dynamic-slice_fusion
  5.2 0.1 collective-permute-start.1
  5.3 3.9 %collective-permute-start.2 = (bf16[192,1536]{1,0:T(8,128)(2,1)}, bf16[192,1536]{1,0:T(8,128)(2,1)}, u32[]{:S(2)}, u32[]{:S(2)}) collective-permute-start(bf16[192,1536]{1,0:T(8,128)(2,1)} %constant_dynamic-slice_fusion), channel_id=1, source_target_pairs={{0,5},{1,4},{6,3},{7,2},{8,13},{9,12},{14,11},{15,10},{16,21},{17,... | collective-permute-start | bytes 1769480 | tf_op jit(solution)/shard_map/ppermute | solution.py:668
  9.1 0.0 copy-done.7
  9.1 0.7 pad_add_fusion.1.scalars_ref
  9.8 9.2 %shard_map.127.entered_ref = bf16[6,180,768]{2,1,0:T(8,128)(2,1)S(1)} custom-call(s32[2]{0:T(128)} %pad_add_fusion.1.scalars_ref, bf16[6,180,768]{2,1,0:T(8,128)(2,1)} %bitcast.17, bf16[768,1280]{1,0:T(8,128)(2,1)} %readout_hbm.1, bf16[1280,768]{1,0:T(8,128)(2,1)} %lifting_hbm.1, bf16[6,180,768]{2,1,0:T(8,128)(2,1)} %pos_hbm.1, bf16[100,768]{1,0:T(8,128)(2,1)} %table_hbm.1), custom_call_target="tpu_custom_call" | custom-call | flops 1800000000 | tf_op jit(solution)/shard_map/pallas_call | solution.py:709
  19.0 0.0 copy-start.5
  19.0 0.0 copy-start.6
  19.1 0.0 collective-permute-done.first_ref
  19.1 0.0 collective-permute-done.1.second_ref
  19.1 0.0 collective-permute-done.2.third_ref
  19.1 1.9 %collective-permute-start.3 = (bf16[6,180,768]{2,1,0:T(8,128)(2,1)S(1)}, bf16[6,180,768]{2,1,0:T(8,128)(2,1)}, u32[]{:S(2)}, u32[]{:S(2)}) collective-permute-start(bf16[6,180,768]{2,1,0:T(8,128)(2,1)S(1)} %shard_map.127.entered_ref), channel_id=1, source_target_pairs={{2,4},{3,5},{4,2},{5,3},{10,12},{11,13},{12,10},{13,11},{18,20},{1... | collective-permute-start | bytes 4976648 | tf_op jit(solution)/shard_map/ppermute | solution.py:668
  21.0 3.7 %collective-permute-start.4 = (bf16[6,180,768]{2,1,0:T(8,128)(2,1)S(1)}, bf16[6,180,768]{2,1,0:T(8,128)(2,1)}, u32[]{:S(2)}, u32[]{:S(2)}) collective-permute-start(bf16[6,180,768]{2,1,0:T(8,128)(2,1)S(1)} %shard_map.127.entered_ref), channel_id=1, source_target_pairs={{0,4},{1,5},{6,2},{7,3},{8,12},{9,13},{14,10},{15,11},{16,20},{17,... | collective-permute-start | bytes 4976648 | tf_op jit(solution)/shard_map/ppermute | solution.py:668
  24.6 2.5 %collective-permute-start.7 = (f32[2,2,8,96,96]{4,3,2,1,0:T(8,128)}, f32[2,2,8,96,96]{4,3,2,1,0:T(8,128)}, u32[]{:S(2)}, u32[]{:S(2)}) collective-permute-start(f32[2,2,8,96,96]{4,3,2,1,0:T(8,128)} %bitcast.11.filters_hbm), channel_id=1, source_target_pairs={{0,4},{1,5},{6,2},{7,3},{8,12},{9,13},{14,10},{15,11},{16,20},{17,... | collective-permute-start | bytes 3538952 | tf_op jit(solution)/shard_map/ppermute | solution.py:668
  27.1 1.1 broadcast_select_fusion
  28.2 1.6 %collective-permute-start.5 = (bf16[192,1536]{1,0:T(8,128)(2,1)S(1)}, bf16[192,1536]{1,0:T(8,128)(2,1)S(1)}, u32[]{:S(2)}, u32[]{:S(2)}) collective-permute-start(bf16[192,1536]{1,0:T(8,128)(2,1)S(1)} %broadcast_select_fusion), channel_id=1, source_target_pairs={{0,1},{1,0},{2,3},{3,2},{4,5},{5,4},{6,7},{7,6},{8,9},{9,8},{10,11... | collective-permute-start | bytes 1769480 | tf_op jit(solution)/shard_map/ppermute | solution.py:668
  29.8 0.0 copy-done.5
  29.8 0.0 copy-done.6
  29.8 1.3 %collective-permute-start.6 = (f32[4,768]{1,0:T(4,128)S(1)}, f32[4,768]{1,0:T(4,128)S(1)}, u32[]{:S(2)}, u32[]{:S(2)}) collective-permute-start(f32[4,768]{1,0:T(4,128)S(1)} %pad_maximum_fusion.norms_ref), channel_id=1, source_target_pairs={{0,4},{1,5},{6,2},{7,3},{8,12},{9,13},{14,10},{15,11},{16,20},{17,... | collective-permute-start | bytes 36872 | tf_op jit(solution)/shard_map/ppermute | solution.py:668
  31.1 0.8 collective-permute-done.6.taken_norms_ref
  31.9 8.6 %collective-permute-done.5.relayed_ref = bf16[192,1536]{1,0:T(8,128)(2,1)S(1)} collective-permute-done((bf16[192,1536]{1,0:T(8,128)(2,1)S(1)}, bf16[192,1536]{1,0:T(8,128)(2,1)S(1)}, u32[]{:S(2)}, u32[]{:S(2)}) %collective-permute-start.5) | collective-permute-done | bytes 589856 | tf_op jit(solution)/shard_map/ppermute | solution.py:668
  40.6 0.0 copy-start.1
  40.6 0.8 copy-done.1
  41.4 0.0 collective-permute-done.7.taken_filters_hbm
  41.4 0.0 collective-permute-done.3.moved_ref
  41.4 0.0 collective-permute-done.4.near_state_ref
  41.4 1.3 %collective-permute-start.8 = (bf16[6,180,768]{2,1,0:T(8,128)(2,1)}, bf16[6,180,768]{2,1,0:T(8,128)(2,1)}, u32[]{:S(2)}, u32[]{:S(2)}) collective-permute-start(bf16[6,180,768]{2,1,0:T(8,128)(2,1)} %collective-permute-done.3.moved_ref), channel_id=1, source_target_pairs={{2,6},{3,7},{4,0},{5,1},{10,14},{11,15},{12,8},{13,9},{18,22},{19,... | collective-permute-start | bytes 4976648 | tf_op jit(solution)/shard_map/ppermute | solution.py:668
  42.7 1.8 %collective-permute-start.9 = (bf16[768,768]{1,0:T(8,128)(2,1)}, bf16[768,768]{1,0:T(8,128)(2,1)}, u32[]{:S(2)}, u32[]{:S(2)}) collective-permute-start(bf16[768,768]{1,0:T(8,128)(2,1)} %bitcast.12.held_ref), channel_id=1, source_target_pairs={{2,4},{3,5},{4,2},{5,3},{10,12},{11,13},{12,10},{13,11},{18,20},{1... | collective-permute-start | bytes 3538952 | tf_op jit(solution)/shard_map/ppermute | solution.py:668
  44.5 3.4 %collective-permute-start.10 = (bf16[768,768]{1,0:T(8,128)(2,1)}, bf16[768,768]{1,0:T(8,128)(2,1)}, u32[]{:S(2)}, u32[]{:S(2)}) collective-permute-start(bf16[768,768]{1,0:T(8,128)(2,1)} %bitcast.12.held_ref), channel_id=1, source_target_pairs={{0,1},{1,0},{6,7},{7,6},{8,9},{9,8},{14,15},{15,14},{16,17},{17,16... | collective-permute-start | bytes 3538952 | tf_op jit(solution)/shard_map/ppermute | solution.py:668
  47.9 0.1 pad_add_fusion.scalars_ref
  48.0 0.0 collective-permute-done.8.far_state_ref
  48.0 0.0 copy-start.3
  48.0 1.0 copy-done.3
  49.0 0.0 copy-start.4
  49.0 0.9 copy-done.4
  49.9 11.4 %shard_map.128.mine_ref = bf16[12,180,384]{2,1,0:T(8,128)(2,1)S(1)} custom-call(s32[3]{0:T(128)S(1)} %pad_add_fusion.scalars_ref, bf16[6,180,768]{2,1,0:T(8,128)(2,1)S(1)} %shard_map.127.entered_ref, bf16[6,180,768]{2,1,0:T(8,128)(2,1)} %collective-permute-done.3.moved_ref, bf16[6,180,768]{2,1,0:T(8,128)(2,1)} %collective-permute-done.4.near_state_ref, ...), custom_call_target="tpu_custom_call" | custom-call | flops 2200000000 | tf_op jit(solution)/shard_map/pallas_call | solution.py:756
  61.3 0.0 collective-permute-done.9.far_ref
  61.3 1.6 %collective-permute-done.10.near_ref = bf16[768,768]{1,0:T(8,128)(2,1)} collective-permute-done((bf16[768,768]{1,0:T(8,128)(2,1)}, bf16[768,768]{1,0:T(8,128)(2,1)}, u32[]{:S(2)}, u32[]{:S(2)}) %collective-permute-start.10) | collective-permute-done | bytes 1179680 | tf_op jit(solution)/shard_map/ppermute | solution.py:668
  62.9 1.2 collective-permute-start.11
  64.1 0.7 collective-permute-start.12
  64.9 2.5 %collective-permute-done.11.theirs_ref = bf16[12,180,384]{2,1,0:T(8,128)(2,1)S(1)} collective-permute-done((bf16[12,180,384]{2,1,0:T(8,128)(2,1)S(1)}, bf16[12,180,384]{2,1,0:T(8,128)(2,1)S(1)}, u32[]{:S(2)}, u32[]{:S(2)}) %collective-permute-start.11) | collective-permute-done | bytes 1658912 | tf_op jit(solution)/shard_map/ppermute | solution.py:668
  67.3 0.0 copy-done.2
  67.3 12.8 %shard_map.129 = (f32[6,180,768]{2,1,0:T(8,128)S(1)}, bf16[2304,1536]{1,0:T(8,128)(2,1)S(1)}) custom-call(s32[3]{0:T(128)S(1)} %pad_add_fusion.scalars_ref, bf16[6,180,768]{2,1,0:T(8,128)(2,1)S(1)} %shard_map.127.entered_ref, bf16[6,180,768]{2,1,0:T(8,128)(2,1)} %collective-permute-done.3.moved_ref, ...), custom_call_target="tpu_custom_call" | custom-call | flops 2200000000 | tf_op jit(solution)/shard_map/pallas_call | solution.py:788
  80.2 0.0 collective-permute-done.12.relayed_ref
  80.2 5.2 %shard_map.130 = (f32[3,180,768]{2,1,0:T(8,128)S(1)}, bf16[3,180,768]{2,1,0:T(8,128)(2,1)S(1)}) custom-call(s32[3]{0:T(128)S(1)} %pad_add_fusion.scalars_ref, f32[6,180,768]{2,1,0:T(8,128)S(1)} %get-tuple-element.39.blended_ref, bf16[2304,1536]{1,0:T(8,128)(2,1)S(1)} %get-tuple-element.40.hidden_ref, bf16[768,768]{1,0:T(8,128)(2,1)} %bitcast.12.held_ref, ...), custom_call_target="tpu_custom_call" | custom-call | flops 10000000000 | tf_op jit(solution)/shard_map/pallas_call | solution.py:821
  85.3 1.0 collective-permute-start.13
  86.4 5.2 %shard_map.131 = (f32[3,180,768]{2,1,0:T(8,128)S(1)}, bf16[3,180,768]{2,1,0:T(8,128)(2,1)S(1)}) custom-call(s32[3]{0:T(128)S(1)} %pad_add_fusion.scalars_ref, f32[6,180,768]{2,1,0:T(8,128)S(1)} %get-tuple-element.39.blended_ref, bf16[2304,1536]{1,0:T(8,128)(2,1)S(1)} %get-tuple-element.40.hidden_ref, bf16[768,768]{1,0:T(8,128)(2,1)} %bitcast.12.held_ref, ...), custom_call_target="tpu_custom_call" | custom-call | flops 10000000000 | tf_op jit(solution)/shard_map/pallas_call | solution.py:821
  91.6 0.1 collective-permute-start.16
  91.6 0.0 collective-permute-done.13
  91.6 1.1 add_convert_fusion.1
  92.8 0.5 collective-permute-start.14
  93.3 0.7 collective-permute-done.16
  94.0 1.2 add_convert_fusion
  95.1 0.3 collective-permute-start.17
  95.4 14.2 %collective-permute-done.14.refs_0_ = bf16[3,180,768]{2,1,0:T(8,128)(2,1)S(1)} collective-permute-done((bf16[3,180,768]{2,1,0:T(8,128)(2,1)}, bf16[3,180,768]{2,1,0:T(8,128)(2,1)S(1)}, u32[]{:S(2)}, u32[]{:S(2)}) %collective-permute-start.14) | collective-permute-done | bytes 829472 | tf_op jit(solution)/shard_map/ppermute | solution.py:668
  109.6 5.5 %collective-permute-start.15 = (bf16[3,180,768]{2,1,0:T(8,128)(2,1)S(1)}, bf16[3,180,768]{2,1,0:T(8,128)(2,1)S(1)}, u32[]{:S(2)}, u32[]{:S(2)}) collective-permute-start(bf16[3,180,768]{2,1,0:T(8,128)(2,1)S(1)} %collective-permute-done.14.refs_0_), channel_id=1, source_target_pairs={{0,8},{1,9},{8,16},{9,17},{16,24},{17,25},{24,0},{25,1}} | collective-permute-start | bytes 2488328 | tf_op jit(solution)/shard_map/ppermute | solution.py:668
  115.1 4.8 %collective-permute-done.17.chunk_ref = bf16[3,180,768]{2,1,0:T(8,128)(2,1)S(1)} collective-permute-done((bf16[3,180,768]{2,1,0:T(8,128)(2,1)}, bf16[3,180,768]{2,1,0:T(8,128)(2,1)S(1)}, u32[]{:S(2)}, u32[]{:S(2)}) %collective-permute-start.17) | collective-permute-done | bytes 829472 | tf_op jit(solution)/shard_map/ppermute | solution.py:668
  119.8 0.9 shard_map.132.refs_2_
  120.8 6.9 %collective-permute-done.15.refs_1_ = bf16[3,180,768]{2,1,0:T(8,128)(2,1)S(1)} collective-permute-done((bf16[3,180,768]{2,1,0:T(8,128)(2,1)S(1)}, bf16[3,180,768]{2,1,0:T(8,128)(2,1)S(1)}, u32[]{:S(2)}, u32[]{:S(2)}) %collective-permute-start.15) | collective-permute-done | bytes 829472 | tf_op jit(solution)/shard_map/ppermute | solution.py:668
  127.7 0.9 shard_map.133
  (3 shorter events, 0.1 us)
Async XLA Ops:
  0.0 1.3 copy-start
  0.0 9.1 %copy-start.7 = (s32[1,8,1]{1,2,0:T(1,128)S(1)}, s32[1,8,1]{1,2,0:T(1,128)}, u32[]{:S(2)}) copy-start(s32[1,8,1]{1,2,0:T(1,128)} %param.14) | copy-start | bytes 100
  1.3 17.7 %collective-permute-start = (bf16[192,1536]{1,0:T(8,128)(2,1)S(1)}, bf16[192,1536]{1,0:T(8,128)(2,1)}, u32[]{:S(2)}, u32[]{:S(2)}) collective-permute-start(bf16[192,1536]{1,0:T(8,128)(2,1)S(1)} %dynamic-slice_bitcast_fusion.held_ref), channel_id=1, source_target_pairs={{0,1},{1,0},{2,4},{3,5},{4,2},{5,3},{6,7},{7,6},{8,9},{9,8},{10,12... | collective-permute-start | bytes 1769480 | tf_op jit(solution)/shard_map/ppermute | solution.py:668
  5.2 13.9 %collective-permute-start.1 = (bf16[192,1536]{1,0:T(8,128)(2,1)}, bf16[192,1536]{1,0:T(8,128)(2,1)}, u32[]{:S(2)}, u32[]{:S(2)}) collective-permute-start(bf16[192,1536]{1,0:T(8,128)(2,1)} %constant_dynamic-slice_fusion), channel_id=1, source_target_pairs={{0,4},{1,5},{2,0},{3,1},{4,6},{5,7},{6,2},{7,3},{8,12},{9,13},{10,... | collective-permute-start | bytes 1769480 | tf_op jit(solution)/shard_map/ppermute | solution.py:668
  5.3 13.8 %collective-permute-start.2 = (bf16[192,1536]{1,0:T(8,128)(2,1)}, bf16[192,1536]{1,0:T(8,128)(2,1)}, u32[]{:S(2)}, u32[]{:S(2)}) collective-permute-start(bf16[192,1536]{1,0:T(8,128)(2,1)} %constant_dynamic-slice_fusion), channel_id=1, source_target_pairs={{0,5},{1,4},{6,3},{7,2},{8,13},{9,12},{14,11},{15,10},{16,21},{17,... | collective-permute-start | bytes 1769480 | tf_op jit(solution)/shard_map/ppermute | solution.py:668
  19.0 10.8 %copy-start.5 = (f32[1,2,768]{2,1,0:T(2,128)S(1)}, f32[1,2,768]{2,1,0:T(2,128)}, u32[]{:S(2)}) copy-start(f32[1,2,768]{2,1,0:T(2,128)} %param.20) | copy-start | bytes 18436
  19.0 10.8 %copy-start.6 = (f32[1,2,768]{2,1,0:T(2,128)S(1)}, f32[1,2,768]{2,1,0:T(2,128)}, u32[]{:S(2)}) copy-start(f32[1,2,768]{2,1,0:T(2,128)} %param.19) | copy-start | bytes 18436
  19.1 22.3 %collective-permute-start.3 = (bf16[6,180,768]{2,1,0:T(8,128)(2,1)S(1)}, bf16[6,180,768]{2,1,0:T(8,128)(2,1)}, u32[]{:S(2)}, u32[]{:S(2)}) collective-permute-start(bf16[6,180,768]{2,1,0:T(8,128)(2,1)S(1)} %shard_map.127.entered_ref), channel_id=1, source_target_pairs={{2,4},{3,5},{4,2},{5,3},{10,12},{11,13},{12,10},{13,11},{18,20},{1... | collective-permute-start | bytes 4976648 | tf_op jit(solution)/shard_map/ppermute | solution.py:668
  21.0 20.4 %collective-permute-start.4 = (bf16[6,180,768]{2,1,0:T(8,128)(2,1)S(1)}, bf16[6,180,768]{2,1,0:T(8,128)(2,1)}, u32[]{:S(2)}, u32[]{:S(2)}) collective-permute-start(bf16[6,180,768]{2,1,0:T(8,128)(2,1)S(1)} %shard_map.127.entered_ref), channel_id=1, source_target_pairs={{0,4},{1,5},{6,2},{7,3},{8,12},{9,13},{14,10},{15,11},{16,20},{17,... | collective-permute-start | bytes 4976648 | tf_op jit(solution)/shard_map/ppermute | solution.py:668
  24.6 16.8 %collective-permute-start.7 = (f32[2,2,8,96,96]{4,3,2,1,0:T(8,128)}, f32[2,2,8,96,96]{4,3,2,1,0:T(8,128)}, u32[]{:S(2)}, u32[]{:S(2)}) collective-permute-start(f32[2,2,8,96,96]{4,3,2,1,0:T(8,128)} %bitcast.11.filters_hbm), channel_id=1, source_target_pairs={{0,4},{1,5},{6,2},{7,3},{8,12},{9,13},{14,10},{15,11},{16,20},{17,... | collective-permute-start | bytes 3538952 | tf_op jit(solution)/shard_map/ppermute | solution.py:668
  28.2 12.4 %collective-permute-start.5 = (bf16[192,1536]{1,0:T(8,128)(2,1)S(1)}, bf16[192,1536]{1,0:T(8,128)(2,1)S(1)}, u32[]{:S(2)}, u32[]{:S(2)}) collective-permute-start(bf16[192,1536]{1,0:T(8,128)(2,1)S(1)} %broadcast_select_fusion), channel_id=1, source_target_pairs={{0,1},{1,0},{2,3},{3,2},{4,5},{5,4},{6,7},{7,6},{8,9},{9,8},{10,11... | collective-permute-start | bytes 1769480 | tf_op jit(solution)/shard_map/ppermute | solution.py:668
  29.8 2.1 %collective-permute-start.6 = (f32[4,768]{1,0:T(4,128)S(1)}, f32[4,768]{1,0:T(4,128)S(1)}, u32[]{:S(2)}, u32[]{:S(2)}) collective-permute-start(f32[4,768]{1,0:T(4,128)S(1)} %pad_maximum_fusion.norms_ref), channel_id=1, source_target_pairs={{0,4},{1,5},{6,2},{7,3},{8,12},{9,13},{14,10},{15,11},{16,20},{17,... | collective-permute-start | bytes 36872 | tf_op jit(solution)/shard_map/ppermute | solution.py:668
  40.6 0.8 copy-start.1
  41.4 6.6 %collective-permute-start.8 = (bf16[6,180,768]{2,1,0:T(8,128)(2,1)}, bf16[6,180,768]{2,1,0:T(8,128)(2,1)}, u32[]{:S(2)}, u32[]{:S(2)}) collective-permute-start(bf16[6,180,768]{2,1,0:T(8,128)(2,1)} %collective-permute-done.3.moved_ref), channel_id=1, source_target_pairs={{2,6},{3,7},{4,0},{5,1},{10,14},{11,15},{12,8},{13,9},{18,22},{19,... | collective-permute-start | bytes 4976648 | tf_op jit(solution)/shard_map/ppermute | solution.py:668
  42.7 18.6 %collective-permute-start.9 = (bf16[768,768]{1,0:T(8,128)(2,1)}, bf16[768,768]{1,0:T(8,128)(2,1)}, u32[]{:S(2)}, u32[]{:S(2)}) collective-permute-start(bf16[768,768]{1,0:T(8,128)(2,1)} %bitcast.12.held_ref), channel_id=1, source_target_pairs={{2,4},{3,5},{4,2},{5,3},{10,12},{11,13},{12,10},{13,11},{18,20},{1... | collective-permute-start | bytes 3538952 | tf_op jit(solution)/shard_map/ppermute | solution.py:668
  44.5 18.4 %collective-permute-start.10 = (bf16[768,768]{1,0:T(8,128)(2,1)}, bf16[768,768]{1,0:T(8,128)(2,1)}, u32[]{:S(2)}, u32[]{:S(2)}) collective-permute-start(bf16[768,768]{1,0:T(8,128)(2,1)} %bitcast.12.held_ref), channel_id=1, source_target_pairs={{0,1},{1,0},{6,7},{7,6},{8,9},{9,8},{14,15},{15,14},{16,17},{17,16... | collective-permute-start | bytes 3538952 | tf_op jit(solution)/shard_map/ppermute | solution.py:668
  48.0 19.4 %copy-start.2 = (bf16[192,1536]{1,0:T(8,128)(2,1)S(1)}, bf16[192,1536]{1,0:T(8,128)(2,1)}, u32[]{:S(2)}) copy-start(bf16[192,1536]{1,0:T(8,128)(2,1)} %copy-done.1) | copy-start | bytes 1769476
  48.0 1.0 copy-start.3
  49.0 0.9 copy-start.4
  62.9 4.5 %collective-permute-start.11 = (bf16[12,180,384]{2,1,0:T(8,128)(2,1)S(1)}, bf16[12,180,384]{2,1,0:T(8,128)(2,1)S(1)}, u32[]{:S(2)}, u32[]{:S(2)}) collective-permute-start(bf16[12,180,384]{2,1,0:T(8,128)(2,1)S(1)} %shard_map.128.mine_ref), channel_id=1, source_target_pairs={{0,4},{1,5},{2,6},{3,7},{4,0},{5,1},{6,2},{7,3},{8,12},{9,13},{10,... | collective-permute-start | bytes 4976648 | tf_op jit(solution)/shard_map/ppermute | solution.py:668
  64.1 16.0 %collective-permute-start.12 = (bf16[768,768]{1,0:T(8,128)(2,1)}, bf16[768,768]{1,0:T(8,128)(2,1)S(1)}, u32[]{:S(2)}, u32[]{:S(2)}) collective-permute-start(bf16[768,768]{1,0:T(8,128)(2,1)} %collective-permute-done.9.far_ref), channel_id=1, source_target_pairs={{2,3},{3,2},{4,5},{5,4},{10,11},{11,10},{12,13},{13,12},{18,19},{1... | collective-permute-start | bytes 3538952 | tf_op jit(solution)/shard_map/ppermute | solution.py:668
  85.3 6.3 %collective-permute-start.13 = (bf16[3,180,768]{2,1,0:T(8,128)(2,1)S(1)}, bf16[3,180,768]{2,1,0:T(8,128)(2,1)S(1)}, u32[]{:S(2)}, u32[]{:S(2)}) collective-permute-start(bf16[3,180,768]{2,1,0:T(8,128)(2,1)S(1)} %get-tuple-element.44), channel_id=1, source_target_pairs={{0,4},{1,5},{2,6},{3,7},{4,0},{5,1},{6,2},{7,3},{8,12},{9,13},{10,... | collective-permute-start | bytes 2488328 | tf_op jit(solution)/shard_map/ppermute | solution.py:668
  91.6 2.4 %collective-permute-start.16 = (bf16[3,180,768]{2,1,0:T(8,128)(2,1)S(1)}, bf16[3,180,768]{2,1,0:T(8,128)(2,1)S(1)}, u32[]{:S(2)}, u32[]{:S(2)}) collective-permute-start(bf16[3,180,768]{2,1,0:T(8,128)(2,1)S(1)} %get-tuple-element.46), channel_id=1, source_target_pairs={{0,4},{1,5},{2,6},{3,7},{4,0},{5,1},{6,2},{7,3},{8,12},{9,13},{10,... | collective-permute-start | bytes 2488328 | tf_op jit(solution)/shard_map/ppermute | solution.py:668
  92.8 16.8 %collective-permute-start.14 = (bf16[3,180,768]{2,1,0:T(8,128)(2,1)}, bf16[3,180,768]{2,1,0:T(8,128)(2,1)S(1)}, u32[]{:S(2)}, u32[]{:S(2)}) collective-permute-start(bf16[3,180,768]{2,1,0:T(8,128)(2,1)} %add_convert_fusion.1), channel_id=1, source_target_pairs={{0,4},{1,5},{2,0},{3,1},{4,6},{5,7},{6,10},{7,11},{8,12},{9,13},{1... | collective-permute-start | bytes 2488328 | tf_op jit(solution)/shard_map/ppermute | solution.py:668
  95.1 24.7 %collective-permute-start.17 = (bf16[3,180,768]{2,1,0:T(8,128)(2,1)}, bf16[3,180,768]{2,1,0:T(8,128)(2,1)S(1)}, u32[]{:S(2)}, u32[]{:S(2)}) collective-permute-start(bf16[3,180,768]{2,1,0:T(8,128)(2,1)} %add_convert_fusion), channel_id=1, source_target_pairs={{0,4},{1,5},{2,8},{3,9},{4,6},{5,7},{6,10},{7,11},{8,12},{9,13},{1... | collective-permute-start | bytes 2488328 | tf_op jit(solution)/shard_map/ppermute | solution.py:668
  109.6 18.1 %collective-permute-start.15 = (bf16[3,180,768]{2,1,0:T(8,128)(2,1)S(1)}, bf16[3,180,768]{2,1,0:T(8,128)(2,1)S(1)}, u32[]{:S(2)}, u32[]{:S(2)}) collective-permute-start(bf16[3,180,768]{2,1,0:T(8,128)(2,1)S(1)} %collective-permute-done.14.refs_0_), channel_id=1, source_target_pairs={{0,8},{1,9},{8,16},{9,17},{16,24},{17,25},{24,0},{25,1}} | collective-permute-start | bytes 2488328 | tf_op jit(solution)/shard_map/ppermute | solution.py:668

commit v3 on v2

--- a/solution.py
+++ b/solution.py
@@ -197,7 +197,11 @@
     doubled = np.where(number == 0, 1.0, 2.0) * factor
     forward = np.concatenate([np.cos(angles) * factor, -np.sin(angles) * factor], 0)
     backward = np.concatenate([np.cos(angles) * doubled, -np.sin(angles) * doubled], 0).T
-    return split_table(forward), split_table(backward)
+    size = max(forward.shape)
+    both = np.zeros((2, size, size))
+    both[0, : forward.shape[0], : forward.shape[1]] = forward
+    both[1, : backward.shape[0], : backward.shape[1]] = backward
+    return split_table(both)
 
 
 def three_point(x, sign):
@@ -318,16 +322,83 @@
         out_ref[...] = state_ref[...]
 
 
+def load_one(near, near_ref, far_ref, target, sem):
+    near_copy = pltpu.make_async_copy(near_ref, target, sem)
+    far_copy = pltpu.make_async_copy(far_ref, target, sem)
+    pl.when(near)(near_copy.start)
+    pl.when(jnp.logical_not(near))(far_copy.start)
+    return near_copy
+
+
+def centre(values):
+    average = jnp.mean(values, axis=-1, keepdims=True)
+    centred = values - average
+    spread = jnp.mean(centred * centred, axis=-1, keepdims=True)
+    return centred, lax.rsqrt(spread + EPSILON)
+
+
+def dot(a, b):
+    return jnp.dot(a, b, preferred_element_type=jnp.float32)
+
+
+def row_spectra(lower, centred, factor, norms, forward):
+    channels = centred.shape[1] // 2
+
+    def chosen(values):
+        return jnp.where(lower, values[:, :channels], values[:, channels:])
+
+    normed = chosen(centred) * factor * chosen(norms[0:1]) + chosen(norms[2:3])
+    points = spread_groups(normed).astype(jnp.bfloat16)
+    return dot(forward[0], points) + dot(forward[1], points)
+
+
+def near_kernel(
+    scalars_ref,
+    entered_ref,
+    near_state_ref,
+    norms_ref,
+    taken_norms_ref,
+    tables_ref,
+    grid_ref,
+    base_ref,
+    state_ref,
+    sem,
+):
+    half, space = scalars_ref[0], scalars_ref[1]
+    near = half == space
+    load = load_one(near, entered_ref, near_state_ref, state_ref, sem)
+    rows, width, _ = state_ref.shape
+    norms = jnp.where(near, norms_ref[...], taken_norms_ref[...])
+    forward = [tables_ref[part, 0, : grid_ref.shape[1], :width] for part in range(2)]
+    load.wait()
+    for row in range(rows):
+        carried = state_ref[row].astype(jnp.float32)
+        centred, factor = centre(carried)
+        base_ref[row] = carried + (centred * factor * norms[0:1] + norms[2:3])
+        grid_ref[row] = row_spectra(half == 0, centred, factor, norms, forward)
+
+
+def base_kernel(
+    scalars_ref, moved_ref, far_state_ref, norms_ref, taken_norms_ref, base_ref, state_ref, sem
+):
+    near = scalars_ref[0] == scalars_ref[1]
+    load = load_one(near, far_state_ref, moved_ref, state_ref, sem)
+    norms = jnp.where(near, norms_ref[...], taken_norms_ref[...])
+    load.wait()
+    for row in range(state_ref.shape[0]):
+        carried = state_ref[row].astype(jnp.float32)
+        centred, factor = centre(carried)
+        base_ref[row] = carried + (centred * factor * norms[0:1] + norms[2:3])
+
+
 def filter_kernel(
     scalars_ref,
-    entered_ref,
     moved_ref,
-    near_state_ref,
     far_state_ref,
     norms_ref,
     taken_norms_ref,
-    forward_ref,
-    backward_ref,
+    tables_ref,
+    near_grid_ref,
     filters_hbm,
     taken_filters_hbm,
     out_ref,
@@ -335,53 +406,29 @@
     modes_ref,
     filters_ref,
     mixing_ref,
-    own_ref,
-    other_ref,
+    state_ref,
     sem,
-    state_sems,
+    state_sem,
 ):
-    half = scalars_ref[0]
-    lower = half == 0
-    rows = own_ref.shape[0]
-    channels = own_ref.shape[2] // 2
+    half, space = scalars_ref[0], scalars_ref[1]
+    near = half == space
+    load = load_one(near, far_state_ref, moved_ref, state_ref, state_sem)
+    rows, width, _ = state_ref.shape
     kept = grid_ref.shape[1] // 2
     groups = modes_ref.shape[0]
     side = filters_ref.shape[-1]
-    near = half == scalars_ref[1]
-    state_loads = start_loads(
-        near,
-        [entered_ref, far_state_ref],
-        [moved_ref, near_state_ref],
-        [own_ref, other_ref],
-        state_sems,
-    )
     wanted = pl.ds(half * groups, groups)
-    own_load = pltpu.make_async_copy(filters_hbm.at[:, :, wanted], filters_ref, sem)
-    taken_load = pltpu.make_async_copy(taken_filters_hbm.at[:, :, wanted], filters_ref, sem)
-    pl.when(near)(own_load.start)
-    pl.when(jnp.logical_not(near))(taken_load.start)
+    own_load = load_one(
+        near, filters_hbm.at[:, :, wanted], taken_filters_hbm.at[:, :, wanted], filters_ref, sem
+    )
     norms = jnp.where(near, norms_ref[...], taken_norms_ref[...])
-    bases = (half * rows, (1 - half) * rows)
-
-    def dot(a, b):
-        return jnp.dot(a, b, preferred_element_type=jnp.float32)
-
-    def chosen(values):
-        return jnp.where(lower, values[:, :channels], values[:, channels:])
-
-    gain, shift = chosen(norms[0:1]), chosen(norms[2:3])
+    odd_sign = jnp.where(space == 0, 1.0, -1.0)
+    forward = [tables_ref[part, 0, : 2 * kept, :width] for part in range(2)]
+    backward = [tables_ref[part, 1, :width, : 2 * kept] for part in range(2)]
+    load.wait()
     for row in range(rows):
-        for source, base, load in zip((own_ref, other_ref), bases, state_loads):
-            if row == 0:
-                load.wait()
-            values = source[row].astype(jnp.float32)
-            average = jnp.mean(values, axis=-1, keepdims=True)
-            centred = values - average
-            spread = jnp.mean(centred * centred, axis=-1, keepdims=True)
-            normed = chosen(centred) * lax.rsqrt(spread + EPSILON) * gain + shift
-            points = spread_groups(normed).astype(jnp.bfloat16)
-            grid_ref[base + row] = dot(forward_ref[0], points) + dot(forward_ref[1], points)
-
+        centred, factor = centre(state_ref[row].astype(jnp.float32))
+        grid_ref[rows + row] = row_spectra(half == 0, centred, factor, norms, forward)
     mixing_ref[...] = jnp.zeros_like(mixing_ref)
     own_load.wait()
     first, second = pl.ds(0, side), pl.ds(GROUP_LANES, side)
@@ -398,12 +445,16 @@
         low = pl.multiple_of(step * 8, 8)
         for group in range(groups):
             lanes = pl.ds(GROUP_LANES * group, GROUP_LANES)
-            values = [
-                (grid_ref[h, pl.ds(low, 8), lanes], grid_ref[h, pl.ds(kept + low, 8), lanes])
-                for h in range(12)
-            ]
+            values = []
+            for h in range(12):
+                source = near_grid_ref if h < rows else grid_ref
+                values.append(
+                    (source[h, pl.ds(low, 8), lanes], source[h, pl.ds(kept + low, 8), lanes])
+                )
             for k, (real, imag) in enumerate(twelve_point(values, -1)):
                 at = pl.ds(k * kept + low, 8)
+                if k % 2 == 1:
+                    real, imag = real * odd_sign, imag * odd_sign
                 modes_ref[group, at, pl.ds(0, GROUP_LANES)] = real
                 modes_ref[group, at, pl.ds(GROUP_LANES, GROUP_LANES)] = imag
         return carry
@@ -421,23 +472,21 @@
             values = []
             for k in range(12):
                 at = pl.ds(k * kept + low, 8)
-                values.append(
-                    (
-                        modes_ref[group, at, pl.ds(0, GROUP_LANES)],
-                        modes_ref[group, at, pl.ds(GROUP_LANES, GROUP_LANES)],
-                    )
-                )
+                real = modes_ref[group, at, pl.ds(0, GROUP_LANES)]
+                imag = modes_ref[group, at, pl.ds(GROUP_LANES, GROUP_LANES)]
+                if k % 2 == 1:
+                    real, imag = real * odd_sign, imag * odd_sign
+                values.append((real, imag))
             for h, (real, imag) in enumerate(twelve_point(values, 1)):
                 grid_ref[h, pl.ds(low, 8), lanes] = real
                 grid_ref[h, pl.ds(kept + low, 8), lanes] = imag
         return carry
 
     lax.fori_loop(0, kept // 8, turn_back, 0)
-    for part, base in enumerate(bases):
-        for row in range(rows):
-            spectra = grid_ref[base + row].astype(jnp.bfloat16)
-            filtered = dot(backward_ref[0], spectra) + dot(backward_ref[1], spectra)
-            out_ref[part * rows + row] = gather_groups(filtered).astype(out_ref.dtype)
+    for row in range(2 * rows):
+        spectra = grid_ref[row].astype(jnp.bfloat16)
+        filtered = dot(backward[0], spectra) + dot(backward[1], spectra)
+        out_ref[row] = gather_groups(filtered).astype(out_ref.dtype)
 
 
 def start_loads(near, near_refs, far_refs, targets, sems):
@@ -463,10 +512,8 @@
 def hidden_kernel(
     count,
     scalars_ref,
-    entered_ref,
-    moved_ref,
-    near_state_ref,
-    far_state_ref,
+    near_base_ref,
+    far_base_ref,
     mine_ref,
     theirs_ref,
     norms_ref,
@@ -476,112 +523,94 @@
     second_ref,
     third_ref,
     relayed_ref,
-    blended_ref,
+    down_held_ref,
+    down_first_ref,
+    partial_ref,
     hidden_ref,
     rows_ref,
     up_ref,
-    own_ref,
-    other_ref,
+    down_ref,
     sems,
-    state_sems,
+    down_sem,
 ):
     half, space, member = scalars_ref[0], scalars_ref[1], scalars_ref[2]
-    rows, width, channels = own_ref.shape
-    state_loads = start_loads(
-        half == space,
-        [entered_ref, far_state_ref],
-        [moved_ref, near_state_ref],
-        [own_ref, other_ref],
-        state_sems,
-    )
+    near = half == space
+    rows, width, channels = near_base_ref.shape
+    down_load = load_one(near, down_held_ref, down_first_ref, down_ref, down_sem)
     depth = held_ref.shape[0]
     here, away = 2 * space, 2 * (1 - space)
     order = [here + member, here + 1 - member, away + member, away + 1 - member]
     loads = start_loads(
-        half == space,
+        near,
         [held_ref, first_ref, second_ref, relayed_ref],
         [second_ref, third_ref, first_ref, relayed_ref],
         [up_ref.at[pl.ds(pl.multiple_of(shard * depth, depth), depth)] for shard in order],
         sems,
     )
     rows_ref[...] = jnp.zeros_like(rows_ref)
-    norms = jnp.where(half == space, norms_ref[...], taken_norms_ref[...])
-
-    def enter_rows(part, row):
-        source = (own_ref, other_ref)[part]
-        carried = source[row].astype(jnp.float32)
-        normed = layer_norm(carried) * norms[0:1] + norms[2:3]
+    norms = jnp.where(near, norms_ref[...], taken_norms_ref[...])
+
+    def enter_row(part, row):
         mine = mine_ref[part * rows + row].astype(jnp.float32)
-        theirs = theirs_ref[(1 - part) * rows + row].astype(jnp.float32)
+        theirs = theirs_ref[part * rows + row].astype(jnp.float32)
         low = jnp.where(half == 0, mine, theirs)
         high = jnp.where(half == 0, theirs, mine)
-        blended = carried + normed + jnp.concatenate([low, high], 1)
-        if part == 0:
-            blended_ref[row] = blended
-        again = layer_norm(blended) * norms[1:2] + norms[3:4]
+        base = (near_base_ref, far_base_ref)[part][row]
+        blended = base + jnp.concatenate([low, high], 1)
+        centred, factor = centre(blended)
+        again = centred * factor * norms[1:2] + norms[3:4]
         place = row // count * 2 * count + part * count + row % count
         rows_ref[pl.ds(ROW_STEP * place, width)] = again.astype(jnp.bfloat16)
-
-    for load in state_loads:
-        load.wait()
+        own = near if part == 0 else jnp.logical_not(near)
+        partial_ref[part * rows + row] = jnp.where(own, blended, 0.0)
+
     step = up_ref.shape[1] // 2
+    columns = [pl.ds(pl.multiple_of(m * step, step), step) for m in (member, 1 - member)]
     for block in range(rows // count):
-        for part in range(2):
-            for row in range(count):
-                enter_rows(part, count * block + row)
+        for row in range(count * block, count * block + count):
+            enter_row(0, row)
+            enter_row(1, row)
         if block == 0:
             for copy in loads:
                 copy.wait()
+            down_load.wait()
         at = pl.ds(2 * count * ROW_STEP * block, 2 * count * ROW_STEP)
         values = rows_ref[at]
-        for column in range(0, up_ref.shape[1], step):
-            lifted = jnp.dot(
-                values, up_ref[:, pl.ds(column, step)], preferred_element_type=jnp.float32
-            )
-            hidden_ref[at, pl.ds(column, step)] = gelu(lifted).astype(jnp.bfloat16)
+        hidden = gelu(dot(values, up_ref[:, columns[0]])).astype(jnp.bfloat16)
+        update = dot(hidden, down_ref[...])
+        for part in range(2):
+            for row in range(count):
+                start = ROW_STEP * (part * count + row)
+                partial_ref[part * rows + count * block + row] += update[start : start + width]
+        hidden_ref[at] = gelu(dot(values, up_ref[:, columns[1]])).astype(jnp.bfloat16)
 
 
 def update_kernel(
     number,
     scalars_ref,
-    blended_ref,
+    partial_ref,
     hidden_ref,
-    held_ref,
-    near_ref,
-    far_ref,
-    relayed_ref,
+    first_ref,
+    second_ref,
     own_ref,
     other_ref,
     down_ref,
-    sems,
+    sem,
 ):
-    half, space, member = scalars_ref[0], scalars_ref[1], scalars_ref[2]
-    count, width, channels = own_ref.shape
-    depth = held_ref.shape[0]
-    loads = start_loads(
-        half == space,
-        [held_ref, near_ref],
-        [far_ref, relayed_ref],
-        [
-            down_ref.at[pl.ds(pl.multiple_of(shard * depth, depth), depth)]
-            for shard in (member, 1 - member)
-        ],
-        sems,
-    )
-    rows_here = pl.ds(2 * count * ROW_STEP * number, 2 * count * ROW_STEP)
-    update = None
-    for copy, shard in zip(loads, (member, 1 - member)):
-        copy.wait()
-        at = pl.ds(pl.multiple_of(shard * depth, depth), depth)
-        more = jnp.dot(
-            hidden_ref[rows_here, at], down_ref[at], preferred_element_type=jnp.float32
-        )
-        update = more if update is None else update + more
-    for row in range(count):
-        part = update[ROW_STEP * row : ROW_STEP * row + width]
-        own_ref[row] = blended_ref[count * number + row] + part
-        part = update[ROW_STEP * (count + row) : ROW_STEP * (count + row) + width]
-        other_ref[row] = part.astype(other_ref.dtype)
+    near = scalars_ref[0] == scalars_ref[1]
+    load = load_one(near, first_ref, second_ref, down_ref, sem)
+    count, width, _ = own_ref.shape
+    rows = partial_ref.shape[0] // 2
+    size = count * ROW_STEP
+    own_part = jnp.where(near, 0, 1)
+    load.wait()
+    for target, part in ((other_ref, 1 - own_part), (own_ref, own_part)):
+        here = pl.ds(pl.multiple_of(2 * size * number + part * size, size), size)
+        update = dot(hidden_ref[here], down_ref[...])
+        for row in range(count):
+            more = update[ROW_STEP * row : ROW_STEP * row + width]
+            value = partial_ref[part * rows + count * number + row] + more
+            target[row] = value.astype(target.dtype)
 
 
 def place_kernel(start, chunk_ref, out_ref, sem):
@@ -676,10 +705,11 @@
     far_relocate = table(lambda g, s, e: None if keeps(g, s) else moved_place(g, s, e))
     first_way = table(lambda g, s, e: (g, s, 1 - e) if keeps(g, s) else moved_place(g, s, e))
     second_way = table(lambda g, s, e: (g ^ 1, s, e) if keeps(g, s) else (g, 1 - s, e))
-    near_across = table(lambda g, s, e: (g, s, 1 - e) if keeps(g, s) else None)
+    far_diagonal = table(
+        lambda g, s, e: None if keeps(g, s) else moved_place(g, s, 1 - e)
+    )
     across = table(lambda g, s, e: (g, s, 1 - e))
     third_way = table(lambda g, s, e: (g ^ 1, s, 1 - e) if keeps(g, s) else None)
-    far_across = table(lambda g, s, e: (g, s, 1 - e) if not keeps(g, s) else None)
     far_to_other = table(lambda g, s, e: (g ^ 1, s, e) if not keeps(g, s) else None)
     swap_cores = table(lambda g, s, e: (g ^ 1, s, e))
     near_to_other = table(lambda g, s, e: (g ^ 1, s, e) if keeps(g, s) else None)
@@ -699,7 +729,6 @@
     bf16, f32, i32 = jnp.bfloat16, jnp.float32, jnp.int32
     up, down = up_weight[0], down_weight[0]
     hidden_half = up.shape[1] // 2
-    scalars = jnp.stack([core, space, member]).astype(i32)
 
     up_held = lax.dynamic_slice_in_dim(up, space * hidden_half, hidden_half, 1)
     up_held, up_again = lax.optimization_barrier((up_held, up))
@@ -740,23 +769,28 @@
     taken_norms = send(norms, near_to_other)
     filters = spectral[0]
     taken_filters = send(filters, near_to_other)
-    moved, near_state, up_relayed, taken_norms, taken_filters, down_later = (
-        lax.optimization_barrier(
-            (moved, near_state, up_relayed, taken_norms, taken_filters, down)
-        )
-    )
-    far_state = send(moved, far_to_other)
-    down_far = send(down_later, far_relocate)
-    down_near = send(down_later, near_across)
-    states = (entered, moved, near_state, far_state)
-
-    forward, backward = split_longitude_tables(width, KW, latitudes)
+    scalars = jnp.stack([core, space, member]).astype(i32)
+    tables = jnp.asarray(split_longitude_tables(width, KW, latitudes))
     half_groups = spectral.shape[3] // 2
     lanes = half_groups * GROUP_LANES
+    near_grid, near_base = pl.pallas_call(
+        near_kernel,
+        out_shape=[VMEM((rows, 2 * KW, lanes), f32), VMEM(state.shape, f32)],
+        in_specs=[SCALARS] + [LEFT] * 2 + [WHOLE] * 3,
+        out_specs=[WHOLE] * 2,
+        scratch_shapes=[VMEM(state.shape, bf16), pltpu.SemaphoreType.DMA],
+        cost_estimate=cost(5),
+        compiler_params=params(12),
+    )(scalars, entered, near_state, norms, taken_norms, tables)
+    moved, near_grid, up_relayed, taken_filters, down_later = lax.optimization_barrier(
+        (moved, near_grid, up_relayed, taken_filters, down)
+    )
+    far_state = send(moved, far_to_other)
+    down_first = send(down_later, first_way)
     filtered = pl.pallas_call(
         filter_kernel,
         out_shape=jax.ShapeDtypeStruct((2 * rows, width, channels // 2), bf16),
-        in_specs=[SCALARS] + [LEFT] * 4 + [WHOLE] * 4 + [LEFT] * 2,
+        in_specs=[SCALARS] + [LEFT] * 2 + [WHOLE] * 4 + [LEFT] * 2,
         out_specs=WHOLE,
         scratch_shapes=[
             VMEM((latitudes, 2 * KW, lanes), f32),
@@ -764,48 +798,60 @@
             VMEM((2, 2, half_groups) + filters.shape[3:], f32),
             VMEM((2, half_groups, 2 * GROUP_LANES, 2 * GROUP_LANES), bf16),
             VMEM(state.shape, bf16),
-            VMEM(state.shape, bf16),
             pltpu.SemaphoreType.DMA,
-            pltpu.SemaphoreType.DMA((2,)),
+            pltpu.SemaphoreType.DMA,
         ],
         cost_estimate=cost(11),
         compiler_params=params(24),
     )(
         scalars,
-        *states,
+        moved,
+        far_state,
         norms,
         taken_norms,
-        jnp.asarray(forward),
-        jnp.asarray(backward),
+        tables,
+        near_grid,
         filters,
         taken_filters,
     )
-    filtered, down_far, down_near = lax.optimization_barrier((filtered, down_far, down_near))
-    down_relayed = send(down_far, far_across)
+    filtered, down_first, up_relayed, down_again = lax.optimization_barrier(
+        (filtered, down_first, up_relayed, down)
+    )
+    down_second = send(down_again, far_diagonal)
     filtered_other = send(filtered, swap_cores)
+    scalars_later, _ = lax.optimization_barrier((scalars, filtered))
+    far_base = pl.pallas_call(
+        base_kernel,
+        out_shape=VMEM(state.shape, f32),
+        in_specs=[SCALARS] + [LEFT] * 2 + [WHOLE] * 2,
+        out_specs=WHOLE,
+        scratch_shapes=[VMEM(state.shape, bf16), pltpu.SemaphoreType.DMA],
+        cost_estimate=cost(3),
+        compiler_params=params(12),
+    )(scalars_later, moved, far_state, norms, taken_norms)
 
     parts = 2
-    blended, hidden = pl.pallas_call(
+    partial, hidden = pl.pallas_call(
         functools.partial(hidden_kernel, rows // parts),
         out_shape=[
-            VMEM(state.shape, f32),
-            VMEM((2 * rows * ROW_STEP, hidden_half), bf16),
+            VMEM((2 * rows, width, channels), f32),
+            VMEM((2 * rows * ROW_STEP, hidden_half // 2), bf16),
         ],
-        in_specs=[SCALARS] + [LEFT] * 4 + [WHOLE] * 4 + [LEFT] * 5,
+        in_specs=[SCALARS] + [WHOLE] * 6 + [LEFT] * 7,
         out_specs=[WHOLE] * 2,
         scratch_shapes=[
             VMEM((2 * rows * ROW_STEP, channels), bf16),
             VMEM((channels, hidden_half), bf16),
-            VMEM(state.shape, bf16),
-            VMEM(state.shape, bf16),
+            VMEM((hidden_half // 2, channels), bf16),
             pltpu.SemaphoreType.DMA((4,)),
-            pltpu.SemaphoreType.DMA((2,)),
+            pltpu.SemaphoreType.DMA,
         ],
         cost_estimate=cost(11),
-        compiler_params=params(30),
+        compiler_params=params(26),
     )(
         scalars,
-        *states,
+        near_base,
+        far_base,
         filtered,
         filtered_other,
         norms,
@@ -815,6 +861,8 @@
         up_second,
         up_third,
         up_relayed,
+        down,
+        down_first,
     )
     landed, ready = [], []
     for number in range(parts):
@@ -824,15 +872,15 @@
                 jax.ShapeDtypeStruct((rows // parts, width, channels), f32),
                 jax.ShapeDtypeStruct((rows // parts, width, channels), bf16),
             ],
-            in_specs=[SCALARS] + [WHOLE] * 2 + [LEFT] * 4,
+            in_specs=[SCALARS] + [WHOLE] * 2 + [LEFT] * 2,
             out_specs=[WHOLE] * 2,
             scratch_shapes=[
-                VMEM((2 * hidden_half // 2, channels), bf16),
-                pltpu.SemaphoreType.DMA((2,)),
+                VMEM((hidden_half // 2, channels), bf16),
+                pltpu.SemaphoreType.DMA,
             ],
             cost_estimate=cost(50),
             compiler_params=params(24),
-        )(scalars, blended, hidden, down, down_near, down_far, down_relayed)
+        )(scalars, partial, hidden, down_first, down_second)
         ready.append((own + send(other, swap_cores).astype(f32)).astype(bf16))
         if number + 1 < parts:
             landed.append([send(ready[-1], onward_by_space)])

time: 129 us -> 122 us (0.946)
  starting transfers between devices: 33.6 us -> 25.7 us
    ppermute x18 -> x17, starting transfers between devices: 33.6 us -> 25.7 us  [send(): return lax.ppermute(value, MESH_AXES, pairs)]
    pallas_call x0 -> x2, Pallas kernels: none -> 6.65 us  [the longest x1 4.62 us: fast_on_device(): pl.pallas_call(near_kernel, out_shape=[VMEM((rows, 2 * KW, lanes), f32),...]
    pallas_call x2, Pallas kernels: 10.3 us -> 4.7 us  [fast_on_device(): pl.pallas_call(functools.partial(update_kernel, number), out_shape=[jax.S...]
    pallas_call x1, Pallas kernels: 11.4 us -> 8.75 us  [fast_on_device(): pl.pallas_call(filter_kernel, out_shape=jax.ShapeDtypeStruct((2 * rows, w...]
    ppermute x18 -> x17, waiting for transfers between devices: 40.1 us -> 40.7 us  [send(): return lax.ppermute(value, MESH_AXES, pairs)]
    unnamed x16 -> x28, local copies, waits for them, and re-layouts: 4.01 us -> 4.11 us
  transfers between devices with their start and end apart: 18 -> 17, of which waited for: 8 -> 9; matrix products, arithmetic and copies ran while one was open for 4% -> 5% of each run, Pallas kernels for 31% -> 34%
where the time goes in v3:
time: 122 us
  Pallas kernels  44.8 us (37%)
  waiting for transfers between devices  40.7 us (33%)
  starting transfers between devices  25.7 us (21%)
  local copies, waits for them, and re-layouts  5 us (4%)
  other arithmetic  4.98 us (4%)
    ppermute x17, waiting for transfers between devices, send(): return lax.ppermute(value, MESH_AXES, pairs)  40.7 us
    ppermute x17, starting transfers between devices, send(): return lax.ppermute(value, MESH_AXES, pairs)  25.7 us
    pallas_call x1, Pallas kernels, fast_on_device(): pl.pallas_call(functools.partial(hidden_kernel, rows // parts), out_shape...  12.5 us
    pallas_call x1, Pallas kernels, fast_on_device(): pl.pallas_call(enter_kernel, out_shape=VMEM(state.shape, bf16), in_specs=...  10.3 us
    pallas_call x1, Pallas kernels, fast_on_device(): pl.pallas_call(filter_kernel, out_shape=jax.ShapeDtypeStruct((2 * rows, w...  8.75 us
    pallas_call x2, Pallas kernels, fast_on_device(): pl.pallas_call(functools.partial(update_kernel, number), out_shape=[jax.S...  4.7 us
    pallas_call x1, Pallas kernels, fast_on_device(): pl.pallas_call(near_kernel, out_shape=[VMEM((rows, 2 * KW, lanes), f32),...  4.62 us
    unnamed x28, local copies, waits for them, and re-layouts  4.11 us
  transfers between devices with their start and end apart: 17, of which 9 were waited for; matrix products, arithmetic and copies ran while one was open for 5% of the time, Pallas kernels for 34%

profile of v3, /device:TPU:0, one launch (start us, length us, event | category | flops | bytes accessed | tf_op | source)
XLA Modules:
  0.0 121.6 jit_solution(12772339485450834245)
XLA Ops:
  0.0 0.0 copy-start
  0.0 1.3 %copy-done = bf16[1,192,3072]{2,1,0:T(8,128)(2,1)S(1)} copy-done((bf16[1,192,3072]{2,1,0:T(8,128)(2,1)S(1)}, bf16[1,192,3072]{2,1,0:T(8,128)(2,1)}, u32[]{:S(2)}) %copy-start) | copy-done | bytes 1179672
  1.3 3.0 %collective-permute-start = (bf16[192,1536]{1,0:T(8,128)(2,1)S(1)}, bf16[192,1536]{1,0:T(8,128)(2,1)S(1)}, u32[]{:S(2)}, u32[]{:S(2)}) collective-permute-start(bf16[192,1536]{1,0:T(8,128)(2,1)S(1)} %dynamic-slice_bitcast_fusion.held_ref), channel_id=1, source_target_pairs={{0,1},{1,0},{2,4},{3,5},{4,2},{5,3},{6,7},{7,6},{8,9},{9,8},{10,12... | collective-permute-start | bytes 1769480 | tf_op jit(solution)/shard_map/ppermute | solution.py:697
  4.3 0.9 constant_dynamic-slice_fusion
  5.2 0.1 collective-permute-start.1
  5.3 3.1 %collective-permute-start.2 = (bf16[192,1536]{1,0:T(8,128)(2,1)}, bf16[192,1536]{1,0:T(8,128)(2,1)S(1)}, u32[]{:S(2)}, u32[]{:S(2)}) collective-permute-start(bf16[192,1536]{1,0:T(8,128)(2,1)} %constant_dynamic-slice_fusion), channel_id=1, source_target_pairs={{0,5},{1,4},{6,3},{7,2},{8,13},{9,12},{14,11},{15,10},{16,21},{17,... | collective-permute-start | bytes 1769480 | tf_op jit(solution)/shard_map/ppermute | solution.py:697
  8.4 0.0 copy-done.13
  8.4 0.7 pad_add_fusion.1.scalars_ref
  9.1 10.3 %shard_map.118.entered_ref = bf16[6,180,768]{2,1,0:T(8,128)(2,1)} custom-call(s32[2]{0:T(128)} %pad_add_fusion.1.scalars_ref, bf16[6,180,768]{2,1,0:T(8,128)(2,1)} %bitcast.22, bf16[768,1280]{1,0:T(8,128)(2,1)} %readout_hbm.1, bf16[1280,768]{1,0:T(8,128)(2,1)} %lifting_hbm.1, bf16[6,180,768]{2,1,0:T(8,128)(2,1)} %pos_hbm.1, bf16[100,768]{1,0:T(8,128)(2,1)} %table_hbm.1), custom_call_target="tpu_custom_call" | custom-call | flops 1800000000 | tf_op jit(solution)/shard_map/pallas_call | solution.py:738
  19.4 0.0 copy-start.11
  19.4 0.0 copy-start.12
  19.4 0.0 collective-permute-done.first_ref
  19.4 0.0 copy-start.1
  19.4 0.0 collective-permute-done.1.second_ref
  19.5 0.0 copy-start.3
  19.5 0.0 collective-permute-done.2.third_ref
  19.5 0.8 copy-done.1
  20.2 0.2 copy-done.3
  20.5 0.8 copy-done.9
  21.3 2.5 %collective-permute-start.3 = (bf16[6,180,768]{2,1,0:T(8,128)(2,1)}, bf16[6,180,768]{2,1,0:T(8,128)(2,1)}, u32[]{:S(2)}, u32[]{:S(2)}) collective-permute-start(bf16[6,180,768]{2,1,0:T(8,128)(2,1)} %shard_map.118.entered_ref), channel_id=1, source_target_pairs={{0,4},{1,5},{6,2},{7,3},{8,12},{9,13},{14,10},{15,11},{16,20},{17,... | collective-permute-start | bytes 4976648 | tf_op jit(solution)/shard_map/ppermute | solution.py:697
  23.8 0.8 collective-permute-start.5
  24.6 3.3 %collective-permute-start.7 = (f32[2,2,8,96,96]{4,3,2,1,0:T(8,128)}, f32[2,2,8,96,96]{4,3,2,1,0:T(8,128)}, u32[]{:S(2)}, u32[]{:S(2)}) collective-permute-start(f32[2,2,8,96,96]{4,3,2,1,0:T(8,128)} %bitcast.17), channel_id=1, source_target_pairs={{0,4},{1,5},{6,2},{7,3},{8,12},{9,13},{14,10},{15,11},{16,20},{17,... | collective-permute-start | bytes 3538952 | tf_op jit(solution)/shard_map/ppermute | solution.py:697
  27.8 2.0 %broadcast_select_fusion = bf16[192,1536]{1,0:T(8,128)(2,1)} fusion(bf16[192,1536]{1,0:T(8,128)(2,1)} %copy-done.3, bf16[192,1536]{1,0:T(8,128)(2,1)} %copy-done.1, pred[]{:T(512)S(6)} %eq.9), kind=kLoop, calls=%fused_computation.3 | loop fusion | flops 294912 | bytes 1769473 | tf_op jit(solution)/shard_map/jit(_where)/select_n | solution.py:767
  29.8 0.4 collective-permute-start.6
  30.2 0.0 copy-done.11
  30.2 0.0 copy-done.12
  30.2 1.3 %collective-permute-start.4 = (f32[4,768]{1,0:T(4,128)S(1)}, f32[4,768]{1,0:T(4,128)S(1)}, u32[]{:S(2)}, u32[]{:S(2)}) collective-permute-start(f32[4,768]{1,0:T(4,128)S(1)} %pad_maximum_fusion.norms_ref), channel_id=1, source_target_pairs={{0,4},{1,5},{6,2},{7,3},{8,12},{9,13},{14,10},{15,11},{16,20},{17,... | collective-permute-start | bytes 36872 | tf_op jit(solution)/shard_map/ppermute | solution.py:697
  31.5 0.1 pad_add_fusion.scalars_ref
  31.6 0.7 collective-permute-done.4.taken_norms_ref
  32.3 0.0 collective-permute-done.3.near_state_ref
  32.3 1.0 copy-done.6
  33.3 4.6 %shard_map.119 = (f32[6,176,512]{2,1,0:T(8,128)S(1)}, f32[6,180,768]{2,1,0:T(8,128)S(1)}) custom-call(s32[3]{0:T(128)S(1)} %pad_add_fusion.scalars_ref, bf16[6,180,768]{2,1,0:T(8,128)(2,1)} %shard_map.118.entered_ref, bf16[6,180,768]{2,1,0:T(8,128)(2,1)} %collective-permute-done.3.near_state_ref, f32[4,768]{1,0:T(4,128)S(1)} %pad_maximum_fusion.norms_ref, ...), custom_call_target="tpu_custom_call" | custom-call | flops 1000000000 | tf_op jit(solution)/shard_map/pallas_call | solution.py:776
  37.9 5.7 %collective-permute-done.6.relayed_ref = bf16[192,1536]{1,0:T(8,128)(2,1)} collective-permute-done((bf16[192,1536]{1,0:T(8,128)(2,1)}, bf16[192,1536]{1,0:T(8,128)(2,1)}, u32[]{:S(2)}, u32[]{:S(2)}) %collective-permute-start.6) | collective-permute-done | bytes 589856 | tf_op jit(solution)/shard_map/ppermute | solution.py:697
  43.6 0.0 collective-permute-done.7.taken_filters_hbm
  43.6 0.0 collective-permute-done.5.moved_ref
  43.6 1.3 %collective-permute-start.8 = (bf16[6,180,768]{2,1,0:T(8,128)(2,1)S(1)}, bf16[6,180,768]{2,1,0:T(8,128)(2,1)S(1)}, u32[]{:S(2)}, u32[]{:S(2)}) collective-permute-start(bf16[6,180,768]{2,1,0:T(8,128)(2,1)S(1)} %collective-permute-done.5.moved_ref), channel_id=1, source_target_pairs={{2,6},{3,7},{4,0},{5,1},{10,14},{11,15},{12,8},{13,9},{18,22},{19,... | collective-permute-start | bytes 4976648 | tf_op jit(solution)/shard_map/ppermute | solution.py:697
  44.9 0.0 copy-done.8
  44.9 0.4 collective-permute-start.9
  45.3 3.8 %collective-permute-done.8.far_state_ref = bf16[6,180,768]{2,1,0:T(8,128)(2,1)S(1)} collective-permute-done((bf16[6,180,768]{2,1,0:T(8,128)(2,1)S(1)}, bf16[6,180,768]{2,1,0:T(8,128)(2,1)S(1)}, u32[]{:S(2)}, u32[]{:S(2)}) %collective-permute-start.8) | collective-permute-done | bytes 1658912 | tf_op jit(solution)/shard_map/ppermute | solution.py:697
  49.1 0.0 copy-done.5
  49.1 8.8 %shard_map.120.mine_ref = bf16[12,180,384]{2,1,0:T(8,128)(2,1)S(1)} custom-call(s32[3]{0:T(128)S(1)} %pad_add_fusion.scalars_ref, bf16[6,180,768]{2,1,0:T(8,128)(2,1)S(1)} %collective-permute-done.5.moved_ref, bf16[6,180,768]{2,1,0:T(8,128)(2,1)S(1)} %collective-permute-done.8.far_state_ref, f32[4,768]{1,0:T(4,128)S(1)} %pad_maximum_fusion.norms_ref, ...), custom_call_target="tpu_custom_call" | custom-call | flops 2200000000 | tf_op jit(solution)/shard_map/pallas_call | solution.py:790
  57.9 3.3 %collective-permute-done.9.down_first_ref.first_ref = bf16[768,768]{1,0:T(8,128)(2,1)S(1)} collective-permute-done((bf16[768,768]{1,0:T(8,128)(2,1)S(1)}, bf16[768,768]{1,0:T(8,128)(2,1)S(1)}, u32[]{:S(2)}, u32[]{:S(2)}) %collective-permute-start.9) | collective-permute-done | bytes 1179680 | tf_op jit(solution)/shard_map/ppermute | solution.py:697
  61.2 0.7 collective-permute-start.10
  61.8 0.7 collective-permute-start.11
  62.6 2.0 %shard_map.121.far_base_ref = f32[6,180,768]{2,1,0:T(8,128)S(1)} custom-call(s32[3]{0:T(128)S(1)} %pad_add_fusion.scalars_ref, bf16[6,180,768]{2,1,0:T(8,128)(2,1)S(1)} %collective-permute-done.5.moved_ref, bf16[6,180,768]{2,1,0:T(8,128)(2,1)S(1)} %collective-permute-done.8.far_state_ref, f32[4,768]{1,0:T(4,128)S(1)} %pad_maximum_fusion.norms_ref, ...), custom_call_target="tpu_custom_call" | custom-call | flops 600000000 | tf_op jit(solution)/shard_map/pallas_call | solution.py:823
  64.6 0.4 collective-permute-done.10.theirs_ref
  65.1 12.5 %shard_map.122 = (f32[12,180,768]{2,1,0:T(8,128)S(1)}, bf16[2304,768]{1,0:T(8,128)(2,1)S(1)}) custom-call(s32[3]{0:T(128)S(1)} %pad_add_fusion.scalars_ref, f32[6,180,768]{2,1,0:T(8,128)S(1)} %get-tuple-element.32.near_base_ref, f32[6,180,768]{2,1,0:T(8,128)S(1)} %shard_map.121.far_base_ref, bf16[12,180,384]{2,1,0:T(8,128)(2,1)S(1)} %shard_map.120.mine_ref, ...), custom_call_target="tpu_custom_call" | custom-call | flops 2200000000 | tf_op jit(solution)/shard_map/pallas_call | solution.py:834
  77.6 0.0 collective-permute-done.11.second_ref
  77.6 2.4 %shard_map.123 = (f32[3,180,768]{2,1,0:T(8,128)S(1)}, bf16[3,180,768]{2,1,0:T(8,128)(2,1)S(1)}) custom-call(s32[3]{0:T(128)S(1)} %pad_add_fusion.scalars_ref, f32[12,180,768]{2,1,0:T(8,128)S(1)} %get-tuple-element.46.partial_ref, bf16[2304,768]{1,0:T(8,128)(2,1)S(1)} %get-tuple-element.47.hidden_ref, ...), custom_call_target="tpu_custom_call" | custom-call | flops 10000000000 | tf_op jit(solution)/shard_map/pallas_call | solution.py:869
  80.0 2.7 %collective-permute-start.12 = (bf16[3,180,768]{2,1,0:T(8,128)(2,1)S(1)}, bf16[3,180,768]{2,1,0:T(8,128)(2,1)S(1)}, u32[]{:S(2)}, u32[]{:S(2)}) collective-permute-start(bf16[3,180,768]{2,1,0:T(8,128)(2,1)S(1)} %get-tuple-element.50), channel_id=1, source_target_pairs={{0,4},{1,5},{2,6},{3,7},{4,0},{5,1},{6,2},{7,3},{8,12},{9,13},{10,... | collective-permute-start | bytes 2488328 | tf_op jit(solution)/shard_map/ppermute | solution.py:697
  82.7 2.3 %shard_map.124 = (f32[3,180,768]{2,1,0:T(8,128)S(1)}, bf16[3,180,768]{2,1,0:T(8,128)(2,1)S(1)}) custom-call(s32[3]{0:T(128)S(1)} %pad_add_fusion.scalars_ref, f32[12,180,768]{2,1,0:T(8,128)S(1)} %get-tuple-element.46.partial_ref, bf16[2304,768]{1,0:T(8,128)(2,1)S(1)} %get-tuple-element.47.hidden_ref, ...), custom_call_target="tpu_custom_call" | custom-call | flops 10000000000 | tf_op jit(solution)/shard_map/pallas_call | solution.py:869
  85.0 0.1 collective-permute-start.15
  85.1 0.0 collective-permute-done.12
  85.1 1.1 add_convert_fusion.1
  86.2 0.5 collective-permute-start.13
  86.7 0.7 collective-permute-done.15
  87.5 1.1 add_convert_fusion
  88.6 0.3 collective-permute-start.16
  88.8 14.3 %collective-permute-done.13.refs_0_ = bf16[3,180,768]{2,1,0:T(8,128)(2,1)S(1)} collective-permute-done((bf16[3,180,768]{2,1,0:T(8,128)(2,1)}, bf16[3,180,768]{2,1,0:T(8,128)(2,1)S(1)}, u32[]{:S(2)}, u32[]{:S(2)}) %collective-permute-start.13) | collective-permute-done | bytes 829472 | tf_op jit(solution)/shard_map/ppermute | solution.py:697
  103.1 4.8 %collective-permute-start.14 = (bf16[3,180,768]{2,1,0:T(8,128)(2,1)S(1)}, bf16[3,180,768]{2,1,0:T(8,128)(2,1)S(1)}, u32[]{:S(2)}, u32[]{:S(2)}) collective-permute-start(bf16[3,180,768]{2,1,0:T(8,128)(2,1)S(1)} %collective-permute-done.13.refs_0_), channel_id=1, source_target_pairs={{0,8},{1,9},{8,16},{9,17},{16,24},{17,25},{24,0},{25,1}} | collective-permute-start | bytes 2488328 | tf_op jit(solution)/shard_map/ppermute | solution.py:697
  107.9 5.4 %collective-permute-done.16.chunk_ref = bf16[3,180,768]{2,1,0:T(8,128)(2,1)S(1)} collective-permute-done((bf16[3,180,768]{2,1,0:T(8,128)(2,1)}, bf16[3,180,768]{2,1,0:T(8,128)(2,1)S(1)}, u32[]{:S(2)}, u32[]{:S(2)}) %collective-permute-start.16) | collective-permute-done | bytes 829472 | tf_op jit(solution)/shard_map/ppermute | solution.py:697
  113.3 0.9 shard_map.125.refs_2_
  114.2 6.3 %collective-permute-done.14.refs_1_ = bf16[3,180,768]{2,1,0:T(8,128)(2,1)S(1)} collective-permute-done((bf16[3,180,768]{2,1,0:T(8,128)(2,1)S(1)}, bf16[3,180,768]{2,1,0:T(8,128)(2,1)S(1)}, u32[]{:S(2)}, u32[]{:S(2)}) %collective-permute-start.14) | collective-permute-done | bytes 829472 | tf_op jit(solution)/shard_map/ppermute | solution.py:697
  120.5 0.9 shard_map.126
  (15 shorter events, 0.1 us)
Async XLA Ops:
  0.0 1.3 %copy-start = (bf16[1,192,3072]{2,1,0:T(8,128)(2,1)S(1)}, bf16[1,192,3072]{2,1,0:T(8,128)(2,1)}, u32[]{:S(2)}) copy-start(bf16[1,192,3072]{2,1,0:T(8,128)(2,1)} %param.21) | copy-start | bytes 3538948
  0.0 8.4 %copy-start.13 = (s32[1,8,1]{1,2,0:T(1,128)S(1)}, s32[1,8,1]{1,2,0:T(1,128)}, u32[]{:S(2)}) copy-start(s32[1,8,1]{1,2,0:T(1,128)} %param.13) | copy-start | bytes 100
  1.3 18.1 %collective-permute-start = (bf16[192,1536]{1,0:T(8,128)(2,1)S(1)}, bf16[192,1536]{1,0:T(8,128)(2,1)S(1)}, u32[]{:S(2)}, u32[]{:S(2)}) collective-permute-start(bf16[192,1536]{1,0:T(8,128)(2,1)S(1)} %dynamic-slice_bitcast_fusion.held_ref), channel_id=1, source_target_pairs={{0,1},{1,0},{2,4},{3,5},{4,2},{5,3},{6,7},{7,6},{8,9},{9,8},{10,12... | collective-permute-start | bytes 1769480 | tf_op jit(solution)/shard_map/ppermute | solution.py:697
  5.2 14.2 %collective-permute-start.1 = (bf16[192,1536]{1,0:T(8,128)(2,1)}, bf16[192,1536]{1,0:T(8,128)(2,1)S(1)}, u32[]{:S(2)}, u32[]{:S(2)}) collective-permute-start(bf16[192,1536]{1,0:T(8,128)(2,1)} %constant_dynamic-slice_fusion), channel_id=1, source_target_pairs={{0,4},{1,5},{2,0},{3,1},{4,6},{5,7},{6,2},{7,3},{8,12},{9,13},{10,... | collective-permute-start | bytes 1769480 | tf_op jit(solution)/shard_map/ppermute | solution.py:697
  5.3 14.2 %collective-permute-start.2 = (bf16[192,1536]{1,0:T(8,128)(2,1)}, bf16[192,1536]{1,0:T(8,128)(2,1)S(1)}, u32[]{:S(2)}, u32[]{:S(2)}) collective-permute-start(bf16[192,1536]{1,0:T(8,128)(2,1)} %constant_dynamic-slice_fusion), channel_id=1, source_target_pairs={{0,5},{1,4},{6,3},{7,2},{8,13},{9,12},{14,11},{15,10},{16,21},{17,... | collective-permute-start | bytes 1769480 | tf_op jit(solution)/shard_map/ppermute | solution.py:697
  19.4 10.8 %copy-start.11 = (f32[1,2,768]{2,1,0:T(2,128)S(1)}, f32[1,2,768]{2,1,0:T(2,128)}, u32[]{:S(2)}) copy-start(f32[1,2,768]{2,1,0:T(2,128)} %param.19) | copy-start | bytes 18436
  19.4 10.8 %copy-start.12 = (f32[1,2,768]{2,1,0:T(2,128)S(1)}, f32[1,2,768]{2,1,0:T(2,128)}, u32[]{:S(2)}) copy-start(f32[1,2,768]{2,1,0:T(2,128)} %param.18) | copy-start | bytes 18436
  19.4 0.8 copy-start.1
  19.5 1.0 copy-start.3
  20.5 0.8 copy-start.9
  21.3 11.0 %collective-permute-start.3 = (bf16[6,180,768]{2,1,0:T(8,128)(2,1)}, bf16[6,180,768]{2,1,0:T(8,128)(2,1)}, u32[]{:S(2)}, u32[]{:S(2)}) collective-permute-start(bf16[6,180,768]{2,1,0:T(8,128)(2,1)} %shard_map.118.entered_ref), channel_id=1, source_target_pairs={{0,4},{1,5},{6,2},{7,3},{8,12},{9,13},{14,10},{15,11},{16,20},{17,... | collective-permute-start | bytes 4976648 | tf_op jit(solution)/shard_map/ppermute | solution.py:697
  23.8 19.8 %collective-permute-start.5 = (bf16[6,180,768]{2,1,0:T(8,128)(2,1)}, bf16[6,180,768]{2,1,0:T(8,128)(2,1)S(1)}, u32[]{:S(2)}, u32[]{:S(2)}) collective-permute-start(bf16[6,180,768]{2,1,0:T(8,128)(2,1)} %shard_map.118.entered_ref), channel_id=1, source_target_pairs={{2,4},{3,5},{4,2},{5,3},{10,12},{11,13},{12,10},{13,11},{18,20},{1... | collective-permute-start | bytes 4976648 | tf_op jit(solution)/shard_map/ppermute | solution.py:697
  24.6 19.1 %collective-permute-start.7 = (f32[2,2,8,96,96]{4,3,2,1,0:T(8,128)}, f32[2,2,8,96,96]{4,3,2,1,0:T(8,128)}, u32[]{:S(2)}, u32[]{:S(2)}) collective-permute-start(f32[2,2,8,96,96]{4,3,2,1,0:T(8,128)} %bitcast.17), channel_id=1, source_target_pairs={{0,4},{1,5},{6,2},{7,3},{8,12},{9,13},{14,10},{15,11},{16,20},{17,... | collective-permute-start | bytes 3538952 | tf_op jit(solution)/shard_map/ppermute | solution.py:697
  29.8 13.8 %collective-permute-start.6 = (bf16[192,1536]{1,0:T(8,128)(2,1)}, bf16[192,1536]{1,0:T(8,128)(2,1)}, u32[]{:S(2)}, u32[]{:S(2)}) collective-permute-start(bf16[192,1536]{1,0:T(8,128)(2,1)} %broadcast_select_fusion), channel_id=1, source_target_pairs={{0,1},{1,0},{2,3},{3,2},{4,5},{5,4},{6,7},{7,6},{8,9},{9,8},{10,11... | collective-permute-start | bytes 1769480 | tf_op jit(solution)/shard_map/ppermute | solution.py:697
  30.2 2.1 %collective-permute-start.4 = (f32[4,768]{1,0:T(4,128)S(1)}, f32[4,768]{1,0:T(4,128)S(1)}, u32[]{:S(2)}, u32[]{:S(2)}) collective-permute-start(f32[4,768]{1,0:T(4,128)S(1)} %pad_maximum_fusion.norms_ref), channel_id=1, source_target_pairs={{0,4},{1,5},{6,2},{7,3},{8,12},{9,13},{14,10},{15,11},{16,20},{17,... | collective-permute-start | bytes 36872 | tf_op jit(solution)/shard_map/ppermute | solution.py:697
  31.6 17.5 %copy-start.5 = (f32[1,2,2,8,96,96]{5,4,3,2,1,0:T(8,128)S(1)}, f32[1,2,2,8,96,96]{5,4,3,2,1,0:T(8,128)}, u32[]{:S(2)}) copy-start(f32[1,2,2,8,96,96]{5,4,3,2,1,0:T(8,128)} %param.20) | copy-start | bytes 3538948
  32.3 1.0 copy-start.6
  33.3 11.6 %copy-start.8 = (bf16[1,768,768]{2,1,0:T(8,128)(2,1)S(1)}, bf16[1,768,768]{2,1,0:T(8,128)(2,1)}, u32[]{:S(2)}) copy-start(bf16[1,768,768]{2,1,0:T(8,128)(2,1)} %param.22) | copy-start | bytes 3538948
  33.3 15.8 %copy-start.7 = (bf16[2,2,180,180]{3,2,1,0:T(8,128)(2,1)S(1)}, bf16[2,2,180,180]{3,2,1,0:T(8,128)(2,1)}, u32[]{:S(2)}) copy-start(bf16[2,2,180,180]{3,2,1,0:T(8,128)(2,1)} %constant.34.clone.tables_ref) | copy-start | bytes 777604
  43.6 5.5 %collective-permute-start.8 = (bf16[6,180,768]{2,1,0:T(8,128)(2,1)S(1)}, bf16[6,180,768]{2,1,0:T(8,128)(2,1)S(1)}, u32[]{:S(2)}, u32[]{:S(2)}) collective-permute-start(bf16[6,180,768]{2,1,0:T(8,128)(2,1)S(1)} %collective-permute-done.5.moved_ref), channel_id=1, source_target_pairs={{2,6},{3,7},{4,0},{5,1},{10,14},{11,15},{12,8},{13,9},{18,22},{19,... | collective-permute-start | bytes 4976648 | tf_op jit(solution)/shard_map/ppermute | solution.py:697
  44.9 16.3 %collective-permute-start.9 = (bf16[768,768]{1,0:T(8,128)(2,1)S(1)}, bf16[768,768]{1,0:T(8,128)(2,1)S(1)}, u32[]{:S(2)}, u32[]{:S(2)}) collective-permute-start(bf16[768,768]{1,0:T(8,128)(2,1)S(1)} %bitcast.19), channel_id=1, source_target_pairs={{0,1},{1,0},{2,4},{3,5},{4,2},{5,3},{6,7},{7,6},{8,9},{9,8},{10,12... | collective-permute-start | bytes 3538952 | tf_op jit(solution)/shard_map/ppermute | solution.py:697
  57.8 7.2 %copy-start.2 = (bf16[192,1536]{1,0:T(8,128)(2,1)S(1)}, bf16[192,1536]{1,0:T(8,128)(2,1)}, u32[]{:S(2)}) copy-start(bf16[192,1536]{1,0:T(8,128)(2,1)} %copy-done.1) | copy-start | bytes 1769476
  57.9 7.2 %copy-start.4 = (bf16[192,1536]{1,0:T(8,128)(2,1)S(1)}, bf16[192,1536]{1,0:T(8,128)(2,1)}, u32[]{:S(2)}) copy-start(bf16[192,1536]{1,0:T(8,128)(2,1)} %copy-done.3) | copy-start | bytes 1769476
  57.9 7.2 %copy-start.10 = (bf16[192,1536]{1,0:T(8,128)(2,1)S(1)}, bf16[192,1536]{1,0:T(8,128)(2,1)}, u32[]{:S(2)}) copy-start(bf16[192,1536]{1,0:T(8,128)(2,1)} %copy-done.9) | copy-start | bytes 1769476
  61.2 3.9 %collective-permute-start.10 = (bf16[12,180,384]{2,1,0:T(8,128)(2,1)S(1)}, bf16[12,180,384]{2,1,0:T(8,128)(2,1)S(1)}, u32[]{:S(2)}, u32[]{:S(2)}) collective-permute-start(bf16[12,180,384]{2,1,0:T(8,128)(2,1)S(1)} %shard_map.120.mine_ref), channel_id=1, source_target_pairs={{0,4},{1,5},{2,6},{3,7},{4,0},{5,1},{6,2},{7,3},{8,12},{9,13},{10,... | collective-permute-start | bytes 4976648 | tf_op jit(solution)/shard_map/ppermute | solution.py:697
  61.8 15.8 %collective-permute-start.11 = (bf16[768,768]{1,0:T(8,128)(2,1)S(1)}, bf16[768,768]{1,0:T(8,128)(2,1)S(1)}, u32[]{:S(2)}, u32[]{:S(2)}) collective-permute-start(bf16[768,768]{1,0:T(8,128)(2,1)S(1)} %bitcast.20), channel_id=1, source_target_pairs={{2,5},{3,4},{4,3},{5,2},{10,13},{11,12},{12,11},{13,10},{18,21},{1... | collective-permute-start | bytes 3538952 | tf_op jit(solution)/shard_map/ppermute | solution.py:697
  80.0 5.1 %collective-permute-start.12 = (bf16[3,180,768]{2,1,0:T(8,128)(2,1)S(1)}, bf16[3,180,768]{2,1,0:T(8,128)(2,1)S(1)}, u32[]{:S(2)}, u32[]{:S(2)}) collective-permute-start(bf16[3,180,768]{2,1,0:T(8,128)(2,1)S(1)} %get-tuple-element.50), channel_id=1, source_target_pairs={{0,4},{1,5},{2,6},{3,7},{4,0},{5,1},{6,2},{7,3},{8,12},{9,13},{10,... | collective-permute-start | bytes 2488328 | tf_op jit(solution)/shard_map/ppermute | solution.py:697
  85.0 2.4 %collective-permute-start.15 = (bf16[3,180,768]{2,1,0:T(8,128)(2,1)S(1)}, bf16[3,180,768]{2,1,0:T(8,128)(2,1)S(1)}, u32[]{:S(2)}, u32[]{:S(2)}) collective-permute-start(bf16[3,180,768]{2,1,0:T(8,128)(2,1)S(1)} %get-tuple-element.52), channel_id=1, source_target_pairs={{0,4},{1,5},{2,6},{3,7},{4,0},{5,1},{6,2},{7,3},{8,12},{9,13},{10,... | collective-permute-start | bytes 2488328 | tf_op jit(solution)/shard_map/ppermute | solution.py:697
  86.2 16.8 %collective-permute-start.13 = (bf16[3,180,768]{2,1,0:T(8,128)(2,1)}, bf16[3,180,768]{2,1,0:T(8,128)(2,1)S(1)}, u32[]{:S(2)}, u32[]{:S(2)}) collective-permute-start(bf16[3,180,768]{2,1,0:T(8,128)(2,1)} %add_convert_fusion.1), channel_id=1, source_target_pairs={{0,4},{1,5},{2,0},{3,1},{4,6},{5,7},{6,10},{7,11},{8,12},{9,13},{1... | collective-permute-start | bytes 2488328 | tf_op jit(solution)/shard_map/ppermute | solution.py:697
  88.6 24.7 %collective-permute-start.16 = (bf16[3,180,768]{2,1,0:T(8,128)(2,1)}, bf16[3,180,768]{2,1,0:T(8,128)(2,1)S(1)}, u32[]{:S(2)}, u32[]{:S(2)}) collective-permute-start(bf16[3,180,768]{2,1,0:T(8,128)(2,1)} %add_convert_fusion), channel_id=1, source_target_pairs={{0,4},{1,5},{2,8},{3,9},{4,6},{5,7},{6,10},{7,11},{8,12},{9,13},{1... | collective-permute-start | bytes 2488328 | tf_op jit(solution)/shard_map/ppermute | solution.py:697
  103.1 17.4 %collective-permute-start.14 = (bf16[3,180,768]{2,1,0:T(8,128)(2,1)S(1)}, bf16[3,180,768]{2,1,0:T(8,128)(2,1)S(1)}, u32[]{:S(2)}, u32[]{:S(2)}) collective-permute-start(bf16[3,180,768]{2,1,0:T(8,128)(2,1)S(1)} %collective-permute-done.13.refs_0_), channel_id=1, source_target_pairs={{0,8},{1,9},{8,16},{9,17},{16,24},{17,25},{24,0},{25,1}} | collective-permute-start | bytes 2488328 | tf_op jit(solution)/shard_map/ppermute | solution.py:697

commit v4 on v3

--- a/solution.py
+++ b/solution.py
@@ -378,19 +378,6 @@
         grid_ref[row] = row_spectra(half == 0, centred, factor, norms, forward)
 
 
-def base_kernel(
-    scalars_ref, moved_ref, far_state_ref, norms_ref, taken_norms_ref, base_ref, state_ref, sem
-):
-    near = scalars_ref[0] == scalars_ref[1]
-    load = load_one(near, far_state_ref, moved_ref, state_ref, sem)
-    norms = jnp.where(near, norms_ref[...], taken_norms_ref[...])
-    load.wait()
-    for row in range(state_ref.shape[0]):
-        carried = state_ref[row].astype(jnp.float32)
-        centred, factor = centre(carried)
-        base_ref[row] = carried + (centred * factor * norms[0:1] + norms[2:3])
-
-
 def filter_kernel(
     scalars_ref,
     moved_ref,
@@ -402,6 +389,7 @@
     filters_hbm,
     taken_filters_hbm,
     out_ref,
+    base_ref,
     grid_ref,
     modes_ref,
     filters_ref,
@@ -427,7 +415,9 @@
     backward = [tables_ref[part, 1, :width, : 2 * kept] for part in range(2)]
     load.wait()
     for row in range(rows):
-        centred, factor = centre(state_ref[row].astype(jnp.float32))
+        carried = state_ref[row].astype(jnp.float32)
+        centred, factor = centre(carried)
+        base_ref[row] = carried + (centred * factor * norms[0:1] + norms[2:3])
         grid_ref[rows + row] = row_spectra(half == 0, centred, factor, norms, forward)
     mixing_ref[...] = jnp.zeros_like(mixing_ref)
     own_load.wait()
@@ -710,9 +700,7 @@
     )
     across = table(lambda g, s, e: (g, s, 1 - e))
     third_way = table(lambda g, s, e: (g ^ 1, s, 1 - e) if keeps(g, s) else None)
-    far_to_other = table(lambda g, s, e: (g ^ 1, s, e) if not keeps(g, s) else None)
     swap_cores = table(lambda g, s, e: (g ^ 1, s, e))
-    near_to_other = table(lambda g, s, e: (g ^ 1, s, e) if keeps(g, s) else None)
     onward = table(lambda g, s, e: ((g // 2 * 2 + s + 1) % segments, g % 2, e))
     onward_by_space = table(
         lambda g, s, e: (g, 0, e)
@@ -763,12 +751,12 @@
         (entered, up_first, up_second, up_third)
     )
     moved = send(entered, far_relocate)
-    near_state = send(entered, near_to_other)
+    near_state = send(entered, swap_cores)
     up_relayed = send(jnp.where(near, up_second, up_first), across)
     norms = jnp.concatenate([norm_gain[0], norm_shift[0]], 0)
-    taken_norms = send(norms, near_to_other)
+    taken_norms = send(norms, swap_cores)
     filters = spectral[0]
-    taken_filters = send(filters, near_to_other)
+    taken_filters = send(filters, swap_cores)
     scalars = jnp.stack([core, space, member]).astype(i32)
     tables = jnp.asarray(split_longitude_tables(width, KW, latitudes))
     half_groups = spectral.shape[3] // 2
@@ -785,13 +773,16 @@
     moved, near_grid, up_relayed, taken_filters, down_later = lax.optimization_barrier(
         (moved, near_grid, up_relayed, taken_filters, down)
     )
-    far_state = send(moved, far_to_other)
+    far_state = send(moved, swap_cores)
     down_first = send(down_later, first_way)
-    filtered = pl.pallas_call(
+    filtered, far_base = pl.pallas_call(
         filter_kernel,
-        out_shape=jax.ShapeDtypeStruct((2 * rows, width, channels // 2), bf16),
+        out_shape=[
+            jax.ShapeDtypeStruct((2 * rows, width, channels // 2), bf16),
+            VMEM(state.shape, f32),
+        ],
         in_specs=[SCALARS] + [LEFT] * 2 + [WHOLE] * 4 + [LEFT] * 2,
-        out_specs=WHOLE,
+        out_specs=[WHOLE] * 2,
         scratch_shapes=[
             VMEM((latitudes, 2 * KW, lanes), f32),
             VMEM((half_groups, latitudes * KW, 2 * GROUP_LANES), f32),
@@ -819,16 +810,6 @@
     )
     down_second = send(down_again, far_diagonal)
     filtered_other = send(filtered, swap_cores)
-    scalars_later, _ = lax.optimization_barrier((scalars, filtered))
-    far_base = pl.pallas_call(
-        base_kernel,
-        out_shape=VMEM(state.shape, f32),
-        in_specs=[SCALARS] + [LEFT] * 2 + [WHOLE] * 2,
-        out_specs=WHOLE,
-        scratch_shapes=[VMEM(state.shape, bf16), pltpu.SemaphoreType.DMA],
-        cost_estimate=cost(3),
-        compiler_params=params(12),
-    )(scalars_later, moved, far_state, norms, taken_norms)
 
     parts = 2
     partial, hidden = pl.pallas_call(
@@ -879,7 +860,7 @@
                 pltpu.SemaphoreType.DMA,
             ],
             cost_estimate=cost(50),
-            compiler_params=params(24),
+            compiler_params=params(12),
         )(scalars, partial, hidden, down_first, down_second)
         ready.append((own + send(other, swap_cores).astype(f32)).astype(bf16))
         if number + 1 < parts:

time: 122 us -> 120 us (0.984)
  waiting for transfers between devices: 40.7 us -> 45 us
  Pallas kernels: 44.8 us -> 40.7 us
  local copies, waits for them, and re-layouts: 5 us -> 3.17 us
    ppermute x17, waiting for transfers between devices: 40.7 us -> 45 us  [send(): return lax.ppermute(value, MESH_AXES, pairs)]
    unnamed x28 -> x14, local copies, waits for them, and re-layouts: 4.11 us -> 2.28 us
    pallas_call x2 -> x1, Pallas kernels: 10.8 us -> 9.01 us  [fast_on_device(): pl.pallas_call(filter_kernel, out_shape=[jax.ShapeDtypeStruct((2 * rows,...]
  transfers between devices with their start and end apart: 17 -> 17, of which waited for: 9 -> 9; matrix products, arithmetic and copies ran while one was open for 5% -> 5% of each run, Pallas kernels for 34% -> 31%
where the time goes in v4:
time: 120 us; the launch traced here: 119 us
  waiting for transfers between devices  45 us (38%)
  Pallas kernels  40.7 us (34%)
  starting transfers between devices  25.1 us (21%)
  other arithmetic  4.94 us (4%)
  local copies, waits for them, and re-layouts  3.17 us (3%)
    ppermute x17, waiting for transfers between devices, send(): return lax.ppermute(value, MESH_AXES, pairs)  45 us
    ppermute x17, starting transfers between devices, send(): return lax.ppermute(value, MESH_AXES, pairs)  25.1 us
    pallas_call x1, Pallas kernels, fast_on_device(): pl.pallas_call(functools.partial(hidden_kernel, rows // parts), out_shape...  12.4 us
    pallas_call x1, Pallas kernels, fast_on_device(): pl.pallas_call(enter_kernel, out_shape=VMEM(state.shape, bf16), in_specs=...  9.14 us
    pallas_call x1, Pallas kernels, fast_on_device(): pl.pallas_call(filter_kernel, out_shape=[jax.ShapeDtypeStruct((2 * rows,...  9.01 us
    pallas_call x2, Pallas kernels, fast_on_device(): pl.pallas_call(functools.partial(update_kernel, number), out_shape=[jax.S...  4.8 us
    pallas_call x1, Pallas kernels, fast_on_device(): pl.pallas_call(near_kernel, out_shape=[VMEM((rows, 2 * KW, lanes), f32),...  3.45 us
  transfers between devices with their start and end apart: 17, of which 9 were waited for; matrix products, arithmetic and copies ran while one was open for 5% of the time, Pallas kernels for 31%

profile of v4, /device:TPU:0, one launch (start us, length us, event | category | flops | bytes accessed | tf_op | source)
XLA Modules:
  0.0 119.2 jit_solution(3191860919025613820)
XLA Ops:
  0.0 0.0 copy-start
  0.0 0.0 copy-start.6
  0.0 1.3 %copy-done = bf16[1,192,3072]{2,1,0:T(8,128)(2,1)S(1)} copy-done((bf16[1,192,3072]{2,1,0:T(8,128)(2,1)S(1)}, bf16[1,192,3072]{2,1,0:T(8,128)(2,1)}, u32[]{:S(2)}) %copy-start) | copy-done | bytes 1179672
  1.3 3.0 %collective-permute-start = (bf16[192,1536]{1,0:T(8,128)(2,1)S(1)}, bf16[192,1536]{1,0:T(8,128)(2,1)}, u32[]{:S(2)}, u32[]{:S(2)}) collective-permute-start(bf16[192,1536]{1,0:T(8,128)(2,1)S(1)} %dynamic-slice_bitcast_fusion.held_ref), channel_id=1, source_target_pairs={{0,1},{1,0},{2,4},{3,5},{4,2},{5,3},{6,7},{7,6},{8,9},{9,8},{10,12... | collective-permute-start | bytes 1769480 | tf_op jit(solution)/shard_map/ppermute | solution.py:687
  4.3 0.9 constant_dynamic-slice_fusion
  5.2 0.1 collective-permute-start.1
  5.3 3.9 %collective-permute-start.2 = (bf16[192,1536]{1,0:T(8,128)(2,1)}, bf16[192,1536]{1,0:T(8,128)(2,1)}, u32[]{:S(2)}, u32[]{:S(2)}) collective-permute-start(bf16[192,1536]{1,0:T(8,128)(2,1)} %constant_dynamic-slice_fusion), channel_id=1, source_target_pairs={{0,5},{1,4},{6,3},{7,2},{8,13},{9,12},{14,11},{15,10},{16,21},{17,... | collective-permute-start | bytes 1769480 | tf_op jit(solution)/shard_map/ppermute | solution.py:687
  9.1 0.0 copy-done.6
  9.2 0.7 pad_add_fusion.1.scalars_ref
  9.8 9.1 %shard_map.118.entered_ref = bf16[6,180,768]{2,1,0:T(8,128)(2,1)S(1)} custom-call(s32[2]{0:T(128)} %pad_add_fusion.1.scalars_ref, bf16[6,180,768]{2,1,0:T(8,128)(2,1)} %bitcast.20, bf16[768,1280]{1,0:T(8,128)(2,1)} %readout_hbm.1, bf16[1280,768]{1,0:T(8,128)(2,1)} %lifting_hbm.1, bf16[6,180,768]{2,1,0:T(8,128)(2,1)} %pos_hbm.1, bf16[100,768]{1,0:T(8,128)(2,1)} %table_hbm.1), custom_call_target="tpu_custom_call" | custom-call | flops 1800000000 | tf_op jit(solution)/shard_map/pallas_call | solution.py:726
  18.9 0.0 copy-start.4
  19.0 0.0 copy-start.5
  19.0 0.0 collective-permute-done.first_ref
  19.0 0.0 collective-permute-done.1.second_ref
  19.0 0.0 collective-permute-done.2.third_ref
  19.0 0.1 collective-permute-start.3
  19.1 1.9 %collective-permute-start.5 = (bf16[6,180,768]{2,1,0:T(8,128)(2,1)S(1)}, bf16[6,180,768]{2,1,0:T(8,128)(2,1)}, u32[]{:S(2)}, u32[]{:S(2)}) collective-permute-start(bf16[6,180,768]{2,1,0:T(8,128)(2,1)S(1)} %shard_map.118.entered_ref), channel_id=1, source_target_pairs={{2,4},{3,5},{4,2},{5,3},{10,12},{11,13},{12,10},{13,11},{18,20},{1... | collective-permute-start | bytes 4976648 | tf_op jit(solution)/shard_map/ppermute | solution.py:687
  21.0 1.0 collective-permute-start.7
  22.0 1.9 %broadcast_select_fusion = bf16[192,1536]{1,0:T(8,128)(2,1)} fusion(bf16[192,1536]{1,0:T(8,128)(2,1)} %collective-permute-done.1.second_ref, bf16[192,1536]{1,0:T(8,128)(2,1)} %collective-permute-done.first_ref, pred[]{:T(512)S(6)} %eq.9), kind=kLoop, calls=%fused_computation.3 | loop fusion | flops 294912 | bytes 1769473 | tf_op jit(solution)/shard_map/jit(_where)/select_n | solution.py:755
  23.9 1.5 %collective-permute-start.6 = (bf16[192,1536]{1,0:T(8,128)(2,1)}, bf16[192,1536]{1,0:T(8,128)(2,1)}, u32[]{:S(2)}, u32[]{:S(2)}) collective-permute-start(bf16[192,1536]{1,0:T(8,128)(2,1)} %broadcast_select_fusion), channel_id=1, source_target_pairs={{0,1},{1,0},{2,3},{3,2},{4,5},{5,4},{6,7},{7,6},{8,9},{9,8},{10,11... | collective-permute-start | bytes 1769480 | tf_op jit(solution)/shard_map/ppermute | solution.py:687
  25.4 0.0 copy-done.4
  25.4 0.0 copy-done.5
  25.4 0.1 collective-permute-start.4
  25.5 0.1 pad_add_fusion.scalars_ref
  25.6 1.1 collective-permute-done.4.taken_norms_ref
  26.7 0.0 collective-permute-done.3.near_state_ref
  26.7 0.0 copy-start.1
  26.7 1.0 copy-done.1
  27.7 0.0 copy-start.3
  27.7 0.0 copy-start.2
  27.7 3.4 %shard_map.119 = (f32[6,176,512]{2,1,0:T(8,128)S(1)}, f32[6,180,768]{2,1,0:T(8,128)S(1)}) custom-call(s32[3]{0:T(128)S(1)} %pad_add_fusion.scalars_ref, bf16[6,180,768]{2,1,0:T(8,128)(2,1)S(1)} %shard_map.118.entered_ref, bf16[6,180,768]{2,1,0:T(8,128)(2,1)} %collective-permute-done.3.near_state_ref, f32[4,768]{1,0:T(4,128)S(1)} %pad_maximum_fusion.norms_ref, ...), custom_call_target="tpu_custom_call" | custom-call | flops 1000000000 | tf_op jit(solution)/shard_map/pallas_call | solution.py:764
  31.1 8.4 %collective-permute-done.6.relayed_ref = bf16[192,1536]{1,0:T(8,128)(2,1)} collective-permute-done((bf16[192,1536]{1,0:T(8,128)(2,1)}, bf16[192,1536]{1,0:T(8,128)(2,1)}, u32[]{:S(2)}, u32[]{:S(2)}) %collective-permute-start.6) | collective-permute-done | bytes 589856 | tf_op jit(solution)/shard_map/ppermute | solution.py:687
  39.5 0.0 collective-permute-done.7.taken_filters_hbm
  39.5 0.0 collective-permute-done.5.moved_ref
  39.5 3.2 %collective-permute-start.8 = (bf16[6,180,768]{2,1,0:T(8,128)(2,1)}, bf16[6,180,768]{2,1,0:T(8,128)(2,1)S(1)}, u32[]{:S(2)}, u32[]{:S(2)}) collective-permute-start(bf16[6,180,768]{2,1,0:T(8,128)(2,1)} %collective-permute-done.5.moved_ref), channel_id=1, source_target_pairs={{0,4},{1,5},{2,6},{3,7},{4,0},{5,1},{6,2},{7,3},{8,12},{9,13},{10,... | collective-permute-start | bytes 4976648 | tf_op jit(solution)/shard_map/ppermute | solution.py:687
  42.7 0.0 copy-done.3
  42.7 1.2 collective-permute-start.9
  43.9 2.2 %collective-permute-done.8.far_state_ref = bf16[6,180,768]{2,1,0:T(8,128)(2,1)S(1)} collective-permute-done((bf16[6,180,768]{2,1,0:T(8,128)(2,1)}, bf16[6,180,768]{2,1,0:T(8,128)(2,1)S(1)}, u32[]{:S(2)}, u32[]{:S(2)}) %collective-permute-start.8) | collective-permute-done | bytes 1658912 | tf_op jit(solution)/shard_map/ppermute | solution.py:687
  46.2 0.0 copy-done.2
  46.2 9.0 %shard_map.120 = (bf16[12,180,384]{2,1,0:T(8,128)(2,1)S(1)}, f32[6,180,768]{2,1,0:T(8,128)S(1)}) custom-call(s32[3]{0:T(128)S(1)} %pad_add_fusion.scalars_ref, bf16[6,180,768]{2,1,0:T(8,128)(2,1)} %collective-permute-done.5.moved_ref, bf16[6,180,768]{2,1,0:T(8,128)(2,1)S(1)} %collective-permute-done.8.far_state_ref, f32[4,768]{1,0:T(4,128)S(1)} %pad_maximum_fusion.norms_ref, ...), custom_call_target="tpu_custom_call" | custom-call | flops 2200000000 | tf_op jit(solution)/shard_map/pallas_call | solution.py:778
  55.2 3.8 %collective-permute-done.9.down_first_ref.first_ref = bf16[768,768]{1,0:T(8,128)(2,1)S(1)} collective-permute-done((bf16[768,768]{1,0:T(8,128)(2,1)S(1)}, bf16[768,768]{1,0:T(8,128)(2,1)S(1)}, u32[]{:S(2)}, u32[]{:S(2)}) %collective-permute-start.9) | collective-permute-done | bytes 1179680 | tf_op jit(solution)/shard_map/ppermute | solution.py:687
  58.9 0.0 collective-permute-start.10
  58.9 0.7 collective-permute-start.11
  59.7 2.8 %collective-permute-done.10.theirs_ref = bf16[12,180,384]{2,1,0:T(8,128)(2,1)S(1)} collective-permute-done((bf16[12,180,384]{2,1,0:T(8,128)(2,1)S(1)}, bf16[12,180,384]{2,1,0:T(8,128)(2,1)S(1)}, u32[]{:S(2)}, u32[]{:S(2)}) %collective-permute-start.10) | collective-permute-done | bytes 1658912 | tf_op jit(solution)/shard_map/ppermute | solution.py:687
  62.5 12.4 %shard_map.121 = (f32[12,180,768]{2,1,0:T(8,128)S(1)}, bf16[2304,768]{1,0:T(8,128)(2,1)S(1)}) custom-call(s32[3]{0:T(128)S(1)} %pad_add_fusion.scalars_ref, f32[6,180,768]{2,1,0:T(8,128)S(1)} %get-tuple-element.33.near_base_ref, f32[6,180,768]{2,1,0:T(8,128)S(1)} %get-tuple-element.40.far_base_ref, bf16[12,180,384]{2,1,0:T(8,128)(2,1)S(1)} %get-tuple-element.44.mine_ref, ...), custom_call_target="tpu_custom_call" | custom-call | flops 2200000000 | tf_op jit(solution)/shard_map/pallas_call | solution.py:815
  75.0 0.0 collective-permute-done.11.second_ref
  75.0 2.4 %shard_map.122 = (f32[3,180,768]{2,1,0:T(8,128)S(1)}, bf16[3,180,768]{2,1,0:T(8,128)(2,1)S(1)}) custom-call(s32[3]{0:T(128)S(1)} %pad_add_fusion.scalars_ref, f32[12,180,768]{2,1,0:T(8,128)S(1)} %get-tuple-element.48.partial_ref, bf16[2304,768]{1,0:T(8,128)(2,1)S(1)} %get-tuple-element.49.hidden_ref, ...), custom_call_target="tpu_custom_call" | custom-call | flops 10000000000 | tf_op jit(solution)/shard_map/pallas_call | solution.py:850
  77.4 2.9 %collective-permute-start.12 = (bf16[3,180,768]{2,1,0:T(8,128)(2,1)S(1)}, bf16[3,180,768]{2,1,0:T(8,128)(2,1)S(1)}, u32[]{:S(2)}, u32[]{:S(2)}) collective-permute-start(bf16[3,180,768]{2,1,0:T(8,128)(2,1)S(1)} %get-tuple-element.52), channel_id=1, source_target_pairs={{0,4},{1,5},{2,6},{3,7},{4,0},{5,1},{6,2},{7,3},{8,12},{9,13},{10,... | collective-permute-start | bytes 2488328 | tf_op jit(solution)/shard_map/ppermute | solution.py:687
  80.3 2.4 %shard_map.123 = (f32[3,180,768]{2,1,0:T(8,128)S(1)}, bf16[3,180,768]{2,1,0:T(8,128)(2,1)S(1)}) custom-call(s32[3]{0:T(128)S(1)} %pad_add_fusion.scalars_ref, f32[12,180,768]{2,1,0:T(8,128)S(1)} %get-tuple-element.48.partial_ref, bf16[2304,768]{1,0:T(8,128)(2,1)S(1)} %get-tuple-element.49.hidden_ref, ...), custom_call_target="tpu_custom_call" | custom-call | flops 10000000000 | tf_op jit(solution)/shard_map/pallas_call | solution.py:850
  82.7 0.1 collective-permute-start.15
  82.8 0.0 collective-permute-done.12
  82.8 1.1 add_convert_fusion.1
  83.9 0.5 collective-permute-start.13
  84.4 0.8 collective-permute-done.15
  85.2 1.2 add_convert_fusion
  86.3 0.1 collective-permute-start.16
  86.5 14.2 %collective-permute-done.13.refs_0_ = bf16[3,180,768]{2,1,0:T(8,128)(2,1)S(1)} collective-permute-done((bf16[3,180,768]{2,1,0:T(8,128)(2,1)}, bf16[3,180,768]{2,1,0:T(8,128)(2,1)S(1)}, u32[]{:S(2)}, u32[]{:S(2)}) %collective-permute-start.13) | collective-permute-done | bytes 829472 | tf_op jit(solution)/shard_map/ppermute | solution.py:687
  100.7 4.8 %collective-permute-start.14 = (bf16[3,180,768]{2,1,0:T(8,128)(2,1)S(1)}, bf16[3,180,768]{2,1,0:T(8,128)(2,1)S(1)}, u32[]{:S(2)}, u32[]{:S(2)}) collective-permute-start(bf16[3,180,768]{2,1,0:T(8,128)(2,1)S(1)} %collective-permute-done.13.refs_0_), channel_id=1, source_target_pairs={{0,8},{1,9},{8,16},{9,17},{16,24},{17,25},{24,0},{25,1}} | collective-permute-start | bytes 2488328 | tf_op jit(solution)/shard_map/ppermute | solution.py:687
  105.5 5.6 %collective-permute-done.16.chunk_ref = bf16[3,180,768]{2,1,0:T(8,128)(2,1)S(1)} collective-permute-done((bf16[3,180,768]{2,1,0:T(8,128)(2,1)}, bf16[3,180,768]{2,1,0:T(8,128)(2,1)S(1)}, u32[]{:S(2)}, u32[]{:S(2)}) %collective-permute-start.16) | collective-permute-done | bytes 829472 | tf_op jit(solution)/shard_map/ppermute | solution.py:687
  111.1 0.9 shard_map.124.refs_2_
  112.0 6.1 %collective-permute-done.14.refs_1_ = bf16[3,180,768]{2,1,0:T(8,128)(2,1)S(1)} collective-permute-done((bf16[3,180,768]{2,1,0:T(8,128)(2,1)S(1)}, bf16[3,180,768]{2,1,0:T(8,128)(2,1)S(1)}, u32[]{:S(2)}, u32[]{:S(2)}) %collective-permute-start.14) | collective-permute-done | bytes 829472 | tf_op jit(solution)/shard_map/ppermute | solution.py:687
  118.1 0.9 shard_map.125
  (2 shorter events, 0.0 us)
Async XLA Ops:
  0.0 1.3 %copy-start = (bf16[1,192,3072]{2,1,0:T(8,128)(2,1)S(1)}, bf16[1,192,3072]{2,1,0:T(8,128)(2,1)}, u32[]{:S(2)}) copy-start(bf16[1,192,3072]{2,1,0:T(8,128)(2,1)} %param.21) | copy-start | bytes 3538948
  0.0 9.1 %copy-start.6 = (s32[1,8,1]{1,2,0:T(1,128)S(1)}, s32[1,8,1]{1,2,0:T(1,128)}, u32[]{:S(2)}) copy-start(s32[1,8,1]{1,2,0:T(1,128)} %param.13) | copy-start | bytes 100
  1.3 17.7 %collective-permute-start = (bf16[192,1536]{1,0:T(8,128)(2,1)S(1)}, bf16[192,1536]{1,0:T(8,128)(2,1)}, u32[]{:S(2)}, u32[]{:S(2)}) collective-permute-start(bf16[192,1536]{1,0:T(8,128)(2,1)S(1)} %dynamic-slice_bitcast_fusion.held_ref), channel_id=1, source_target_pairs={{0,1},{1,0},{2,4},{3,5},{4,2},{5,3},{6,7},{7,6},{8,9},{9,8},{10,12... | collective-permute-start | bytes 1769480 | tf_op jit(solution)/shard_map/ppermute | solution.py:687
  5.2 13.8 %collective-permute-start.1 = (bf16[192,1536]{1,0:T(8,128)(2,1)}, bf16[192,1536]{1,0:T(8,128)(2,1)}, u32[]{:S(2)}, u32[]{:S(2)}) collective-permute-start(bf16[192,1536]{1,0:T(8,128)(2,1)} %constant_dynamic-slice_fusion), channel_id=1, source_target_pairs={{0,4},{1,5},{2,0},{3,1},{4,6},{5,7},{6,2},{7,3},{8,12},{9,13},{10,... | collective-permute-start | bytes 1769480 | tf_op jit(solution)/shard_map/ppermute | solution.py:687
  5.3 13.7 %collective-permute-start.2 = (bf16[192,1536]{1,0:T(8,128)(2,1)}, bf16[192,1536]{1,0:T(8,128)(2,1)}, u32[]{:S(2)}, u32[]{:S(2)}) collective-permute-start(bf16[192,1536]{1,0:T(8,128)(2,1)} %constant_dynamic-slice_fusion), channel_id=1, source_target_pairs={{0,5},{1,4},{6,3},{7,2},{8,13},{9,12},{14,11},{15,10},{16,21},{17,... | collective-permute-start | bytes 1769480 | tf_op jit(solution)/shard_map/ppermute | solution.py:687
  18.9 6.5 %copy-start.4 = (f32[1,2,768]{2,1,0:T(2,128)S(1)}, f32[1,2,768]{2,1,0:T(2,128)}, u32[]{:S(2)}) copy-start(f32[1,2,768]{2,1,0:T(2,128)} %param.19) | copy-start | bytes 18436
  19.0 6.5 %copy-start.5 = (f32[1,2,768]{2,1,0:T(2,128)S(1)}, f32[1,2,768]{2,1,0:T(2,128)}, u32[]{:S(2)}) copy-start(f32[1,2,768]{2,1,0:T(2,128)} %param.18) | copy-start | bytes 18436
  19.0 7.7 %collective-permute-start.3 = (bf16[6,180,768]{2,1,0:T(8,128)(2,1)S(1)}, bf16[6,180,768]{2,1,0:T(8,128)(2,1)}, u32[]{:S(2)}, u32[]{:S(2)}) collective-permute-start(bf16[6,180,768]{2,1,0:T(8,128)(2,1)S(1)} %shard_map.118.entered_ref), channel_id=1, source_target_pairs={{0,4},{1,5},{2,6},{3,7},{4,0},{5,1},{6,2},{7,3},{8,12},{9,13},{10,... | collective-permute-start | bytes 4976648 | tf_op jit(solution)/shard_map/ppermute | solution.py:687
  19.1 20.4 %collective-permute-start.5 = (bf16[6,180,768]{2,1,0:T(8,128)(2,1)S(1)}, bf16[6,180,768]{2,1,0:T(8,128)(2,1)}, u32[]{:S(2)}, u32[]{:S(2)}) collective-permute-start(bf16[6,180,768]{2,1,0:T(8,128)(2,1)S(1)} %shard_map.118.entered_ref), channel_id=1, source_target_pairs={{2,4},{3,5},{4,2},{5,3},{10,12},{11,13},{12,10},{13,11},{18,20},{1... | collective-permute-start | bytes 4976648 | tf_op jit(solution)/shard_map/ppermute | solution.py:687
  21.0 18.5 %collective-permute-start.7 = (f32[2,2,8,96,96]{4,3,2,1,0:T(8,128)}, f32[2,2,8,96,96]{4,3,2,1,0:T(8,128)}, u32[]{:S(2)}, u32[]{:S(2)}) collective-permute-start(f32[2,2,8,96,96]{4,3,2,1,0:T(8,128)} %bitcast.11.filters_hbm), channel_id=1, source_target_pairs={{0,4},{1,5},{2,6},{3,7},{4,0},{5,1},{6,2},{7,3},{8,12},{9,13},{10,... | collective-permute-start | bytes 3538952 | tf_op jit(solution)/shard_map/ppermute | solution.py:687
  23.9 15.6 %collective-permute-start.6 = (bf16[192,1536]{1,0:T(8,128)(2,1)}, bf16[192,1536]{1,0:T(8,128)(2,1)}, u32[]{:S(2)}, u32[]{:S(2)}) collective-permute-start(bf16[192,1536]{1,0:T(8,128)(2,1)} %broadcast_select_fusion), channel_id=1, source_target_pairs={{0,1},{1,0},{2,3},{3,2},{4,5},{5,4},{6,7},{7,6},{8,9},{9,8},{10,11... | collective-permute-start | bytes 1769480 | tf_op jit(solution)/shard_map/ppermute | solution.py:687
  25.4 1.2 %collective-permute-start.4 = (f32[4,768]{1,0:T(4,128)S(1)}, f32[4,768]{1,0:T(4,128)S(1)}, u32[]{:S(2)}, u32[]{:S(2)}) collective-permute-start(f32[4,768]{1,0:T(4,128)S(1)} %pad_maximum_fusion.norms_ref), channel_id=1, source_target_pairs={{0,4},{1,5},{2,6},{3,7},{4,0},{5,1},{6,2},{7,3},{8,12},{9,13},{10,... | collective-permute-start | bytes 36872 | tf_op jit(solution)/shard_map/ppermute | solution.py:687
  26.7 1.0 copy-start.1
  27.7 15.0 %copy-start.3 = (bf16[1,768,768]{2,1,0:T(8,128)(2,1)S(1)}, bf16[1,768,768]{2,1,0:T(8,128)(2,1)}, u32[]{:S(2)}) copy-start(bf16[1,768,768]{2,1,0:T(8,128)(2,1)} %param.22) | copy-start | bytes 3538948
  27.7 18.5 %copy-start.2 = (bf16[2,2,180,180]{3,2,1,0:T(8,128)(2,1)S(1)}, bf16[2,2,180,180]{3,2,1,0:T(8,128)(2,1)}, u32[]{:S(2)}) copy-start(bf16[2,2,180,180]{3,2,1,0:T(8,128)(2,1)} %constant.34.clone.tables_ref) | copy-start | bytes 777604
  39.5 6.6 %collective-permute-start.8 = (bf16[6,180,768]{2,1,0:T(8,128)(2,1)}, bf16[6,180,768]{2,1,0:T(8,128)(2,1)S(1)}, u32[]{:S(2)}, u32[]{:S(2)}) collective-permute-start(bf16[6,180,768]{2,1,0:T(8,128)(2,1)} %collective-permute-done.5.moved_ref), channel_id=1, source_target_pairs={{0,4},{1,5},{2,6},{3,7},{4,0},{5,1},{6,2},{7,3},{8,12},{9,13},{10,... | collective-permute-start | bytes 4976648 | tf_op jit(solution)/shard_map/ppermute | solution.py:687
  42.7 16.2 %collective-permute-start.9 = (bf16[768,768]{1,0:T(8,128)(2,1)S(1)}, bf16[768,768]{1,0:T(8,128)(2,1)S(1)}, u32[]{:S(2)}, u32[]{:S(2)}) collective-permute-start(bf16[768,768]{1,0:T(8,128)(2,1)S(1)} %bitcast.17), channel_id=1, source_target_pairs={{0,1},{1,0},{2,4},{3,5},{4,2},{5,3},{6,7},{7,6},{8,9},{9,8},{10,12... | collective-permute-start | bytes 3538952 | tf_op jit(solution)/shard_map/ppermute | solution.py:687
  58.9 3.6 %collective-permute-start.10 = (bf16[12,180,384]{2,1,0:T(8,128)(2,1)S(1)}, bf16[12,180,384]{2,1,0:T(8,128)(2,1)S(1)}, u32[]{:S(2)}, u32[]{:S(2)}) collective-permute-start(bf16[12,180,384]{2,1,0:T(8,128)(2,1)S(1)} %get-tuple-element.44.mine_ref), channel_id=1, source_target_pairs={{0,4},{1,5},{2,6},{3,7},{4,0},{5,1},{6,2},{7,3},{8,12},{9,13},{10,... | collective-permute-start | bytes 4976648 | tf_op jit(solution)/shard_map/ppermute | solution.py:687
  58.9 16.0 %collective-permute-start.11 = (bf16[768,768]{1,0:T(8,128)(2,1)S(1)}, bf16[768,768]{1,0:T(8,128)(2,1)S(1)}, u32[]{:S(2)}, u32[]{:S(2)}) collective-permute-start(bf16[768,768]{1,0:T(8,128)(2,1)S(1)} %bitcast.18), channel_id=1, source_target_pairs={{2,5},{3,4},{4,3},{5,2},{10,13},{11,12},{12,11},{13,10},{18,21},{1... | collective-permute-start | bytes 3538952 | tf_op jit(solution)/shard_map/ppermute | solution.py:687
  77.4 5.4 %collective-permute-start.12 = (bf16[3,180,768]{2,1,0:T(8,128)(2,1)S(1)}, bf16[3,180,768]{2,1,0:T(8,128)(2,1)S(1)}, u32[]{:S(2)}, u32[]{:S(2)}) collective-permute-start(bf16[3,180,768]{2,1,0:T(8,128)(2,1)S(1)} %get-tuple-element.52), channel_id=1, source_target_pairs={{0,4},{1,5},{2,6},{3,7},{4,0},{5,1},{6,2},{7,3},{8,12},{9,13},{10,... | collective-permute-start | bytes 2488328 | tf_op jit(solution)/shard_map/ppermute | solution.py:687
  82.7 2.4 %collective-permute-start.15 = (bf16[3,180,768]{2,1,0:T(8,128)(2,1)S(1)}, bf16[3,180,768]{2,1,0:T(8,128)(2,1)S(1)}, u32[]{:S(2)}, u32[]{:S(2)}) collective-permute-start(bf16[3,180,768]{2,1,0:T(8,128)(2,1)S(1)} %get-tuple-element.54), channel_id=1, source_target_pairs={{0,4},{1,5},{2,6},{3,7},{4,0},{5,1},{6,2},{7,3},{8,12},{9,13},{10,... | collective-permute-start | bytes 2488328 | tf_op jit(solution)/shard_map/ppermute | solution.py:687
  83.9 16.7 %collective-permute-start.13 = (bf16[3,180,768]{2,1,0:T(8,128)(2,1)}, bf16[3,180,768]{2,1,0:T(8,128)(2,1)S(1)}, u32[]{:S(2)}, u32[]{:S(2)}) collective-permute-start(bf16[3,180,768]{2,1,0:T(8,128)(2,1)} %add_convert_fusion.1), channel_id=1, source_target_pairs={{0,4},{1,5},{2,0},{3,1},{4,6},{5,7},{6,10},{7,11},{8,12},{9,13},{1... | collective-permute-start | bytes 2488328 | tf_op jit(solution)/shard_map/ppermute | solution.py:687
  86.3 24.7 %collective-permute-start.16 = (bf16[3,180,768]{2,1,0:T(8,128)(2,1)}, bf16[3,180,768]{2,1,0:T(8,128)(2,1)S(1)}, u32[]{:S(2)}, u32[]{:S(2)}) collective-permute-start(bf16[3,180,768]{2,1,0:T(8,128)(2,1)} %add_convert_fusion), channel_id=1, source_target_pairs={{0,4},{1,5},{2,8},{3,9},{4,6},{5,7},{6,10},{7,11},{8,12},{9,13},{1... | collective-permute-start | bytes 2488328 | tf_op jit(solution)/shard_map/ppermute | solution.py:687
  100.7 17.5 %collective-permute-start.14 = (bf16[3,180,768]{2,1,0:T(8,128)(2,1)S(1)}, bf16[3,180,768]{2,1,0:T(8,128)(2,1)S(1)}, u32[]{:S(2)}, u32[]{:S(2)}) collective-permute-start(bf16[3,180,768]{2,1,0:T(8,128)(2,1)S(1)} %collective-permute-done.13.refs_0_), channel_id=1, source_target_pairs={{0,8},{1,9},{8,16},{9,17},{16,24},{17,25},{24,0},{25,1}} | collective-permute-start | bytes 2488328 | tf_op jit(solution)/shard_map/ppermute | solution.py:687

commit v5 on v4

--- a/solution.py
+++ b/solution.py
@@ -400,8 +400,14 @@
 ):
     half, space = scalars_ref[0], scalars_ref[1]
     near = half == space
-    load = load_one(near, far_state_ref, moved_ref, state_ref, state_sem)
     rows, width, _ = state_ref.shape
+    row_loads = start_loads(
+        near,
+        [far_state_ref.at[row] for row in range(rows)],
+        [moved_ref.at[row] for row in range(rows)],
+        [state_ref.at[row] for row in range(rows)],
+        state_sem,
+    )
     kept = grid_ref.shape[1] // 2
     groups = modes_ref.shape[0]
     side = filters_ref.shape[-1]
@@ -413,13 +419,13 @@
     odd_sign = jnp.where(space == 0, 1.0, -1.0)
     forward = [tables_ref[part, 0, : 2 * kept, :width] for part in range(2)]
     backward = [tables_ref[part, 1, :width, : 2 * kept] for part in range(2)]
-    load.wait()
+    mixing_ref[...] = jnp.zeros_like(mixing_ref)
     for row in range(rows):
+        row_loads[row].wait()
         carried = state_ref[row].astype(jnp.float32)
         centred, factor = centre(carried)
         base_ref[row] = carried + (centred * factor * norms[0:1] + norms[2:3])
         grid_ref[rows + row] = row_spectra(half == 0, centred, factor, norms, forward)
-    mixing_ref[...] = jnp.zeros_like(mixing_ref)
     own_load.wait()
     first, second = pl.ds(0, side), pl.ds(GROUP_LANES, side)
     for layer in range(2):
@@ -580,20 +586,20 @@
     scalars_ref,
     partial_ref,
     hidden_ref,
-    first_ref,
-    second_ref,
-    own_ref,
-    other_ref,
-    down_ref,
-    sem,
+    *rest,
 ):
     near = scalars_ref[0] == scalars_ref[1]
-    load = load_one(near, first_ref, second_ref, down_ref, sem)
+    if number == 0:
+        first_ref, second_ref, own_ref, other_ref, down_ref, sem = rest
+        load = load_one(near, first_ref, second_ref, down_ref, sem)
+    else:
+        down_ref, own_ref, other_ref = rest
     count, width, _ = own_ref.shape
     rows = partial_ref.shape[0] // 2
     size = count * ROW_STEP
     own_part = jnp.where(near, 0, 1)
-    load.wait()
+    if number == 0:
+        load.wait()
     for target, part in ((other_ref, 1 - own_part), (own_ref, own_part)):
         here = pl.ds(pl.multiple_of(2 * size * number + part * size, size), size)
         update = dot(hidden_ref[here], down_ref[...])
@@ -790,7 +796,7 @@
             VMEM((2, half_groups, 2 * GROUP_LANES, 2 * GROUP_LANES), bf16),
             VMEM(state.shape, bf16),
             pltpu.SemaphoreType.DMA,
-            pltpu.SemaphoreType.DMA,
+            pltpu.SemaphoreType.DMA((rows,)),
         ],
         cost_estimate=cost(11),
         compiler_params=params(24),
@@ -847,21 +853,26 @@
     )
     landed, ready = [], []
     for number in range(parts):
-        own, other = pl.pallas_call(
+        sums = [
+            jax.ShapeDtypeStruct((rows // parts, width, channels), f32),
+            jax.ShapeDtypeStruct((rows // parts, width, channels), bf16),
+        ]
+        if number == 0:
+            shapes = sums + [VMEM((hidden_half // 2, channels), bf16)]
+            weights, specs = (down_first, down_second), [LEFT] * 2
+            scratch = [pltpu.SemaphoreType.DMA]
+        else:
+            shapes, weights, specs, scratch = sums, (down_last,), [WHOLE], []
+        own, other, *handed = pl.pallas_call(
             functools.partial(update_kernel, number),
-            out_shape=[
-                jax.ShapeDtypeStruct((rows // parts, width, channels), f32),
-                jax.ShapeDtypeStruct((rows // parts, width, channels), bf16),
-            ],
-            in_specs=[SCALARS] + [WHOLE] * 2 + [LEFT] * 2,
-            out_specs=[WHOLE] * 2,
-            scratch_shapes=[
-                VMEM((hidden_half // 2, channels), bf16),
-                pltpu.SemaphoreType.DMA,
-            ],
+            out_shape=shapes,
+            in_specs=[SCALARS] + [WHOLE] * 2 + specs,
+            out_specs=[WHOLE] * len(shapes),
+            scratch_shapes=scratch,
             cost_estimate=cost(50),
             compiler_params=params(12),
-        )(scalars, partial, hidden, down_first, down_second)
+        )(scalars, partial, hidden, *weights)
+        down_last = handed[0] if handed else down_last
         ready.append((own + send(other, swap_cores).astype(f32)).astype(bf16))
         if number + 1 < parts:
             landed.append([send(ready[-1], onward_by_space)])

time: 120 us -> 120 us (level)
  transfers between devices with their start and end apart: 17 -> 17, of which waited for: 9 -> 9; matrix products, arithmetic and copies ran while one was open for 5% -> 5% of each run, Pallas kernels for 31% -> 32%
where the time goes in v5:
time: 120 us; the launch traced here: 119 us
  waiting for transfers between devices  44 us (37%)
  Pallas kernels  41.7 us (35%)
  starting transfers between devices  25.1 us (21%)
  other arithmetic  4.9 us (4%)
  local copies, waits for them, and re-layouts  3.17 us (3%)
    ppermute x17, waiting for transfers between devices, send(): return lax.ppermute(value, MESH_AXES, pairs)  44 us
    ppermute x17, starting transfers between devices, send(): return lax.ppermute(value, MESH_AXES, pairs)  25.1 us
    pallas_call x1, Pallas kernels, fast_on_device(): pl.pallas_call(functools.partial(hidden_kernel, rows // parts), out_shape...  12.4 us
    pallas_call x1, Pallas kernels, fast_on_device(): pl.pallas_call(filter_kernel, out_shape=[jax.ShapeDtypeStruct((2 * rows,...  10.2 us
    pallas_call x1, Pallas kernels, fast_on_device(): pl.pallas_call(enter_kernel, out_shape=VMEM(state.shape, bf16), in_specs=...  9.14 us
    pallas_call x2, Pallas kernels, fast_on_device(): pl.pallas_call(functools.partial(update_kernel, number), out_shape=shapes...  4.78 us
    pallas_call x1, Pallas kernels, fast_on_device(): pl.pallas_call(near_kernel, out_shape=[VMEM((rows, 2 * KW, lanes), f32),...  3.45 us
  transfers between devices with their start and end apart: 17, of which 9 were waited for; matrix products, arithmetic and copies ran while one was open for 5% of the time, Pallas kernels for 32%

profile of v5, /device:TPU:0, one launch (start us, length us, event | category | flops | bytes accessed | tf_op | source)
XLA Modules:
  0.0 119.3 jit_solution(4942414595621580284)
XLA Ops:
  0.0 0.0 copy-start
  0.0 0.0 copy-start.6
  0.0 1.3 %copy-done = bf16[1,192,3072]{2,1,0:T(8,128)(2,1)S(1)} copy-done((bf16[1,192,3072]{2,1,0:T(8,128)(2,1)S(1)}, bf16[1,192,3072]{2,1,0:T(8,128)(2,1)}, u32[]{:S(2)}) %copy-start) | copy-done | bytes 1179672
  1.3 3.0 %collective-permute-start = (bf16[192,1536]{1,0:T(8,128)(2,1)S(1)}, bf16[192,1536]{1,0:T(8,128)(2,1)}, u32[]{:S(2)}, u32[]{:S(2)}) collective-permute-start(bf16[192,1536]{1,0:T(8,128)(2,1)S(1)} %dynamic-slice_bitcast_fusion.held_ref), channel_id=1, source_target_pairs={{0,1},{1,0},{2,4},{3,5},{4,2},{5,3},{6,7},{7,6},{8,9},{9,8},{10,12... | collective-permute-start | bytes 1769480 | tf_op jit(solution)/shard_map/ppermute | solution.py:693
  4.3 0.9 constant_dynamic-slice_fusion
  5.2 0.1 collective-permute-start.1
  5.3 3.9 %collective-permute-start.2 = (bf16[192,1536]{1,0:T(8,128)(2,1)}, bf16[192,1536]{1,0:T(8,128)(2,1)}, u32[]{:S(2)}, u32[]{:S(2)}) collective-permute-start(bf16[192,1536]{1,0:T(8,128)(2,1)} %constant_dynamic-slice_fusion), channel_id=1, source_target_pairs={{0,5},{1,4},{6,3},{7,2},{8,13},{9,12},{14,11},{15,10},{16,21},{17,... | collective-permute-start | bytes 1769480 | tf_op jit(solution)/shard_map/ppermute | solution.py:693
  9.1 0.0 copy-done.6
  9.2 0.7 pad_add_fusion.1.scalars_ref
  9.8 9.1 %shard_map.118.entered_ref = bf16[6,180,768]{2,1,0:T(8,128)(2,1)S(1)} custom-call(s32[2]{0:T(128)} %pad_add_fusion.1.scalars_ref, bf16[6,180,768]{2,1,0:T(8,128)(2,1)} %bitcast.20, bf16[768,1280]{1,0:T(8,128)(2,1)} %readout_hbm.1, bf16[1280,768]{1,0:T(8,128)(2,1)} %lifting_hbm.1, bf16[6,180,768]{2,1,0:T(8,128)(2,1)} %pos_hbm.1, bf16[100,768]{1,0:T(8,128)(2,1)} %table_hbm.1), custom_call_target="tpu_custom_call" | custom-call | flops 1800000000 | tf_op jit(solution)/shard_map/pallas_call | solution.py:732
  18.9 0.0 copy-start.4
  19.0 0.0 copy-start.5
  19.0 0.0 collective-permute-done.first_ref
  19.0 0.0 collective-permute-done.1.second_ref
  19.0 0.0 collective-permute-done.2.third_ref
  19.0 0.1 collective-permute-start.3
  19.1 1.9 %collective-permute-start.5 = (bf16[6,180,768]{2,1,0:T(8,128)(2,1)S(1)}, bf16[6,180,768]{2,1,0:T(8,128)(2,1)}, u32[]{:S(2)}, u32[]{:S(2)}) collective-permute-start(bf16[6,180,768]{2,1,0:T(8,128)(2,1)S(1)} %shard_map.118.entered_ref), channel_id=1, source_target_pairs={{2,4},{3,5},{4,2},{5,3},{10,12},{11,13},{12,10},{13,11},{18,20},{1... | collective-permute-start | bytes 4976648 | tf_op jit(solution)/shard_map/ppermute | solution.py:693
  21.0 1.0 collective-permute-start.7
  22.0 1.9 %broadcast_select_fusion = bf16[192,1536]{1,0:T(8,128)(2,1)} fusion(bf16[192,1536]{1,0:T(8,128)(2,1)} %collective-permute-done.1.second_ref, bf16[192,1536]{1,0:T(8,128)(2,1)} %collective-permute-done.first_ref, pred[]{:T(512)S(6)} %eq.9), kind=kLoop, calls=%fused_computation.3 | loop fusion | flops 294912 | bytes 1769473 | tf_op jit(solution)/shard_map/jit(_where)/select_n | solution.py:761
  23.9 1.5 %collective-permute-start.6 = (bf16[192,1536]{1,0:T(8,128)(2,1)}, bf16[192,1536]{1,0:T(8,128)(2,1)}, u32[]{:S(2)}, u32[]{:S(2)}) collective-permute-start(bf16[192,1536]{1,0:T(8,128)(2,1)} %broadcast_select_fusion), channel_id=1, source_target_pairs={{0,1},{1,0},{2,3},{3,2},{4,5},{5,4},{6,7},{7,6},{8,9},{9,8},{10,11... | collective-permute-start | bytes 1769480 | tf_op jit(solution)/shard_map/ppermute | solution.py:693
  25.4 0.0 copy-done.4
  25.4 0.0 copy-done.5
  25.4 0.1 collective-permute-start.4
  25.5 0.1 pad_add_fusion.scalars_ref
  25.6 1.1 collective-permute-done.4.taken_norms_ref
  26.7 0.0 collective-permute-done.3.near_state_ref
  26.7 0.0 copy-start.1
  26.7 1.0 copy-done.1
  27.7 0.0 copy-start.3
  27.7 0.0 copy-start.2
  27.7 3.4 %shard_map.119 = (f32[6,176,512]{2,1,0:T(8,128)S(1)}, f32[6,180,768]{2,1,0:T(8,128)S(1)}) custom-call(s32[3]{0:T(128)S(1)} %pad_add_fusion.scalars_ref, bf16[6,180,768]{2,1,0:T(8,128)(2,1)S(1)} %shard_map.118.entered_ref, bf16[6,180,768]{2,1,0:T(8,128)(2,1)} %collective-permute-done.3.near_state_ref, f32[4,768]{1,0:T(4,128)S(1)} %pad_maximum_fusion.norms_ref, ...), custom_call_target="tpu_custom_call" | custom-call | flops 1000000000 | tf_op jit(solution)/shard_map/pallas_call | solution.py:770
  31.1 8.4 %collective-permute-done.6.relayed_ref = bf16[192,1536]{1,0:T(8,128)(2,1)} collective-permute-done((bf16[192,1536]{1,0:T(8,128)(2,1)}, bf16[192,1536]{1,0:T(8,128)(2,1)}, u32[]{:S(2)}, u32[]{:S(2)}) %collective-permute-start.6) | collective-permute-done | bytes 589856 | tf_op jit(solution)/shard_map/ppermute | solution.py:693
  39.5 0.0 collective-permute-done.7.taken_filters_hbm
  39.5 0.0 collective-permute-done.5.moved_ref
  39.5 3.2 %collective-permute-start.8 = (bf16[6,180,768]{2,1,0:T(8,128)(2,1)}, bf16[6,180,768]{2,1,0:T(8,128)(2,1)S(1)}, u32[]{:S(2)}, u32[]{:S(2)}) collective-permute-start(bf16[6,180,768]{2,1,0:T(8,128)(2,1)} %collective-permute-done.5.moved_ref), channel_id=1, source_target_pairs={{0,4},{1,5},{2,6},{3,7},{4,0},{5,1},{6,2},{7,3},{8,12},{9,13},{10,... | collective-permute-start | bytes 4976648 | tf_op jit(solution)/shard_map/ppermute | solution.py:693
  42.7 0.0 copy-done.3
  42.7 1.2 collective-permute-start.9
  43.9 2.2 %collective-permute-done.8.far_state_ref = bf16[6,180,768]{2,1,0:T(8,128)(2,1)S(1)} collective-permute-done((bf16[6,180,768]{2,1,0:T(8,128)(2,1)}, bf16[6,180,768]{2,1,0:T(8,128)(2,1)S(1)}, u32[]{:S(2)}, u32[]{:S(2)}) %collective-permute-start.8) | collective-permute-done | bytes 1658912 | tf_op jit(solution)/shard_map/ppermute | solution.py:693
  46.2 0.0 copy-done.2
  46.2 10.2 %shard_map.120 = (bf16[12,180,384]{2,1,0:T(8,128)(2,1)S(1)}, f32[6,180,768]{2,1,0:T(8,128)S(1)}) custom-call(s32[3]{0:T(128)S(1)} %pad_add_fusion.scalars_ref, bf16[6,180,768]{2,1,0:T(8,128)(2,1)} %collective-permute-done.5.moved_ref, bf16[6,180,768]{2,1,0:T(8,128)(2,1)S(1)} %collective-permute-done.8.far_state_ref, f32[4,768]{1,0:T(4,128)S(1)} %pad_maximum_fusion.norms_ref, ...), custom_call_target="tpu_custom_call" | custom-call | flops 2200000000 | tf_op jit(solution)/shard_map/pallas_call | solution.py:784
  56.3 2.6 %collective-permute-done.9.down_first_ref.rest_0_ = bf16[768,768]{1,0:T(8,128)(2,1)S(1)} collective-permute-done((bf16[768,768]{1,0:T(8,128)(2,1)S(1)}, bf16[768,768]{1,0:T(8,128)(2,1)S(1)}, u32[]{:S(2)}, u32[]{:S(2)}) %collective-permute-start.9) | collective-permute-done | bytes 1179680 | tf_op jit(solution)/shard_map/ppermute | solution.py:693
  58.9 0.0 collective-permute-start.10
  58.9 0.7 collective-permute-start.11
  59.7 2.8 %collective-permute-done.10.theirs_ref = bf16[12,180,384]{2,1,0:T(8,128)(2,1)S(1)} collective-permute-done((bf16[12,180,384]{2,1,0:T(8,128)(2,1)S(1)}, bf16[12,180,384]{2,1,0:T(8,128)(2,1)S(1)}, u32[]{:S(2)}, u32[]{:S(2)}) %collective-permute-start.10) | collective-permute-done | bytes 1658912 | tf_op jit(solution)/shard_map/ppermute | solution.py:693
  62.5 12.4 %shard_map.121 = (f32[12,180,768]{2,1,0:T(8,128)S(1)}, bf16[2304,768]{1,0:T(8,128)(2,1)S(1)}) custom-call(s32[3]{0:T(128)S(1)} %pad_add_fusion.scalars_ref, f32[6,180,768]{2,1,0:T(8,128)S(1)} %get-tuple-element.34.near_base_ref, f32[6,180,768]{2,1,0:T(8,128)S(1)} %get-tuple-element.41.far_base_ref, bf16[12,180,384]{2,1,0:T(8,128)(2,1)S(1)} %get-tuple-element.45.mine_ref, ...), custom_call_target="tpu_custom_call" | custom-call | flops 2200000000 | tf_op jit(solution)/shard_map/pallas_call | solution.py:821
  74.9 0.0 collective-permute-done.11.rest_1_
  74.9 2.7 %shard_map.122 = (f32[3,180,768]{2,1,0:T(8,128)S(1)}, bf16[3,180,768]{2,1,0:T(8,128)(2,1)S(1)}, bf16[768,768]{1,0:T(8,128)(2,1)S(1)}) custom-call(s32[3]{0:T(128)S(1)} %pad_add_fusion.scalars_ref, f32[12,180,768]{2,1,0:T(8,128)S(1)} %get-tuple-element.49.partial_ref, bf16[2304,768]{1,0:T(8,128)(2,1)S(1)} %get-tuple-element.50.hidden_ref, ...), custom_call_target="tpu_custom_call" | custom-call | flops 10000000000 | tf_op jit(solution)/shard_map/pallas_call | solution.py:866
  77.6 3.0 %collective-permute-start.12 = (bf16[3,180,768]{2,1,0:T(8,128)(2,1)S(1)}, bf16[3,180,768]{2,1,0:T(8,128)(2,1)S(1)}, u32[]{:S(2)}, u32[]{:S(2)}) collective-permute-start(bf16[3,180,768]{2,1,0:T(8,128)(2,1)S(1)} %get-tuple-element.53), channel_id=1, source_target_pairs={{0,4},{1,5},{2,6},{3,7},{4,0},{5,1},{6,2},{7,3},{8,12},{9,13},{10,... | collective-permute-start | bytes 2488328 | tf_op jit(solution)/shard_map/ppermute | solution.py:693
  80.6 2.1 %shard_map.123 = (f32[3,180,768]{2,1,0:T(8,128)S(1)}, bf16[3,180,768]{2,1,0:T(8,128)(2,1)S(1)}) custom-call(s32[3]{0:T(128)S(1)} %pad_add_fusion.scalars_ref, f32[12,180,768]{2,1,0:T(8,128)S(1)} %get-tuple-element.49.partial_ref, bf16[2304,768]{1,0:T(8,128)(2,1)S(1)} %get-tuple-element.50.hidden_ref, bf16[768,768]{1,0:T(8,128)(2,1)S(1)} %get-tuple-element.54.rest_0_), custom_call_target="tpu_custom_call" | custom-call | flops 10000000000 | tf_op jit(solution)/shard_map/pallas_call | solution.py:866
  82.7 0.1 collective-permute-start.15
  82.8 0.0 collective-permute-done.12
  82.8 1.1 add_convert_fusion.1
  83.9 0.5 collective-permute-start.13
  84.4 0.8 collective-permute-done.15
  85.2 1.1 add_convert_fusion
  86.3 0.1 collective-permute-start.16
  86.4 14.3 %collective-permute-done.13.refs_0_ = bf16[3,180,768]{2,1,0:T(8,128)(2,1)S(1)} collective-permute-done((bf16[3,180,768]{2,1,0:T(8,128)(2,1)}, bf16[3,180,768]{2,1,0:T(8,128)(2,1)S(1)}, u32[]{:S(2)}, u32[]{:S(2)}) %collective-permute-start.13) | collective-permute-done | bytes 829472 | tf_op jit(solution)/shard_map/ppermute | solution.py:693
  100.7 4.8 %collective-permute-start.14 = (bf16[3,180,768]{2,1,0:T(8,128)(2,1)S(1)}, bf16[3,180,768]{2,1,0:T(8,128)(2,1)S(1)}, u32[]{:S(2)}, u32[]{:S(2)}) collective-permute-start(bf16[3,180,768]{2,1,0:T(8,128)(2,1)S(1)} %collective-permute-done.13.refs_0_), channel_id=1, source_target_pairs={{0,8},{1,9},{8,16},{9,17},{16,24},{17,25},{24,0},{25,1}} | collective-permute-start | bytes 2488328 | tf_op jit(solution)/shard_map/ppermute | solution.py:693
  105.6 5.4 %collective-permute-done.16.chunk_ref = bf16[3,180,768]{2,1,0:T(8,128)(2,1)S(1)} collective-permute-done((bf16[3,180,768]{2,1,0:T(8,128)(2,1)}, bf16[3,180,768]{2,1,0:T(8,128)(2,1)S(1)}, u32[]{:S(2)}, u32[]{:S(2)}) %collective-permute-start.16) | collective-permute-done | bytes 829472 | tf_op jit(solution)/shard_map/ppermute | solution.py:693
  111.0 0.9 shard_map.124.refs_2_
  111.9 6.3 %collective-permute-done.14.refs_1_ = bf16[3,180,768]{2,1,0:T(8,128)(2,1)S(1)} collective-permute-done((bf16[3,180,768]{2,1,0:T(8,128)(2,1)S(1)}, bf16[3,180,768]{2,1,0:T(8,128)(2,1)S(1)}, u32[]{:S(2)}, u32[]{:S(2)}) %collective-permute-start.14) | collective-permute-done | bytes 829472 | tf_op jit(solution)/shard_map/ppermute | solution.py:693
  118.2 0.9 shard_map.125
  (2 shorter events, 0.0 us)
Async XLA Ops:
  0.0 1.3 %copy-start = (bf16[1,192,3072]{2,1,0:T(8,128)(2,1)S(1)}, bf16[1,192,3072]{2,1,0:T(8,128)(2,1)}, u32[]{:S(2)}) copy-start(bf16[1,192,3072]{2,1,0:T(8,128)(2,1)} %param.21) | copy-start | bytes 3538948
  0.0 9.1 %copy-start.6 = (s32[1,8,1]{1,2,0:T(1,128)S(1)}, s32[1,8,1]{1,2,0:T(1,128)}, u32[]{:S(2)}) copy-start(s32[1,8,1]{1,2,0:T(1,128)} %param.13) | copy-start | bytes 100
  1.3 17.7 %collective-permute-start = (bf16[192,1536]{1,0:T(8,128)(2,1)S(1)}, bf16[192,1536]{1,0:T(8,128)(2,1)}, u32[]{:S(2)}, u32[]{:S(2)}) collective-permute-start(bf16[192,1536]{1,0:T(8,128)(2,1)S(1)} %dynamic-slice_bitcast_fusion.held_ref), channel_id=1, source_target_pairs={{0,1},{1,0},{2,4},{3,5},{4,2},{5,3},{6,7},{7,6},{8,9},{9,8},{10,12... | collective-permute-start | bytes 1769480 | tf_op jit(solution)/shard_map/ppermute | solution.py:693
  5.2 13.8 %collective-permute-start.1 = (bf16[192,1536]{1,0:T(8,128)(2,1)}, bf16[192,1536]{1,0:T(8,128)(2,1)}, u32[]{:S(2)}, u32[]{:S(2)}) collective-permute-start(bf16[192,1536]{1,0:T(8,128)(2,1)} %constant_dynamic-slice_fusion), channel_id=1, source_target_pairs={{0,4},{1,5},{2,0},{3,1},{4,6},{5,7},{6,2},{7,3},{8,12},{9,13},{10,... | collective-permute-start | bytes 1769480 | tf_op jit(solution)/shard_map/ppermute | solution.py:693
  5.3 13.7 %collective-permute-start.2 = (bf16[192,1536]{1,0:T(8,128)(2,1)}, bf16[192,1536]{1,0:T(8,128)(2,1)}, u32[]{:S(2)}, u32[]{:S(2)}) collective-permute-start(bf16[192,1536]{1,0:T(8,128)(2,1)} %constant_dynamic-slice_fusion), channel_id=1, source_target_pairs={{0,5},{1,4},{6,3},{7,2},{8,13},{9,12},{14,11},{15,10},{16,21},{17,... | collective-permute-start | bytes 1769480 | tf_op jit(solution)/shard_map/ppermute | solution.py:693
  18.9 6.5 %copy-start.4 = (f32[1,2,768]{2,1,0:T(2,128)S(1)}, f32[1,2,768]{2,1,0:T(2,128)}, u32[]{:S(2)}) copy-start(f32[1,2,768]{2,1,0:T(2,128)} %param.19) | copy-start | bytes 18436
  19.0 6.5 %copy-start.5 = (f32[1,2,768]{2,1,0:T(2,128)S(1)}, f32[1,2,768]{2,1,0:T(2,128)}, u32[]{:S(2)}) copy-start(f32[1,2,768]{2,1,0:T(2,128)} %param.18) | copy-start | bytes 18436
  19.0 7.7 %collective-permute-start.3 = (bf16[6,180,768]{2,1,0:T(8,128)(2,1)S(1)}, bf16[6,180,768]{2,1,0:T(8,128)(2,1)}, u32[]{:S(2)}, u32[]{:S(2)}) collective-permute-start(bf16[6,180,768]{2,1,0:T(8,128)(2,1)S(1)} %shard_map.118.entered_ref), channel_id=1, source_target_pairs={{0,4},{1,5},{2,6},{3,7},{4,0},{5,1},{6,2},{7,3},{8,12},{9,13},{10,... | collective-permute-start | bytes 4976648 | tf_op jit(solution)/shard_map/ppermute | solution.py:693
  19.1 20.4 %collective-permute-start.5 = (bf16[6,180,768]{2,1,0:T(8,128)(2,1)S(1)}, bf16[6,180,768]{2,1,0:T(8,128)(2,1)}, u32[]{:S(2)}, u32[]{:S(2)}) collective-permute-start(bf16[6,180,768]{2,1,0:T(8,128)(2,1)S(1)} %shard_map.118.entered_ref), channel_id=1, source_target_pairs={{2,4},{3,5},{4,2},{5,3},{10,12},{11,13},{12,10},{13,11},{18,20},{1... | collective-permute-start | bytes 4976648 | tf_op jit(solution)/shard_map/ppermute | solution.py:693
  21.0 18.5 %collective-permute-start.7 = (f32[2,2,8,96,96]{4,3,2,1,0:T(8,128)}, f32[2,2,8,96,96]{4,3,2,1,0:T(8,128)}, u32[]{:S(2)}, u32[]{:S(2)}) collective-permute-start(f32[2,2,8,96,96]{4,3,2,1,0:T(8,128)} %bitcast.11.filters_hbm), channel_id=1, source_target_pairs={{0,4},{1,5},{2,6},{3,7},{4,0},{5,1},{6,2},{7,3},{8,12},{9,13},{10,... | collective-permute-start | bytes 3538952 | tf_op jit(solution)/shard_map/ppermute | solution.py:693
  23.9 15.6 %collective-permute-start.6 = (bf16[192,1536]{1,0:T(8,128)(2,1)}, bf16[192,1536]{1,0:T(8,128)(2,1)}, u32[]{:S(2)}, u32[]{:S(2)}) collective-permute-start(bf16[192,1536]{1,0:T(8,128)(2,1)} %broadcast_select_fusion), channel_id=1, source_target_pairs={{0,1},{1,0},{2,3},{3,2},{4,5},{5,4},{6,7},{7,6},{8,9},{9,8},{10,11... | collective-permute-start | bytes 1769480 | tf_op jit(solution)/shard_map/ppermute | solution.py:693
  25.4 1.2 %collective-permute-start.4 = (f32[4,768]{1,0:T(4,128)S(1)}, f32[4,768]{1,0:T(4,128)S(1)}, u32[]{:S(2)}, u32[]{:S(2)}) collective-permute-start(f32[4,768]{1,0:T(4,128)S(1)} %pad_maximum_fusion.norms_ref), channel_id=1, source_target_pairs={{0,4},{1,5},{2,6},{3,7},{4,0},{5,1},{6,2},{7,3},{8,12},{9,13},{10,... | collective-permute-start | bytes 36872 | tf_op jit(solution)/shard_map/ppermute | solution.py:693
  26.7 1.0 copy-start.1
  27.7 15.0 %copy-start.3 = (bf16[1,768,768]{2,1,0:T(8,128)(2,1)S(1)}, bf16[1,768,768]{2,1,0:T(8,128)(2,1)}, u32[]{:S(2)}) copy-start(bf16[1,768,768]{2,1,0:T(8,128)(2,1)} %param.22) | copy-start | bytes 3538948
  27.7 18.5 %copy-start.2 = (bf16[2,2,180,180]{3,2,1,0:T(8,128)(2,1)S(1)}, bf16[2,2,180,180]{3,2,1,0:T(8,128)(2,1)}, u32[]{:S(2)}) copy-start(bf16[2,2,180,180]{3,2,1,0:T(8,128)(2,1)} %constant.34.clone.tables_ref) | copy-start | bytes 777604
  39.5 6.6 %collective-permute-start.8 = (bf16[6,180,768]{2,1,0:T(8,128)(2,1)}, bf16[6,180,768]{2,1,0:T(8,128)(2,1)S(1)}, u32[]{:S(2)}, u32[]{:S(2)}) collective-permute-start(bf16[6,180,768]{2,1,0:T(8,128)(2,1)} %collective-permute-done.5.moved_ref), channel_id=1, source_target_pairs={{0,4},{1,5},{2,6},{3,7},{4,0},{5,1},{6,2},{7,3},{8,12},{9,13},{10,... | collective-permute-start | bytes 4976648 | tf_op jit(solution)/shard_map/ppermute | solution.py:693
  42.7 16.2 %collective-permute-start.9 = (bf16[768,768]{1,0:T(8,128)(2,1)S(1)}, bf16[768,768]{1,0:T(8,128)(2,1)S(1)}, u32[]{:S(2)}, u32[]{:S(2)}) collective-permute-start(bf16[768,768]{1,0:T(8,128)(2,1)S(1)} %bitcast.17), channel_id=1, source_target_pairs={{0,1},{1,0},{2,4},{3,5},{4,2},{5,3},{6,7},{7,6},{8,9},{9,8},{10,12... | collective-permute-start | bytes 3538952 | tf_op jit(solution)/shard_map/ppermute | solution.py:693
  58.9 3.6 %collective-permute-start.10 = (bf16[12,180,384]{2,1,0:T(8,128)(2,1)S(1)}, bf16[12,180,384]{2,1,0:T(8,128)(2,1)S(1)}, u32[]{:S(2)}, u32[]{:S(2)}) collective-permute-start(bf16[12,180,384]{2,1,0:T(8,128)(2,1)S(1)} %get-tuple-element.45.mine_ref), channel_id=1, source_target_pairs={{0,4},{1,5},{2,6},{3,7},{4,0},{5,1},{6,2},{7,3},{8,12},{9,13},{10,... | collective-permute-start | bytes 4976648 | tf_op jit(solution)/shard_map/ppermute | solution.py:693
  58.9 16.0 %collective-permute-start.11 = (bf16[768,768]{1,0:T(8,128)(2,1)S(1)}, bf16[768,768]{1,0:T(8,128)(2,1)S(1)}, u32[]{:S(2)}, u32[]{:S(2)}) collective-permute-start(bf16[768,768]{1,0:T(8,128)(2,1)S(1)} %bitcast.18), channel_id=1, source_target_pairs={{2,5},{3,4},{4,3},{5,2},{10,13},{11,12},{12,11},{13,10},{18,21},{1... | collective-permute-start | bytes 3538952 | tf_op jit(solution)/shard_map/ppermute | solution.py:693
  77.6 5.2 %collective-permute-start.12 = (bf16[3,180,768]{2,1,0:T(8,128)(2,1)S(1)}, bf16[3,180,768]{2,1,0:T(8,128)(2,1)S(1)}, u32[]{:S(2)}, u32[]{:S(2)}) collective-permute-start(bf16[3,180,768]{2,1,0:T(8,128)(2,1)S(1)} %get-tuple-element.53), channel_id=1, source_target_pairs={{0,4},{1,5},{2,6},{3,7},{4,0},{5,1},{6,2},{7,3},{8,12},{9,13},{10,... | collective-permute-start | bytes 2488328 | tf_op jit(solution)/shard_map/ppermute | solution.py:693
  82.7 2.4 %collective-permute-start.15 = (bf16[3,180,768]{2,1,0:T(8,128)(2,1)S(1)}, bf16[3,180,768]{2,1,0:T(8,128)(2,1)S(1)}, u32[]{:S(2)}, u32[]{:S(2)}) collective-permute-start(bf16[3,180,768]{2,1,0:T(8,128)(2,1)S(1)} %get-tuple-element.56), channel_id=1, source_target_pairs={{0,4},{1,5},{2,6},{3,7},{4,0},{5,1},{6,2},{7,3},{8,12},{9,13},{10,... | collective-permute-start | bytes 2488328 | tf_op jit(solution)/shard_map/ppermute | solution.py:693
  83.9 16.8 %collective-permute-start.13 = (bf16[3,180,768]{2,1,0:T(8,128)(2,1)}, bf16[3,180,768]{2,1,0:T(8,128)(2,1)S(1)}, u32[]{:S(2)}, u32[]{:S(2)}) collective-permute-start(bf16[3,180,768]{2,1,0:T(8,128)(2,1)} %add_convert_fusion.1), channel_id=1, source_target_pairs={{0,4},{1,5},{2,0},{3,1},{4,6},{5,7},{6,10},{7,11},{8,12},{9,13},{1... | collective-permute-start | bytes 2488328 | tf_op jit(solution)/shard_map/ppermute | solution.py:693
  86.3 24.7 %collective-permute-start.16 = (bf16[3,180,768]{2,1,0:T(8,128)(2,1)}, bf16[3,180,768]{2,1,0:T(8,128)(2,1)S(1)}, u32[]{:S(2)}, u32[]{:S(2)}) collective-permute-start(bf16[3,180,768]{2,1,0:T(8,128)(2,1)} %add_convert_fusion), channel_id=1, source_target_pairs={{0,4},{1,5},{2,8},{3,9},{4,6},{5,7},{6,10},{7,11},{8,12},{9,13},{1... | collective-permute-start | bytes 2488328 | tf_op jit(solution)/shard_map/ppermute | solution.py:693
  100.7 17.5 %collective-permute-start.14 = (bf16[3,180,768]{2,1,0:T(8,128)(2,1)S(1)}, bf16[3,180,768]{2,1,0:T(8,128)(2,1)S(1)}, u32[]{:S(2)}, u32[]{:S(2)}) collective-permute-start(bf16[3,180,768]{2,1,0:T(8,128)(2,1)S(1)} %collective-permute-done.13.refs_0_), channel_id=1, source_target_pairs={{0,8},{1,9},{8,16},{9,17},{16,24},{17,25},{24,0},{25,1}} | collective-permute-start | bytes 2488328 | tf_op jit(solution)/shard_map/ppermute | solution.py:693
